TPU v7x, 512 devices: a whole 4x4x16 slice. The times are simulated.
512 devices in a mesh: pair: 8 (over y, z_hi), rng: 64 (over z_lo, x, core).
Axes of the slice: x: 4, y: 4, z: 16 (z_hi: 2, z_lo: 8; z = z_hi * 8 + z_lo), core: 2. Of those that a mesh axis runs over, the one named last changes fastest.
Arguments:
- stack: bfloat16 [8, 2, 16, 163840], P('pair', None, None, 'rng'), as said below
Outputs:
- coherence: float32 [8, 8, 2, 2, 8192], P('pair', None, None, None, 'rng')
Inputs may be any that keep to these rules, and one draw needn't show every extreme that they name: A coherent stack: every date is a scaled and rotated copy of one common scene plus noise of its own.
All inputs are finite; a program needn't handle non-finite values.
Results may differ from a plain program's by a relative error of at most 0.0003.
Values may be sent and summed in bfloat16 or wider, within the bound.
No kernel may reach another device: no remote copies, remote signals or barrier semaphores. Data moves between devices by JAX's collectives and lax.ppermute only.
A program may use at most 64 MiB of HBM per device.

v0:
```python
import jax
import jax.numpy as jnp
from jax import lax
from jax.sharding import PartitionSpec as P

AZ_TAPS = 31
RG_TAPS = 60
AZ_STEP = 8
RG_STEP = 20


epsilon = 1e-06
highest = lax.Precision.HIGHEST


def with_halo(shard, sides, width):
    for axis, dim in sides:
        count, length = (lax.axis_size(axis), shard.shape[dim])
        up = [(i, (i + 1) % count) for i in range(count - 1)]
        down = [(j, i) for i, j in up]
        last = lax.slice_in_dim(shard, length - width, length, axis=dim)
        initial = lax.slice_in_dim(shard, 0, width, axis=dim)
        before = lax.ppermute(last, axis, up)
        after = lax.ppermute(initial, axis, down)
        shard = jnp.concatenate([before, shard, after], axis=dim)
    return shard


def look_weights(lines_total):
    lines = jnp.arange(lines_total, dtype=jnp.int32)
    looks = jnp.arange(lines_total // AZ_STEP, dtype=jnp.int32)
    offset = lines[None, :] - (AZ_STEP * looks[:, None] + (AZ_STEP - AZ_TAPS) // 2)
    centred = (offset.astype(jnp.float32) - (AZ_TAPS - 1) / 2.0) / (AZ_TAPS / 4.0)
    inside = (offset >= 0) & (offset < AZ_TAPS)
    az_weights = jnp.where(inside, jnp.exp(-0.5 * centred * centred), jnp.zeros_like(centred))
    taps = jnp.arange(RG_TAPS, dtype=jnp.int32).astype(jnp.float32)
    centred_range = (taps - (RG_TAPS - 1) / 2.0) / (RG_TAPS / 4.0)
    range_weights = jnp.exp(-0.5 * centred_range * centred_range).reshape(3, RG_STEP)
    return (az_weights, range_weights)


def multilook(product, az_weights, range_weights):
    columns = product.shape[-1] // RG_STEP - 2
    blocks = product.reshape(product.shape[:-1] + (columns + 2, RG_STEP))
    summed = jnp.einsum(
        "...lrc,c->...lr", blocks[..., 0:columns, :], range_weights[0], precision=highest
    )
    summed = summed + jnp.einsum(
        "...lrc,c->...lr", blocks[..., 1 : columns + 1, :], range_weights[1], precision=highest
    )
    summed = summed + jnp.einsum(
        "...lrc,c->...lr", blocks[..., 2 : columns + 2, :], range_weights[2], precision=highest
    )
    return jnp.einsum("al,...lr->...ar", az_weights, summed, precision=highest)


def powers_of(tiles, az_weights, range_weights):
    real_tile = tiles[:, 0].astype(jnp.float32)
    imag_tile = tiles[:, 1].astype(jnp.float32)
    return (
        multilook(real_tile * real_tile + imag_tile * imag_tile, az_weights, range_weights)
        + epsilon
    )


def cross_terms(row_tiles, col_tiles, az_weights, range_weights):
    row_real = row_tiles[:, None, 0].astype(jnp.float32)
    row_imag = row_tiles[:, None, 1].astype(jnp.float32)
    col_real = col_tiles[None, :, 0].astype(jnp.float32)
    col_imag = col_tiles[None, :, 1].astype(jnp.float32)
    real_part = row_real * col_real + row_imag * col_imag
    imag_part = row_imag * col_real - row_real * col_imag
    product = jnp.stack([real_part, imag_part], axis=2)
    return multilook(product, az_weights, range_weights)


def normalized(cross, row_power, col_power):
    return cross * lax.rsqrt(row_power[:, None, None] * col_power[None, :, None])


def local(stack):
    az_weights, range_weights = look_weights(stack.shape[2])
    padded = with_halo(stack, (("rng", 3),), RG_STEP)
    own_power = powers_of(padded, az_weights, range_weights)
    arrived = lax.all_gather(padded, "pair", axis=0, tiled=True)
    cross = cross_terms(padded, arrived, az_weights, range_weights)
    col_power = powers_of(arrived, az_weights, range_weights)
    cross_all = cross
    power_all = col_power
    cross_all, power_all = (cross_all, power_all)
    result = normalized(cross_all, own_power, power_all)
    return result


def solution(mesh):
    in_specs = (P("pair", None, None, "rng"),)
    out_specs = P("pair", None, None, None, "rng")
    return jax.shard_map(local, mesh=mesh, in_specs=in_specs, out_specs=out_specs, check_vma=False)
```

profile of v0, /device:TPU:2, one launch (start us, length us, event | category | flops | bytes accessed | tf_op | source)
XLA Modules:
  0.0 217.6 jit_solution(2534883165095737052)
XLA Ops:
  6.5 0.0 all-gather.2.cloned.1.call-start
  6.5 0.8 fusion.69
  7.3 1.9 collective-permute-start
  9.2 3.6 %collective-permute-start.1 = (bf16[1,2,16,20]{3,2,1,0:T(8,128)(2,1)S(1)}, bf16[1,2,16,20]{3,2,1,0:T(8,128)(2,1)S(1)}, u32[]{:S(2)}, u32[]{:S(2)}) collective-permute-start(bf16[1,2,16,20]{3,2,1,0:T(8,128)(2,1)S(1)} %get-tuple-element.14), channel_id=1, source_target_pairs={{1,0},{2,1},{3,2},{4,3},{5,4},{6,5},{7,6},{8,7},{9,8},{10,9},{11,1... | collective-permute-start | bytes 3848 | tf_op jit(solution)/shard_map/ppermute | solution.py:24
  12.9 0.0 collective-permute-done
  12.9 1.3 collective-permute-done.1
  14.2 1.8 concatenate.4
  16.0 0.0 all-gather.2.cloned.1.call-update
  16.0 1.0 multiply_add_fusion.2
  17.0 0.4 add.97
  17.4 1.0 slice_convert_fusion.3
  18.3 1.4 reshape.201
  19.7 1.4 reshape.203
  21.1 1.0 fusion.24
  22.1 1.1 fusion.23
  23.2 1.1 fusion.22
  24.3 0.2 fusion.21
  24.5 98.5 %all-gather.2.cloned.1.call-done = bf16[8,2,16,2600]{3,2,1,0:T(8,128)(2,1)} async-done(((bf16[1,2,16,2600]{3,2,1,0:T(8,128)(2,1)}), bf16[8,2,16,2600]{3,2,1,0:T(8,128)(2,1)}) %all-gather.2.cloned.1.call-update) | async-done | bytes 1331216 | tf_op jit(solution)/shard_map/all_gather | solution.py:85
  123.0 1.5 multiply_add_fusion.1
  124.6 5.1 %add.105 = f32[8,16,130,20]{3,2,1,0:T(8,128)} reshape(f32[8,1,16,2600]{3,2,1,0:T(8,128)S(1)} %multiply_add_fusion.1) | data formatting | bytes 2662400 | tf_op jit(solution)/shard_map/add | solution.py:61
  129.7 0.0 slice-start
  129.7 0.0 slice-start.1
  129.7 9.8 %fusion.4 = f32[1,8,16,128]{3,0,2,1:T(1,128)S(1)} fusion(f32[8,16,130,20]{3,2,1,0:T(8,128)} %add.105, f32[60]{0:T(128)S(1)} %multiply_exponential_fusion), kind=kOutput, calls=%fused_computation.6 | convolution fusion | flops 3932160 | bytes 8454384 | tf_op jit(solution)/shard_map/...lrc,c->...lr/dot_general | solution.py:45
  139.5 0.0 slice-start.2
  139.5 10.5 %fusion.2 = f32[1,8,16,128]{3,0,2,1:T(1,128)S(1)} fusion(f32[8,16,130,20]{3,2,1,0:T(8,128)} %add.105, f32[60]{0:T(128)S(1)} %multiply_exponential_fusion), kind=kOutput, calls=%fused_computation.4 | convolution fusion | flops 3932160 | bytes 8454384 | tf_op jit(solution)/shard_map/...lrc,c->...lr/dot_general | solution.py:48
  150.0 0.0 slice-done
  150.0 0.0 slice-done.1
  150.0 0.0 slice-done.2
  150.0 0.0 copy-start
  150.1 7.8 %fusion = f32[1,8,16,128]{3,0,2,1:T(1,128)S(1)} fusion(f32[8,16,130,20]{3,2,1,0:T(8,128)S(1)} %bitcast.111, f32[60]{0:T(128)S(1)} %multiply_exponential_fusion), kind=kOutput, calls=%fused_computation.2 | convolution fusion | flops 3932160 | bytes 8454656 | tf_op jit(solution)/shard_map/...lrc,c->...lr/dot_general | solution.py:51
  157.9 0.0 copy-done
  157.9 0.2 slice_convert_fusion.1
  158.1 5.1 %reshape.202 = f32[1,8,1,16,130,20]{5,4,3,1,2,0:T(8,128)} reshape(f32[8,1,16,2600]{3,2,1,0:T(8,128)S(1)} %get-tuple-element.10) | data formatting | bytes 2662400 | tf_op jit(solution)/shard_map/convert_element_type | solution.py:69
  163.2 0.0 copy-start.1
  163.2 5.1 %reshape.204 = f32[1,8,1,16,130,20]{5,4,3,1,2,0:T(8,128)} reshape(f32[8,1,16,2600]{3,2,1,0:T(8,128)S(1)} %get-tuple-element.11) | data formatting | bytes 2662400 | tf_op jit(solution)/shard_map/convert_element_type | solution.py:70
  168.3 0.0 copy-done.1
  168.3 12.4 %multiply_add_fusion = (f32[1,8,1,16,130,20]{5,4,3,1,2,0:T(8,128)}, f32[1,8,1,16,130,20]{5,4,3,1,2,0:T(8,128)}) fusion(f32[1,8,1,16,130,20]{5,4,3,1,2,0:T(8,128)} %reshape.204, f32[1,8,1,16,130,20]{5,4,3,1,2,0:T(8,128)} %reshape.202, f32[16,130,20]{2,1,0:T(8,128)} %reshape.203, f32[16,130,20]{2,1,0:T(8,128)S(1)} %copy-done.1), kind=kLoop, calls=%fused_computation.1 | loop fusion | flops 1996800 | bytes 5657600 | tf_op jit(solution)/shard_map/add | solution.py:71
  180.7 7.2 %copy.2 = f32[1,8,1,16,130,20]{4,3,5,2,1,0:T(8,128)S(1)} copy(f32[1,8,1,16,130,20]{5,4,3,1,2,0:T(8,128)} %get-tuple-element.5) | data formatting | bytes 2662400 | tf_op jit(solution)/shard_map/add | solution.py:71
  188.0 8.2 %copy.3 = f32[1,8,1,16,130,20]{4,3,5,2,1,0:T(8,128)} copy(f32[1,8,1,16,130,20]{5,4,3,1,2,0:T(8,128)} %get-tuple-element.6) | data formatting | bytes 2662400 | tf_op jit(solution)/shard_map/sub | solution.py:72
  196.2 4.9 %fusion.13 = (f32[8,2,16,128,20]{3,2,4,1,0:T(8,128)S(1)}, f32[8,2,16,128,20]{3,2,4,1,0:T(8,128)S(1)}, f32[8,2,16,128,20]{3,2,4,1,0:T(8,128)S(1)}) fusion(f32[1,8,1,16,130,20]{4,3,5,2,1,0:T(8,128)S(1)} %copy.2, f32[1,8,1,16,130,20]{4,3,5,2,1,0:T(8,128)} %copy.3), kind=kLoop, calls=%fused_computation.19 | loop fusion | flops 1966080 | bytes 10526720 | tf_op jit(solution)/shard_map/reshape.14
  201.1 2.8 %fusion.6 = f32[1,8,2,16,128]{4,0,3,2,1:T(1,128)S(1)} fusion(f32[8,2,16,128,20]{3,2,4,1,0:T(8,128)S(1)} %get-tuple-element.9, f32[60]{0:T(128)S(1)} %multiply_exponential_fusion), kind=kOutput, calls=%fused_computation.12 | convolution fusion | flops 7864320 | bytes 2752752 | tf_op jit(solution)/shard_map/...lrc,c->...lr/dot_general | solution.py:51
  203.9 2.9 %fusion.10 = f32[1,8,2,16,128]{4,0,3,2,1:T(1,128)S(1)} fusion(f32[8,2,16,128,20]{3,2,4,1,0:T(8,128)S(1)} %get-tuple-element.8, f32[60]{0:T(128)S(1)} %multiply_exponential_fusion), kind=kOutput, calls=%fused_computation.16 | convolution fusion | flops 7864320 | bytes 2752752 | tf_op jit(solution)/shard_map/...lrc,c->...lr/dot_general | solution.py:45
  206.8 2.8 %fusion.8 = f32[1,8,2,16,128]{4,0,3,2,1:T(1,128)S(1)} fusion(f32[8,2,16,128,20]{3,2,4,1,0:T(8,128)S(1)} %get-tuple-element.7, f32[60]{0:T(128)S(1)} %multiply_exponential_fusion), kind=kOutput, calls=%fused_computation.14 | convolution fusion | flops 7864320 | bytes 2752752 | tf_op jit(solution)/shard_map/...lrc,c->...lr/dot_general | solution.py:48
  209.6 0.2 fusion.20
  209.9 0.9 fusion.17
  (3 shorter events, 0.0 us)
Async XLA Ops:
  6.5 116.5 %all-gather.2.cloned.1.call-start = ((), (), s32[]{:S(2)}) async-start(), calls=%async_computation | async-start | bytes 1548288 | tf_op jit(solution)/shard_map/all_gather | solution.py:85
  7.3 5.6 %collective-permute-start = (bf16[1,2,16,20]{3,2,1,0:T(8,128)(2,1)S(1)}, bf16[1,2,16,20]{3,2,1,0:T(8,128)(2,1)S(1)}, u32[]{:S(2)}, u32[]{:S(2)}) collective-permute-start(bf16[1,2,16,20]{3,2,1,0:T(8,128)(2,1)S(1)} %get-tuple-element.15), channel_id=1, source_target_pairs={{0,1},{1,2},{2,3},{3,4},{4,5},{5,6},{6,7},{7,8},{8,9},{9,10},{10,1... | collective-permute-start | bytes 3848 | tf_op jit(solution)/shard_map/ppermute | solution.py:23
  9.2 5.0 %collective-permute-start.1 = (bf16[1,2,16,20]{3,2,1,0:T(8,128)(2,1)S(1)}, bf16[1,2,16,20]{3,2,1,0:T(8,128)(2,1)S(1)}, u32[]{:S(2)}, u32[]{:S(2)}) collective-permute-start(bf16[1,2,16,20]{3,2,1,0:T(8,128)(2,1)S(1)} %get-tuple-element.14), channel_id=1, source_target_pairs={{1,0},{2,1},{3,2},{4,3},{5,4},{6,5},{7,6},{8,7},{9,8},{10,9},{11,1... | collective-permute-start | bytes 3848 | tf_op jit(solution)/shard_map/ppermute | solution.py:24
  129.7 20.3 %slice-start = ((s8[8912896]{0:T(1024)(128)(4,1)}), s8[4194304]{0:T(1024)(128)(4,1)S(1)}, s32[]{:S(2)}) async-start(s8[8912896]{0:T(1024)(128)(4,1)} %bitcast.110), calls=%async_computation.1 | async-start | bytes 8388608
  129.7 20.3 %slice-start.1 = ((s8[8912896]{0:T(1024)(128)(4,1)}), s8[4194304]{0:T(1024)(128)(4,1)S(1)}, s32[]{:S(2)}) async-start(s8[8912896]{0:T(1024)(128)(4,1)} %bitcast.110), calls=%async_computation.2 | async-start | bytes 8388608
  139.5 10.5 %slice-start.2 = ((s8[8912896]{0:T(1024)(128)(4,1)}), s8[524288]{0:T(1024)(128)(4,1)S(1)}, s32[]{:S(2)}) async-start(s8[8912896]{0:T(1024)(128)(4,1)} %bitcast.110), calls=%async_computation.3 | async-start | bytes 1048576
  150.0 7.8 %copy-start = (bf16[8,2,16,2600]{3,2,1,0:T(8,128)(2,1)S(1)}, bf16[8,2,16,2600]{3,2,1,0:T(8,128)(2,1)}, u32[]{:S(2)}) copy-start(bf16[8,2,16,2600]{3,2,1,0:T(8,128)(2,1)} %all-gather.2.cloned.1.call-done) | copy-start | bytes 3993604
  163.2 5.1 %copy-start.1 = (f32[16,130,20]{2,1,0:T(8,128)S(1)}, f32[16,130,20]{2,1,0:T(8,128)}, u32[]{:S(2)}) copy-start(f32[16,130,20]{2,1,0:T(8,128)} %reshape.201) | copy-start | bytes 499204
Sparse Core Ops, SparseCore 0:
  16.2 106.8 all-gather.1
where the time goes:
time: 218 us
  waiting for transfers between devices  99.8 us (46%)
  matrix products  41.1 us (19%)
  local copies, waits for them, and re-layouts  36.5 us (17%)
  other arithmetic  21 us (10%)
  between operations  13.6 us (6%)
  starting transfers between devices  5.55 us (3%)
    all_gather x1, waiting for transfers between devices, local(): arrived = lax.all_gather(padded, 'pair', axis=0, tiled=True)  98.5 us
    dot_general x3, matrix products, multilook(): jnp.einsum('...lrc,c->...lr', blocks[..., 1:columns + 1, :], range_weight...  14.4 us
    dot_general x3, matrix products, multilook(): jnp.einsum('...lrc,c->...lr', blocks[..., 0:columns, :], range_weights[0]...  13.7 us
    add x1, other arithmetic, cross_terms(): real_part = row_real * col_real + row_imag * col_imag  12.4 us
    dot_general x3, matrix products, multilook(): jnp.einsum('...lrc,c->...lr', blocks[..., 2:columns + 2, :], range_weight...  11.7 us
    sub x1, local copies, waits for them, and re-layouts, cross_terms(): imag_part = row_imag * col_real - row_real * col_imag  8.23 us
    add x1, local copies, waits for them, and re-layouts, cross_terms(): real_part = row_real * col_real + row_imag * col_imag  7.25 us
    add x2, local copies, waits for them, and re-layouts, powers_of(): real_tile * real_tile + imag_tile * imag_tile  5.49 us
  transfers between devices with their start and end apart: 3, of which 2 were waited for; matrix products, arithmetic and copies ran while one was open for 4% of the time, Pallas kernels for 0%

commit v1 on v0

v1 whole, which is shorter than its diff:
```python
import math

import jax
import jax.numpy as jnp
from jax import lax
from jax.experimental import pallas as pl
from jax.experimental.pallas import tpu as pltpu
from jax.sharding import PartitionSpec as P

AZ_TAPS = 31
RG_TAPS = 60
AZ_STEP = 8
RG_STEP = 20
LINES = 16
LANES = 128
EPSILON = 1e-06

Y = 4
GROUPS = [[0, 2, 4, 6], [1, 3, 5, 7]]
INNER = [(i, j) for i in range(Y) for j in range(i + 1, Y)]

f32 = jnp.float32
bf16 = jnp.bfloat16
VMEM = pl.BlockSpec(memory_space=pltpu.VMEM)


def place():
    pair = lax.axis_index("pair")
    return pair // 2, pair % 2


def azimuth_weights():
    line = lax.broadcasted_iota(jnp.int32, (LINES, LANES), 0)
    weights = []
    for look in range(LINES // AZ_STEP):
        offset = line - (AZ_STEP * look + (AZ_STEP - AZ_TAPS) // 2)
        centred = (offset.astype(f32) - (AZ_TAPS - 1) / 2.0) / (AZ_TAPS / 4.0)
        inside = (offset >= 0) & (offset < AZ_TAPS)
        weights.append(jnp.where(inside, jnp.exp(-0.5 * centred * centred), 0.0))
    return weights


def range_weights(quarter, rows, columns):
    row = lax.broadcasted_iota(jnp.int32, (rows + LANES, columns), 0)
    look = lax.broadcasted_iota(jnp.int32, (rows + LANES, columns), 1)
    own = quarter * rows + row
    halo = row - rows + jnp.where(quarter == 0, -LANES, Y * rows)
    sample = jnp.where(row < rows, own, halo)
    tap = sample - RG_STEP * (look - 1)
    centred = (tap.astype(f32) - (RG_TAPS - 1) / 2.0) / (RG_TAPS / 4.0)
    inside = (tap >= 0) & (tap < RG_TAPS)
    return jnp.where(inside, 2.0 * jnp.exp(-0.5 * centred * centred), 0.0)


def prepare_kernel(group_ref, edge_ref, weight_ref):
    quarter, _ = place()
    width = group_ref.shape[-1]
    first = group_ref[:, :, :, 0:LANES]
    last = group_ref[:, :, :, width - LANES : width]
    edge_ref[...] = jnp.where(quarter == Y - 1, last, first)
    weights = range_weights(quarter, width, LANES)
    high = weights.astype(bf16)
    weight_ref[:, 0:LANES] = high
    weight_ref[:, LANES : 2 * LANES] = (weights - high.astype(f32)).astype(bf16)


def load(ref, halo_ref, date, at):
    width = ref.shape[-1]
    if at < width:
        tile = ref[date, :, :, at : at + LANES]
    else:
        tile = halo_ref[date]
    tile = tile.astype(f32)
    return tile[0], tile[1]


def put(x_ref, fields, field, at, value):
    high = value.astype(bf16)
    low = (value - high.astype(f32)).astype(bf16)
    x_ref[field * LINES : (field + 1) * LINES, at : at + LANES] = high
    x_ref[(fields + field) * LINES : (fields + field + 1) * LINES, at : at + LANES] = low


def looks_of(x_ref, weight_ref, d_ref, fields):
    d_ref[...] = jnp.dot(x_ref[...], weight_ref[...], preferred_element_type=f32)
    weights = azimuth_weights()
    for field in range(fields):
        high = d_ref[field * LINES : (field + 1) * LINES, :]
        low = d_ref[(fields + field) * LINES : (fields + field + 1) * LINES, :]
        both = high + low
        summed = both[:, 0:LANES] + both[:, LANES : 2 * LANES]
        yield field, [jnp.sum(summed * w, axis=0, keepdims=True) for w in weights]


def inner_kernel(group_ref, halo_ref, weight_ref, out_ref, x_ref, d_ref):
    fields = Y + 2 * len(INNER)
    for at in range(0, group_ref.shape[-1] + LANES, LANES):
        dates = [load(group_ref, halo_ref, i, at) for i in range(Y)]
        halves = [(0.5 * x, 0.5 * y) for x, y in dates]
        for i, ((x, y), (hx, hy)) in enumerate(zip(dates, halves)):
            put(x_ref, fields, i, at, hx * x + hy * y)
        for k, (i, j) in enumerate(INNER):
            (hx, hy), (x, y) = halves[i], dates[j]
            put(x_ref, fields, Y + 2 * k, at, hx * x + hy * y)
            put(x_ref, fields, Y + 2 * k + 1, at, hy * x - hx * y)
    for field, rows in looks_of(x_ref, weight_ref, d_ref, fields):
        for a, row in enumerate(rows):
            out_ref[2 * field + a : 2 * field + a + 1, :] = row


def outer_kernel(group_ref, other_ref, group_halo_ref, other_halo_ref, weight_ref, inner_ref, out_ref, x_ref, d_ref):
    _, here = place()
    there = 1 - here
    fields = Y + 2 * Y * Y
    for at in range(0, group_ref.shape[-1] + LANES, LANES):
        dates = [load(other_ref, other_halo_ref, j, at) for j in range(Y)]
        for j, (x, y) in enumerate(dates):
            put(x_ref, fields, j, at, (0.5 * x) * x + (0.5 * y) * y)
        for i in range(Y):
            x, y = load(group_ref, group_halo_ref, i, at)
            hx, hy = 0.5 * x, 0.5 * y
            for j, (x, y) in enumerate(dates):
                field = Y + 2 * (Y * i + j)
                put(x_ref, fields, field, at, hx * x + hy * y)
                put(x_ref, fields, field + 1, at, hy * x - hx * y)

    def store(i, side, part, j, a, row):
        at = 8 * part + 2 * j + a
        out_ref[i, side, at : at + 1, :] = row

    def inner(field, a):
        return inner_ref[2 * field + a : 2 * field + a + 1, :]

    for a in range(2):
        for j in range(Y):
            power = inner(j, a)
            store(j, here, 0, j, a, power)
            store(j, here, 1, j, a, jnp.zeros_like(power))
            for i in range(Y):
                store(i, here, 2, j, a, power)
                store(j, here, 3, i, a, power)
                store(j, there, 3, i, a, power)
        for k, (i, j) in enumerate(INNER):
            real, imag = inner(Y + 2 * k, a), inner(Y + 2 * k + 1, a)
            store(i, here, 0, j, a, real)
            store(i, here, 1, j, a, imag)
            store(j, here, 0, i, a, real)
            store(j, here, 1, i, a, -imag)
    for field, rows in looks_of(x_ref, weight_ref, d_ref, fields):
        for a, row in enumerate(rows):
            if field < Y:
                for i in range(Y):
                    store(i, there, 2, field, a, row)
            else:
                i, j = divmod((field - Y) // 2, Y)
                store(i, there, (field - Y) % 2, j, a, row)


def normalise_kernel(parts_ref, out_ref):
    for side in range(2):
        summed = parts_ref[0, side] + parts_ref[1, side] + parts_ref[2, side] + parts_ref[3, side]
        scale = lax.rsqrt((summed[24:32] + EPSILON) * (summed[16:24] + EPSILON))
        for k in range(2):
            rows = summed[8 * k : 8 * k + 8] * scale
            for j in range(Y):
                out_ref[2 * j + side, k] = rows[2 * j : 2 * j + 2]


def call(kernel, out_shape, operands, scratch=(), cost=0):
    return pl.pallas_call(
        kernel,
        out_shape=out_shape,
        in_specs=[VMEM] * len(operands),
        out_specs=jax.tree.map(lambda _: VMEM, out_shape),
        scratch_shapes=list(scratch),
        cost_estimate=pl.CostEstimate(flops=cost, bytes_accessed=1 << 20, transcendentals=0),
    )(*operands)


def edges(tiles, swap):
    pairs = []
    for h in range(2):
        for n in range(tiles):
            source = (h ^ swap) * tiles + n
            if n + 1 < tiles:
                pairs.append((2 * (Y - 1) * tiles + source, h * tiles + n + 1))
            if n > 0:
                pairs.append((source, (2 * (Y - 1) + h) * tiles + n - 1))
    return pairs


def local(stack):
    tiles = lax.axis_size("rng")
    width = stack.shape[-1] // Y
    axes = ("pair", "rng")
    across = [((2 * y + h) * tiles + n, (2 * y + 1 - h) * tiles + n) for y in range(Y) for h in range(2) for n in range(tiles)]

    chunks = stack[0].reshape(2, LINES, Y, width).transpose(2, 0, 1, 3)
    group = lax.all_to_all(chunks, "pair", 0, 0, axis_index_groups=GROUPS)
    other = lax.ppermute(group, axes, across)

    depth = width + LANES
    edge, weights = call(
        prepare_kernel,
        (jax.ShapeDtypeStruct((Y, 2, LINES, LANES), bf16), jax.ShapeDtypeStruct((depth, 2 * LANES), bf16)),
        (group,),
        cost=10 * depth * LANES,
    )
    other_halo = lax.ppermute(edge, axes, edges(tiles, 1))
    group_halo = lax.ppermute(edge, axes, edges(tiles, 0))

    def scratch(fields):
        return [pltpu.VMEM((2 * fields * LINES, depth), bf16), pltpu.VMEM((2 * fields * LINES, 2 * LANES), f32)]

    fields = Y + 2 * len(INNER)
    inner = call(
        inner_kernel,
        jax.ShapeDtypeStruct((2 * fields, LANES), f32),
        (group, group_halo, weights),
        scratch(fields),
        cost=2 * 2 * fields * LINES * depth * 2 * LANES,
    )
    fields = Y + 2 * Y * Y
    parts = call(
        outer_kernel,
        jax.ShapeDtypeStruct((Y, 2, 32, LANES), f32),
        (group, other, group_halo, other_halo, weights, inner),
        scratch(fields),
        cost=2 * 2 * fields * LINES * depth * 2 * LANES,
    )
    parts = lax.all_to_all(parts, "pair", 0, 0, axis_index_groups=GROUPS)
    out = call(normalise_kernel, jax.ShapeDtypeStruct((2 * Y, 2, 2, LANES), f32), (parts,))
    return out[None]


def solution(mesh):
    in_specs = (P("pair", None, None, "rng"),)
    out_specs = P("pair", None, None, None, "rng")
    return jax.shard_map(local, mesh=mesh, in_specs=in_specs, out_specs=out_specs, check_vma=False)
```

time: 218 us -> 66 us (0.30)
  the two profiles are of different devices: /device:TPU:2 before, /device:TPU:96 now
where the time goes in v1:
time: 66 us; the launch traced here: 65.6 us
  starting transfers between devices  21.3 us (32%)
  blocking collectives  20.4 us (31%)
  waiting for transfers between devices  12.5 us (19%)
  Pallas kernels  8.47 us (13%)
  local copies, waits for them, and re-layouts  2.85 us (4%)
    ppermute x1, starting transfers between devices, local(): other = lax.ppermute(group, axes, across)  13 us
    all_to_all x1, blocking collectives, local(): group = lax.all_to_all(chunks, 'pair', 0, 0, axis_index_groups=GROUPS)  10.4 us
    all_to_all x1, blocking collectives, local(): parts = lax.all_to_all(parts, 'pair', 0, 0, axis_index_groups=GROUPS)  9.97 us
    pallas_call x4, Pallas kernels, call(): pl.pallas_call(kernel, out_shape=out_shape, in_specs=[VMEM] * len(operand...  8.47 us
    ppermute x1, waiting for transfers between devices, local(): group_halo = lax.ppermute(edge, axes, edges(tiles, 0))  6.91 us
    ppermute x1, waiting for transfers between devices, local(): other_halo = lax.ppermute(edge, axes, edges(tiles, 1))  5.62 us
    ppermute x1, starting transfers between devices, local(): other_halo = lax.ppermute(edge, axes, edges(tiles, 1))  4.89 us
    ppermute x1, starting transfers between devices, local(): group_halo = lax.ppermute(edge, axes, edges(tiles, 0))  3.43 us
  transfers between devices with their start and end apart: 3, of which 2 were waited for; matrix products, arithmetic and copies ran while one was open for 0% of the time, Pallas kernels for 6%

profile of v1, /device:TPU:96, one launch (start us, length us, event | category | flops | bytes accessed | tf_op | source)
XLA Modules:
  0.0 65.6 jit_solution(18259016100036481422)
XLA Ops:
  0.0 1.0 %reshape_squeeze.3 = bf16[2,16,4,640]{3,2,1,0:T(4,128)(2,1)S(1)} reshape(bf16[1,2,16,2560]{3,2,1,0:T(8,128)(2,1)} %param.1) | data formatting | bytes 327680 | tf_op jit(solution)/shard_map/reshape;squeeze | solution.py:198
  1.0 10.4 %all_to_all.10.group_ref = bf16[4,2,16,640]{3,2,1,0:T(8,128)(2,1)S(1)} all-to-all(bf16[4,2,16,640]{3,2,1,0:T(8,128)(2,1)S(1)} %bitcast.6), channel_id=1, replica_groups={{0,128,256,384},{64,192,320,448},{1,129,257,385},{65,193,321,449},{2,13..., dimensions={0} | all-to-all | bytes 327680 | tf_op jit(solution)/shard_map/all_to_all | solution.py:199
  11.4 0.0 copy-start
  11.4 13.0 %collective-permute-start = (bf16[4,2,16,640]{3,2,1,0:T(8,128)(2,1)S(1)}, bf16[4,2,16,640]{3,2,1,0:T(8,128)(2,1)S(1)}, u32[]{:S(2)}, u32[]{:S(2)}) collective-permute-start(bf16[4,2,16,640]{3,2,1,0:T(8,128)(2,1)S(1)} %all_to_all.10.group_ref), channel_id=1, source_target_pairs={{0,64},{1,65},{2,66},{3,67},{4,68},{5,69},{6,70},{7,71},{8,72},{9,... | collective-permute-start | bytes 491528 | tf_op jit(solution)/shard_map/ppermute | solution.py:200
  24.4 0.0 copy-done
  24.4 1.9 %shard_map.17 = (bf16[4,2,16,128]{3,2,1,0:T(8,128)(2,1)}, bf16[768,256]{1,0:T(8,128)(2,1)}) custom-call(bf16[4,2,16,640]{3,2,1,0:T(8,128)(2,1)} %copy-done), custom_call_target="tpu_custom_call" | custom-call | flops 983040 | bytes 1048576 | tf_op jit(solution)/shard_map/pallas_call | solution.py:170
  26.4 3.4 %collective-permute-start.1 = (bf16[4,2,16,128]{3,2,1,0:T(8,128)(2,1)}, bf16[4,2,16,128]{3,2,1,0:T(8,128)(2,1)S(1)}, u32[]{:S(2)}, u32[]{:S(2)}) collective-permute-start(bf16[4,2,16,128]{3,2,1,0:T(8,128)(2,1)} %get-tuple-element.7), channel_id=1, source_target_pairs={{384,1},{385,2},{1,384},{386,3},{2,385},{387,4},{3,386},{388,5},{4... | collective-permute-start | bytes 98312 | tf_op jit(solution)/shard_map/ppermute | solution.py:210
  29.8 4.9 %collective-permute-start.2 = (bf16[4,2,16,128]{3,2,1,0:T(8,128)(2,1)}, bf16[4,2,16,128]{3,2,1,0:T(8,128)(2,1)S(1)}, u32[]{:S(2)}, u32[]{:S(2)}) collective-permute-start(bf16[4,2,16,128]{3,2,1,0:T(8,128)(2,1)} %get-tuple-element.7), channel_id=1, source_target_pairs={{448,1},{449,2},{65,384},{450,3},{66,385},{451,4},{67,386},{452,5}... | collective-permute-start | bytes 98312 | tf_op jit(solution)/shard_map/ppermute | solution.py:209
  34.7 6.9 %collective-permute-done.1.halo_ref.group_halo_ref = bf16[4,2,16,128]{3,2,1,0:T(8,128)(2,1)S(1)} collective-permute-done((bf16[4,2,16,128]{3,2,1,0:T(8,128)(2,1)}, bf16[4,2,16,128]{3,2,1,0:T(8,128)(2,1)S(1)}, u32[]{:S(2)}, u32[]{:S(2)}) %collective-permute-start.1) | collective-permute-done | bytes 32800 | tf_op jit(solution)/shard_map/ppermute | solution.py:210
  41.6 0.0 copy-start.2
  41.6 0.6 copy-done.2
  42.2 2.2 %shard_map.18.inner_ref = f32[32,128]{1,0:T(8,128)} custom-call(bf16[4,2,16,640]{3,2,1,0:T(8,128)(2,1)} %copy-done, bf16[4,2,16,128]{3,2,1,0:T(8,128)(2,1)} %copy-done.2, bf16[768,256]{1,0:T(8,128)(2,1)} %get-tuple-element.8.weight_ref), custom_call_target="tpu_custom_call" | custom-call | flops 201326592 | bytes 1048576 | tf_op jit(solution)/shard_map/pallas_call | solution.py:170
  44.4 5.6 %collective-permute-done.2.other_halo_ref = bf16[4,2,16,128]{3,2,1,0:T(8,128)(2,1)S(1)} collective-permute-done((bf16[4,2,16,128]{3,2,1,0:T(8,128)(2,1)}, bf16[4,2,16,128]{3,2,1,0:T(8,128)(2,1)S(1)}, u32[]{:S(2)}, u32[]{:S(2)}) %collective-permute-start.2) | collective-permute-done | bytes 32800 | tf_op jit(solution)/shard_map/ppermute | solution.py:209
  50.0 0.0 copy-start.3
  50.0 0.0 collective-permute-done.other_ref
  50.0 0.6 copy-done.3
  50.6 0.0 copy-start.1
  50.6 0.7 %copy-done.1 = bf16[4,2,16,640]{3,2,1,0:T(8,128)(2,1)} copy-done((bf16[4,2,16,640]{3,2,1,0:T(8,128)(2,1)}, bf16[4,2,16,640]{3,2,1,0:T(8,128)(2,1)S(1)}, u32[]{:S(2)}) %copy-start.1) | copy-done | bytes 163864
  51.3 2.8 %shard_map.19 = f32[4,2,32,128]{3,2,1,0:T(8,128)} custom-call(bf16[4,2,16,640]{3,2,1,0:T(8,128)(2,1)} %copy-done, bf16[4,2,16,640]{3,2,1,0:T(8,128)(2,1)} %copy-done.1, bf16[4,2,16,128]{3,2,1,0:T(8,128)(2,1)} %copy-done.2, bf16[4,2,16,128]{3,2,1,0:T(8,128)(2,1)} %copy-done.3, bf16[768,256]{1,0:T(8,128)(2,1)} %get-tuple-element.8.weight_ref, ...), custom_call_target="tpu_custom_call" | custom-call | flops 452984832 | bytes 1048576 | tf_op jit(solution)/shard_map/pallas_call | solution.py:170
  54.1 10.0 %all_to_all.11.parts_ref = f32[4,2,32,128]{3,2,1,0:T(8,128)} all-to-all(f32[4,2,32,128]{3,2,1,0:T(8,128)} %shard_map.19), channel_id=1, replica_groups={{0,128,256,384},{64,192,320,448},{1,129,257,385},{65,193,321,449},{2,13..., dimensions={0} | all-to-all | bytes 262144 | tf_op jit(solution)/shard_map/all_to_all | solution.py:231
  64.1 1.5 %shard_map.20 = f32[8,2,2,128]{3,2,1,0:T(2,128)} custom-call(f32[4,2,32,128]{3,2,1,0:T(8,128)} %all_to_all.11.parts_ref), custom_call_target="tpu_custom_call" | custom-call | bytes 1048576 | tf_op jit(solution)/shard_map/pallas_call | solution.py:170
  (1 shorter events, 0.0 us)
Async XLA Ops:
  11.4 13.0 %copy-start = (bf16[4,2,16,640]{3,2,1,0:T(8,128)(2,1)}, bf16[4,2,16,640]{3,2,1,0:T(8,128)(2,1)S(1)}, u32[]{:S(2)}) copy-start(bf16[4,2,16,640]{3,2,1,0:T(8,128)(2,1)S(1)} %all_to_all.10.group_ref) | copy-start | bytes 491524
  11.4 38.6 %collective-permute-start = (bf16[4,2,16,640]{3,2,1,0:T(8,128)(2,1)S(1)}, bf16[4,2,16,640]{3,2,1,0:T(8,128)(2,1)S(1)}, u32[]{:S(2)}, u32[]{:S(2)}) collective-permute-start(bf16[4,2,16,640]{3,2,1,0:T(8,128)(2,1)S(1)} %all_to_all.10.group_ref), channel_id=1, source_target_pairs={{0,64},{1,65},{2,66},{3,67},{4,68},{5,69},{6,70},{7,71},{8,72},{9,... | collective-permute-start | bytes 491528 | tf_op jit(solution)/shard_map/ppermute | solution.py:200
  26.4 15.2 %collective-permute-start.1 = (bf16[4,2,16,128]{3,2,1,0:T(8,128)(2,1)}, bf16[4,2,16,128]{3,2,1,0:T(8,128)(2,1)S(1)}, u32[]{:S(2)}, u32[]{:S(2)}) collective-permute-start(bf16[4,2,16,128]{3,2,1,0:T(8,128)(2,1)} %get-tuple-element.7), channel_id=1, source_target_pairs={{384,1},{385,2},{1,384},{386,3},{2,385},{387,4},{3,386},{388,5},{4... | collective-permute-start | bytes 98312 | tf_op jit(solution)/shard_map/ppermute | solution.py:210
  29.8 20.2 %collective-permute-start.2 = (bf16[4,2,16,128]{3,2,1,0:T(8,128)(2,1)}, bf16[4,2,16,128]{3,2,1,0:T(8,128)(2,1)S(1)}, u32[]{:S(2)}, u32[]{:S(2)}) collective-permute-start(bf16[4,2,16,128]{3,2,1,0:T(8,128)(2,1)} %get-tuple-element.7), channel_id=1, source_target_pairs={{448,1},{449,2},{65,384},{450,3},{66,385},{451,4},{67,386},{452,5}... | collective-permute-start | bytes 98312 | tf_op jit(solution)/shard_map/ppermute | solution.py:209
  41.6 0.6 copy-start.2
  50.0 0.6 copy-start.3
  50.6 0.7 %copy-start.1 = (bf16[4,2,16,640]{3,2,1,0:T(8,128)(2,1)}, bf16[4,2,16,640]{3,2,1,0:T(8,128)(2,1)S(1)}, u32[]{:S(2)}) copy-start(bf16[4,2,16,640]{3,2,1,0:T(8,128)(2,1)S(1)} %collective-permute-done.other_ref) | copy-start | bytes 491524

commit v2 on v1

v2 whole, which is shorter than its diff:
```python
import jax
import jax.numpy as jnp
from jax import lax
from jax.experimental import pallas as pl
from jax.experimental.pallas import tpu as pltpu
from jax.sharding import PartitionSpec as P

AZ_TAPS = 31
RG_TAPS = 60
AZ_STEP = 8
RG_STEP = 20
LINES = 16
LANES = 128
SLOT = 32
EPSILON = 1e-06
VMEM_LIMIT = 8 << 20

Y = 4
GROUPS = [[0, 2, 4, 6], [1, 3, 5, 7]]
INNER = [(i, j) for i in range(Y) for j in range(i + 1, Y)]
N_INNER = Y + 2 * len(INNER)
N_OUTER = Y + 2 * Y * Y

f32 = jnp.float32
bf16 = jnp.bfloat16
VMEM = pl.BlockSpec(memory_space=pltpu.VMEM)


def quarter_of(y):
    return jnp.where(lax.axis_index("rng") % 2 == 1, Y - 1 - y, y)


def here():
    pair = lax.axis_index("pair")
    return quarter_of(pair // 2), pair % 2


def lanes(rows):
    return lax.broadcasted_iota(jnp.int32, (rows, LANES), 1)


def azimuth_weights():
    line = lax.broadcasted_iota(jnp.int32, (LINES, LANES), 0)
    weights = []
    for look in range(LINES // AZ_STEP):
        offset = line - (AZ_STEP * look + (AZ_STEP - AZ_TAPS) // 2)
        centred = (offset.astype(f32) - (AZ_TAPS - 1) / 2.0) / (AZ_TAPS / 4.0)
        inside = (offset >= 0) & (offset < AZ_TAPS)
        weights.append(jnp.where(inside, jnp.exp(-0.5 * centred * centred), 0.0))
    return weights


def range_weights(quarter, width):
    shape = (width + LANES, LANES)
    row = lax.broadcasted_iota(jnp.int32, shape, 0)
    look = lax.broadcasted_iota(jnp.int32, shape, 1)
    halo = row - width + jnp.where(quarter == 0, -RG_STEP, Y * width)
    sample = jnp.where(row < width, quarter * width + row, halo)
    tap = sample - RG_STEP * (look - 1)
    centred = (tap.astype(f32) - (RG_TAPS - 1) / 2.0) / (RG_TAPS / 4.0)
    inside = (tap >= 0) & (tap < RG_TAPS) & (row < width + RG_STEP)
    return jnp.where(inside, 2.0 * jnp.exp(-0.5 * centred * centred), 0.0)


def cut_kernel(stack_ref, out_ref):
    blocks = out_ref.shape[2]
    for q in range(Y):
        to = quarter_of(q)
        for part in range(2):
            for t in range(blocks):
                at = (q * blocks + t) * LANES
                out_ref[to, part, t] = stack_ref[0, part, :, at : at + LANES]


def edge_kernel(group_ref, edge_ref):
    quarter, _ = here()
    blocks = group_ref.shape[2]
    for part in range(2):
        packed = jnp.zeros((LINES, LANES), f32)
        for i in range(Y):
            first = group_ref[i, part, 0].astype(f32)
            last = group_ref[i, part, blocks - 1].astype(f32)
            edge = jnp.where(quarter == Y - 1, pltpu.roll(last, RG_STEP, 1), first)
            edge = jnp.where(lanes(LINES) < RG_STEP, edge, 0.0)
            packed = packed + (pltpu.roll(edge, SLOT * i, 1) if i else edge)
        edge_ref[part] = packed.astype(bf16)


def join_kernel(group_ref, halo_ref, out_ref):
    blocks = group_ref.shape[2]
    for i in range(Y):
        for part in range(2):
            for t in range(blocks):
                out_ref[(2 * i + part) * blocks + t] = group_ref[i, part, t]
    for part in range(2):
        out_ref[2 * Y * blocks + part] = halo_ref[part]


def blocks_of(ref):
    return (ref.shape[0] - 2) // (2 * Y)


def dates_at(ref, t):
    blocks = blocks_of(ref)
    if t < blocks:
        return [tuple(ref[(2 * i + part) * blocks + t].astype(f32) for part in range(2)) for i in range(Y)]
    packed = [ref[2 * Y * blocks + part].astype(f32) for part in range(2)]
    inside = lanes(LINES) < RG_STEP
    rolled = [[pltpu.roll(p, LANES - SLOT * i, 1) if i else p for p in packed] for i in range(Y)]
    return [tuple(jnp.where(inside, p, 0.0) for p in date) for date in rolled]


def power(date):
    x, y = date
    return ((0.5 * x) * x + (0.5 * y) * y,)


def cross(row, column):
    hx, hy = 0.5 * row[0], 0.5 * row[1]
    x, y = column
    return hx * x + hy * y, hy * x - hx * y


def put(x_ref, fields, t, values):
    at = t * LANES
    for field, value in enumerate(values):
        high = value.astype(bf16)
        low = (value - high.astype(f32)).astype(bf16)
        x_ref[field * LINES : (field + 1) * LINES, at : at + LANES] = high
        x_ref[(fields + field) * LINES : (fields + field + 1) * LINES, at : at + LANES] = low


def looks_of(x_ref, weights, d_ref, fields):
    d_ref[...] = jnp.dot(x_ref[...], weights, preferred_element_type=f32)
    azimuth = azimuth_weights()
    for field in range(fields):
        high = d_ref[field * LINES : (field + 1) * LINES, :]
        low = d_ref[(fields + field) * LINES : (fields + field + 1) * LINES, :]
        both = high + low
        summed = both[:, 0:LANES] + both[:, LANES : 2 * LANES]
        for a, weight in enumerate(azimuth):
            yield field, a, jnp.sum(summed * weight, axis=0, keepdims=True)


def inner_kernel(group_ref, out_ref, weight_ref, x_ref, d_ref):
    blocks = blocks_of(group_ref)
    quarter, _ = here()
    weights = range_weights(quarter, blocks * LANES)
    high = weights.astype(bf16)
    weight_ref[:, 0:LANES] = high
    weight_ref[:, LANES : 2 * LANES] = (weights - high.astype(f32)).astype(bf16)
    for t in range(blocks + 1):
        group = dates_at(group_ref, t)
        fields = [power(d) for d in group] + [cross(group[i], group[j]) for i, j in INNER]
        put(x_ref, N_INNER, t, [value for field in fields for value in field])
    for field, a, row in looks_of(x_ref, weight_ref[...], d_ref, N_INNER):
        out_ref[2 * field + a : 2 * field + a + 1, :] = row


def outer_kernel(group_ref, other_ref, weight_ref, inner_ref, out_ref, x_ref, d_ref):
    _, own = here()
    across = 1 - own
    for t in range(blocks_of(group_ref) + 1):
        group, other = dates_at(group_ref, t), dates_at(other_ref, t)
        fields = [power(d) for d in other] + [cross(i, j) for i in group for j in other]
        put(x_ref, N_OUTER, t, [value for field in fields for value in field])

    def store(i, side, part, j, a, row):
        at = 8 * part + 2 * j + a
        out_ref[i, side, at : at + 1, :] = row

    def inner(field, a):
        return inner_ref[2 * field + a : 2 * field + a + 1, :]

    for a in range(2):
        for j in range(Y):
            row = inner(j, a)
            store(j, own, 0, j, a, row)
            store(j, own, 1, j, a, jnp.zeros_like(row))
            for i in range(Y):
                store(i, own, 2, j, a, row)
                store(j, own, 3, i, a, row)
                store(j, across, 3, i, a, row)
        for k, (i, j) in enumerate(INNER):
            real, imag = inner(Y + 2 * k, a), inner(Y + 2 * k + 1, a)
            store(i, own, 0, j, a, real)
            store(i, own, 1, j, a, imag)
            store(j, own, 0, i, a, real)
            store(j, own, 1, i, a, -imag)
    for field, a, row in looks_of(x_ref, weight_ref[...], d_ref, N_OUTER):
        if field < Y:
            for i in range(Y):
                store(i, across, 2, field, a, row)
        else:
            i, j = divmod((field - Y) // 2, Y)
            store(i, across, (field - Y) % 2, j, a, row)


def normalise_kernel(parts_ref, out_ref):
    for side in range(2):
        summed = parts_ref[0, side] + parts_ref[1, side] + parts_ref[2, side] + parts_ref[3, side]
        scale = lax.rsqrt((summed[24:32] + EPSILON) * (summed[16:24] + EPSILON))
        for k in range(2):
            rows = summed[8 * k : 8 * k + 8] * scale
            for j in range(Y):
                out_ref[2 * j + side, k] = rows[2 * j : 2 * j + 2]


def call(kernel, out_shape, operands, scratch=(), flops=0):
    return pl.pallas_call(
        kernel,
        out_shape=out_shape,
        in_specs=[VMEM] * len(operands),
        out_specs=jax.tree.map(lambda _: VMEM, out_shape),
        scratch_shapes=list(scratch),
        compiler_params=pltpu.CompilerParams(vmem_limit_bytes=VMEM_LIMIT),
        cost_estimate=pl.CostEstimate(flops=flops, bytes_accessed=1 << 20, transcendentals=0),
    )(*operands)


def looks(kernel, out_shape, operands, fields, samples):
    rows = 2 * fields * LINES
    scratch = [pltpu.VMEM((rows, samples), bf16), pltpu.VMEM((rows, 2 * LANES), f32)]
    return call(kernel, out_shape, operands, scratch, flops=2 * rows * samples * 2 * LANES)


def local(stack):
    tiles = lax.axis_size("rng")
    blocks = stack.shape[-1] // (Y * LANES)
    axes = ("pair", "rng")

    def device(y, h, n):
        return (2 * y + h) * tiles + n

    across = [(device(y, h, n), device(y, 1 - h, n)) for y in range(Y) for h in range(2) for n in range(tiles)]
    swap = []
    for h in range(2):
        for n in range(tiles - 1):
            y = 0 if n % 2 else Y - 1
            swap += [(device(y, h, n), device(y, h, n + 1)), (device(y, h, n + 1), device(y, h, n))]

    chunks = call(cut_kernel, jax.ShapeDtypeStruct((Y, 2, blocks, LINES, LANES), bf16), (stack,))
    group = lax.all_to_all(chunks, "pair", 0, 0, axis_index_groups=GROUPS)
    edge = call(edge_kernel, jax.ShapeDtypeStruct((2, LINES, LANES), bf16), (group,))
    halo = lax.ppermute(edge, axes, swap)
    group = call(join_kernel, jax.ShapeDtypeStruct((2 * Y * blocks + 2, LINES, LANES), bf16), (group, halo))
    other = lax.ppermute(group, axes, across)

    samples = (blocks + 1) * LANES
    inner, weights = looks(
        inner_kernel,
        (jax.ShapeDtypeStruct((2 * N_INNER, LANES), f32), jax.ShapeDtypeStruct((samples, 2 * LANES), bf16)),
        (group,),
        N_INNER,
        samples,
    )
    parts = looks(
        outer_kernel,
        jax.ShapeDtypeStruct((Y, 2, 32, LANES), f32),
        (group, other, weights, inner),
        N_OUTER,
        samples,
    )
    parts = lax.all_to_all(parts, "pair", 0, 0, axis_index_groups=GROUPS)
    out = call(normalise_kernel, jax.ShapeDtypeStruct((2 * Y, 2, 2, LANES), f32), (parts,))
    return out[None]


def solution(mesh):
    in_specs = (P("pair", None, None, "rng"),)
    out_specs = P("pair", None, None, None, "rng")
    return jax.shard_map(local, mesh=mesh, in_specs=in_specs, out_specs=out_specs, check_vma=False)
```

time: 66 us -> 57.6 us (0.87)
  the two profiles are of different devices: /device:TPU:96 before, /device:TPU:38 now
where the time goes in v2:
time: 57.6 us; the launch traced here: 57.4 us
  blocking collectives  18.8 us (33%)
  waiting for transfers between devices  18.4 us (32%)
  starting transfers between devices  16.7 us (29%)
  Pallas kernels  2.48 us (4%)
  local copies, waits for them, and re-layouts  0.92 us (2%)
    ppermute x1, waiting for transfers between devices, local(): other = lax.ppermute(group, axes, across)  15.4 us
    ppermute x1, starting transfers between devices, local(): other = lax.ppermute(group, axes, across)  14.8 us
    all_to_all x1, blocking collectives, local(): group = lax.all_to_all(chunks, 'pair', 0, 0, axis_index_groups=GROUPS)  10.4 us
    all_to_all x1, blocking collectives, local(): parts = lax.all_to_all(parts, 'pair', 0, 0, axis_index_groups=GROUPS)  8.36 us
    ppermute x1, waiting for transfers between devices, local(): halo = lax.ppermute(edge, axes, swap)  3.04 us
    pallas_call x6, Pallas kernels, call(): pl.pallas_call(kernel, out_shape=out_shape, in_specs=[VMEM] * len(operand...  2.48 us
    ppermute x1, starting transfers between devices, local(): halo = lax.ppermute(edge, axes, swap)  1.91 us
  transfers between devices with their start and end apart: 2, of which 2 were waited for; matrix products, arithmetic and copies ran while one was open for 0% of the time, Pallas kernels for 1%

profile of v2, /device:TPU:38, one launch (start us, length us, event | category | flops | bytes accessed | tf_op | source)
XLA Modules:
  0.0 57.4 jit_solution(2232609209783640374)
XLA Ops:
  0.0 0.0 copy-start
  0.0 0.9 %copy-done = bf16[1,2,16,2560]{3,2,1,0:T(8,128)(2,1)S(1)} copy-done((bf16[1,2,16,2560]{3,2,1,0:T(8,128)(2,1)S(1)}, bf16[1,2,16,2560]{3,2,1,0:T(8,128)(2,1)}, u32[]{:S(2)}) %copy-start) | copy-done | bytes 163864
  1.0 10.4 %all_to_all.10.group_ref = bf16[4,2,5,16,128]{4,3,2,1,0:T(8,128)(2,1)S(1)} all-to-all(bf16[4,2,5,16,128]{4,3,2,1,0:T(8,128)(2,1)S(1)} %shard_map.17), channel_id=1, replica_groups={{0,128,256,384},{64,192,320,448},{1,129,257,385},{65,193,321,449},{2,13..., dimensions={0} | all-to-all | bytes 327680 | tf_op jit(solution)/shard_map/all_to_all | solution.py:243
  11.4 0.1 shard_map.18
  11.5 1.9 %collective-permute-start = (bf16[2,16,128]{2,1,0:T(8,128)(2,1)S(1)}, bf16[2,16,128]{2,1,0:T(8,128)(2,1)S(1)}, u32[]{:S(2)}, u32[]{:S(2)}) collective-permute-start(bf16[2,16,128]{2,1,0:T(8,128)(2,1)S(1)} %shard_map.18), channel_id=1, source_target_pairs={{384,385},{385,384},{1,2},{2,1},{386,387},{387,386},{3,4},{4,3},{3... | collective-permute-start | bytes 24584 | tf_op jit(solution)/shard_map/ppermute | solution.py:245
  13.4 3.0 %collective-permute-done.halo_ref = bf16[2,16,128]{2,1,0:T(8,128)(2,1)S(1)} collective-permute-done((bf16[2,16,128]{2,1,0:T(8,128)(2,1)S(1)}, bf16[2,16,128]{2,1,0:T(8,128)(2,1)S(1)}, u32[]{:S(2)}, u32[]{:S(2)}) %collective-permute-start) | collective-permute-done | bytes 8224 | tf_op jit(solution)/shard_map/ppermute | solution.py:245
  16.5 14.8 %collective-permute-start.1 = (bf16[42,16,128]{2,1,0:T(8,128)(2,1)S(1)}, bf16[42,16,128]{2,1,0:T(8,128)(2,1)S(1)}, u32[]{:S(2)}, u32[]{:S(2)}) collective-permute-start(bf16[42,16,128]{2,1,0:T(8,128)(2,1)S(1)} %shard_map.19.group_ref), channel_id=1, source_target_pairs={{0,64},{1,65},{2,66},{3,67},{4,68},{5,69},{6,70},{7,71},{8,72},{9,... | collective-permute-start | bytes 516104 | tf_op jit(solution)/shard_map/ppermute | solution.py:247
  31.3 0.8 %shard_map.20 = (f32[32,128]{1,0:T(8,128)S(1)}, bf16[768,256]{1,0:T(8,128)(2,1)S(1)}) custom-call(bf16[42,16,128]{2,1,0:T(8,128)(2,1)S(1)} %shard_map.19.group_ref), custom_call_target="tpu_custom_call" | custom-call | flops 201326592 | bytes 1048576 | tf_op jit(solution)/shard_map/pallas_call | solution.py:210
  32.1 15.4 %collective-permute-done.1.other_ref = bf16[42,16,128]{2,1,0:T(8,128)(2,1)S(1)} collective-permute-done((bf16[42,16,128]{2,1,0:T(8,128)(2,1)S(1)}, bf16[42,16,128]{2,1,0:T(8,128)(2,1)S(1)}, u32[]{:S(2)}, u32[]{:S(2)}) %collective-permute-start.1) | collective-permute-done | bytes 172064 | tf_op jit(solution)/shard_map/ppermute | solution.py:247
  47.5 0.9 %shard_map.21 = f32[4,2,32,128]{3,2,1,0:T(8,128)S(1)} custom-call(bf16[42,16,128]{2,1,0:T(8,128)(2,1)S(1)} %shard_map.19.group_ref, bf16[42,16,128]{2,1,0:T(8,128)(2,1)S(1)} %collective-permute-done.1.other_ref, bf16[768,256]{1,0:T(8,128)(2,1)S(1)} %get-tuple-element.7.weight_ref, f32[32,128]{1,0:T(8,128)S(1)} %get-tuple-element.8.inner_ref), custom_call_target="tpu_custom_call" | custom-call | flops 452984832 | bytes 1048576 | tf_op jit(solution)/shard_map/pallas_call | solution.py:210
  48.4 8.4 %all_to_all.11.parts_ref = f32[4,2,32,128]{3,2,1,0:T(8,128)S(1)} all-to-all(f32[4,2,32,128]{3,2,1,0:T(8,128)S(1)} %shard_map.21), channel_id=1, replica_groups={{0,128,256,384},{64,192,320,448},{1,129,257,385},{65,193,321,449},{2,13..., dimensions={0} | all-to-all | bytes 262144 | tf_op jit(solution)/shard_map/all_to_all | solution.py:264
  56.7 0.6 %shard_map.22 = f32[8,2,2,128]{3,2,1,0:T(2,128)} custom-call(f32[4,2,32,128]{3,2,1,0:T(8,128)S(1)} %all_to_all.11.parts_ref), custom_call_target="tpu_custom_call" | custom-call | bytes 1048576 | tf_op jit(solution)/shard_map/pallas_call | solution.py:210
  (2 shorter events, 0.0 us)
Async XLA Ops:
  0.0 0.9 %copy-start = (bf16[1,2,16,2560]{3,2,1,0:T(8,128)(2,1)S(1)}, bf16[1,2,16,2560]{3,2,1,0:T(8,128)(2,1)}, u32[]{:S(2)}) copy-start(bf16[1,2,16,2560]{3,2,1,0:T(8,128)(2,1)} %stack_ref.1) | copy-start | bytes 491524
  11.5 5.0 %collective-permute-start = (bf16[2,16,128]{2,1,0:T(8,128)(2,1)S(1)}, bf16[2,16,128]{2,1,0:T(8,128)(2,1)S(1)}, u32[]{:S(2)}, u32[]{:S(2)}) collective-permute-start(bf16[2,16,128]{2,1,0:T(8,128)(2,1)S(1)} %shard_map.18), channel_id=1, source_target_pairs={{384,385},{385,384},{1,2},{2,1},{386,387},{387,386},{3,4},{4,3},{3... | collective-permute-start | bytes 24584 | tf_op jit(solution)/shard_map/ppermute | solution.py:245
  16.5 31.0 %collective-permute-start.1 = (bf16[42,16,128]{2,1,0:T(8,128)(2,1)S(1)}, bf16[42,16,128]{2,1,0:T(8,128)(2,1)S(1)}, u32[]{:S(2)}, u32[]{:S(2)}) collective-permute-start(bf16[42,16,128]{2,1,0:T(8,128)(2,1)S(1)} %shard_map.19.group_ref), channel_id=1, source_target_pairs={{0,64},{1,65},{2,66},{3,67},{4,68},{5,69},{6,70},{7,71},{8,72},{9,... | collective-permute-start | bytes 516104 | tf_op jit(solution)/shard_map/ppermute | solution.py:247

commit v3 on v2

--- a/solution.py
+++ b/solution.py
@@ -18,6 +18,9 @@
 Y = 4
 GROUPS = [[0, 2, 4, 6], [1, 3, 5, 7]]
 INNER = [(i, j) for i in range(Y) for j in range(i + 1, Y)]
+SHARES = (3, 6, 6, 5)
+BLOCKS = max(SHARES)
+EDGES = (0, Y - 1)
 N_INNER = Y + 2 * len(INNER)
 N_OUTER = Y + 2 * Y * Y
 
@@ -26,13 +29,24 @@
 VMEM = pl.BlockSpec(memory_space=pltpu.VMEM)
 
 
-def quarter_of(y):
-    return jnp.where(lax.axis_index("rng") % 2 == 1, Y - 1 - y, y)
-
-
-def here():
+def place():
     pair = lax.axis_index("pair")
-    return quarter_of(pair // 2), pair % 2
+    return pair // 2, pair % 2, lax.axis_index("rng") % 2 == 1
+
+
+def start_of(y, odd):
+    return jnp.where(odd, sum(SHARES[y + 1 :]), sum(SHARES[:y]))
+
+
+def pick(y, values):
+    out = jnp.int32(values[0])
+    for i in range(1, Y):
+        out = jnp.where(y == i, values[i], out)
+    return out
+
+
+def at_left(y, odd):
+    return (y == 0) != odd
 
 
 def lanes(rows):
@@ -50,64 +64,75 @@
     return weights
 
 
-def range_weights(quarter, width):
-    shape = (width + LANES, LANES)
+def range_weights(y, odd):
+    shape = (BLOCKS * LANES, LANES)
     row = lax.broadcasted_iota(jnp.int32, shape, 0)
     look = lax.broadcasted_iota(jnp.int32, shape, 1)
-    halo = row - width + jnp.where(quarter == 0, -RG_STEP, Y * width)
-    sample = jnp.where(row < width, quarter * width + row, halo)
+    start = jnp.where(odd, pick(y, [sum(SHARES[i + 1 :]) for i in range(Y)]), pick(y, [sum(SHARES[:i]) for i in range(Y)]))
+    count = pick(y, SHARES) * LANES
+    halo = row - (BLOCKS - 1) * LANES
+    beyond = halo + jnp.where(at_left(y, odd), -RG_STEP, sum(SHARES) * LANES)
+    own = row < count
+    sample = jnp.where(own, start * LANES + row, beyond)
     tap = sample - RG_STEP * (look - 1)
     centred = (tap.astype(f32) - (RG_TAPS - 1) / 2.0) / (RG_TAPS / 4.0)
-    inside = (tap >= 0) & (tap < RG_TAPS) & (row < width + RG_STEP)
+    inside = (tap >= 0) & (tap < RG_TAPS) & (own | ((halo >= 0) & (halo < RG_STEP)))
     return jnp.where(inside, 2.0 * jnp.exp(-0.5 * centred * centred), 0.0)
 
 
 def cut_kernel(stack_ref, out_ref):
-    blocks = out_ref.shape[2]
-    for q in range(Y):
-        to = quarter_of(q)
+    _, _, odd = place()
+    for y in range(Y):
+        start = start_of(y, odd)
         for part in range(2):
-            for t in range(blocks):
-                at = (q * blocks + t) * LANES
-                out_ref[to, part, t] = stack_ref[0, part, :, at : at + LANES]
+            for t in range(BLOCKS):
+                if t < SHARES[y]:
+                    at = pl.multiple_of((start + t) * LANES, LANES)
+                    out_ref[y, part, t] = stack_ref[0, part, :, pl.ds(at, LANES)]
+                else:
+                    out_ref[y, part, t] = jnp.zeros((LINES, LANES), bf16)
 
 
 def edge_kernel(group_ref, edge_ref):
-    quarter, _ = here()
-    blocks = group_ref.shape[2]
+    y, _, odd = place()
     for part in range(2):
         packed = jnp.zeros((LINES, LANES), f32)
         for i in range(Y):
             first = group_ref[i, part, 0].astype(f32)
-            last = group_ref[i, part, blocks - 1].astype(f32)
-            edge = jnp.where(quarter == Y - 1, pltpu.roll(last, RG_STEP, 1), first)
+            last = jnp.where(y == 0, group_ref[i, part, SHARES[0] - 1], group_ref[i, part, SHARES[Y - 1] - 1]).astype(f32)
+            edge = jnp.where(at_left(y, odd), first, pltpu.roll(last, RG_STEP, 1))
             edge = jnp.where(lanes(LINES) < RG_STEP, edge, 0.0)
             packed = packed + (pltpu.roll(edge, SLOT * i, 1) if i else edge)
         edge_ref[part] = packed.astype(bf16)
 
 
-def join_kernel(group_ref, halo_ref, out_ref):
-    blocks = group_ref.shape[2]
-    for i in range(Y):
+def join_kernel(group_ref, halo_ref, *out_refs):
+    for out_ref, y in zip(out_refs, EDGES):
+        share = SHARES[y]
+        for i in range(Y):
+            for part in range(2):
+                for t in range(share):
+                    out_ref[(2 * i + part) * share + t] = group_ref[i, part, t]
         for part in range(2):
-            for t in range(blocks):
-                out_ref[(2 * i + part) * blocks + t] = group_ref[i, part, t]
-    for part in range(2):
-        out_ref[2 * Y * blocks + part] = halo_ref[part]
-
-
-def blocks_of(ref):
-    return (ref.shape[0] - 2) // (2 * Y)
-
-
-def dates_at(ref, t):
-    blocks = blocks_of(ref)
-    if t < blocks:
-        return [tuple(ref[(2 * i + part) * blocks + t].astype(f32) for part in range(2)) for i in range(Y)]
-    packed = [ref[2 * Y * blocks + part].astype(f32) for part in range(2)]
-    inside = lanes(LINES) < RG_STEP
-    rolled = [[pltpu.roll(p, LANES - SLOT * i, 1) if i else p for p in packed] for i in range(Y)]
-    return [tuple(jnp.where(inside, p, 0.0) for p in date) for date in rolled]
+            out_ref[2 * Y * share + part] = halo_ref[part]
+
+
+def unpack(packed, i):
+    rolled = pltpu.roll(packed, LANES - SLOT * i, 1) if i else packed
+    return jnp.where(lanes(LINES) < RG_STEP, rolled, 0.0)
+
+
+def dates_at(ref, t, halos, joined=()):
+    def one(i, part):
+        value = ref[i, part, t].astype(f32)
+        for joined_ref, y in joined:
+            if t < SHARES[y]:
+                value = value + joined_ref[(2 * i + part) * SHARES[y] + t].astype(f32)
+        if t == BLOCKS - 1:
+            value = value + unpack(halos[part], i)
+        return value
+
+    return [(one(i, 0), one(i, 1)) for i in range(Y)]
 
 
 def power(date):
@@ -142,26 +167,29 @@
             yield field, a, jnp.sum(summed * weight, axis=0, keepdims=True)
 
 
-def inner_kernel(group_ref, out_ref, weight_ref, x_ref, d_ref):
-    blocks = blocks_of(group_ref)
-    quarter, _ = here()
-    weights = range_weights(quarter, blocks * LANES)
+def inner_kernel(group_ref, halo_ref, out_ref, weight_ref, x_ref, d_ref):
+    y, _, odd = place()
+    weights = range_weights(y, odd)
     high = weights.astype(bf16)
     weight_ref[:, 0:LANES] = high
     weight_ref[:, LANES : 2 * LANES] = (weights - high.astype(f32)).astype(bf16)
-    for t in range(blocks + 1):
-        group = dates_at(group_ref, t)
+    halos = [halo_ref[part].astype(f32) for part in range(2)]
+    for t in range(BLOCKS):
+        group = dates_at(group_ref, t, halos)
         fields = [power(d) for d in group] + [cross(group[i], group[j]) for i, j in INNER]
         put(x_ref, N_INNER, t, [value for field in fields for value in field])
     for field, a, row in looks_of(x_ref, weight_ref[...], d_ref, N_INNER):
         out_ref[2 * field + a : 2 * field + a + 1, :] = row
 
 
-def outer_kernel(group_ref, other_ref, weight_ref, inner_ref, out_ref, x_ref, d_ref):
-    _, own = here()
+def outer_kernel(group_ref, halo_ref, other_ref, first_ref, last_ref, weight_ref, inner_ref, out_ref, x_ref, d_ref):
+    _, own, _ = place()
     across = 1 - own
-    for t in range(blocks_of(group_ref) + 1):
-        group, other = dates_at(group_ref, t), dates_at(other_ref, t)
+    halos = [halo_ref[part].astype(f32) for part in range(2)]
+    joined = list(zip((first_ref, last_ref), EDGES))
+    other_halos = [sum(ref[2 * Y * SHARES[y] + part].astype(f32) for ref, y in joined) for part in range(2)]
+    for t in range(BLOCKS):
+        group, other = dates_at(group_ref, t, halos), dates_at(other_ref, t, other_halos, joined)
         fields = [power(d) for d in other] + [cross(i, j) for i in group for j in other]
         put(x_ref, N_OUTER, t, [value for field in fields for value in field])
 
@@ -218,48 +246,48 @@
     )(*operands)
 
 
-def looks(kernel, out_shape, operands, fields, samples):
-    rows = 2 * fields * LINES
+def looks(kernel, out_shape, operands, fields):
+    rows, samples = 2 * fields * LINES, BLOCKS * LANES
     scratch = [pltpu.VMEM((rows, samples), bf16), pltpu.VMEM((rows, 2 * LANES), f32)]
     return call(kernel, out_shape, operands, scratch, flops=2 * rows * samples * 2 * LANES)
 
 
 def local(stack):
     tiles = lax.axis_size("rng")
-    blocks = stack.shape[-1] // (Y * LANES)
     axes = ("pair", "rng")
 
     def device(y, h, n):
         return (2 * y + h) * tiles + n
 
-    across = [(device(y, h, n), device(y, 1 - h, n)) for y in range(Y) for h in range(2) for n in range(tiles)]
+    def across(*ys):
+        return [(device(y, h, n), device(y, 1 - h, n)) for y in ys for h in range(2) for n in range(tiles)]
+
     swap = []
     for h in range(2):
         for n in range(tiles - 1):
-            y = 0 if n % 2 else Y - 1
+            y = EDGES[(n + 1) % 2]
             swap += [(device(y, h, n), device(y, h, n + 1)), (device(y, h, n + 1), device(y, h, n))]
 
-    chunks = call(cut_kernel, jax.ShapeDtypeStruct((Y, 2, blocks, LINES, LANES), bf16), (stack,))
+    chunks = call(cut_kernel, jax.ShapeDtypeStruct((Y, 2, BLOCKS, LINES, LANES), bf16), (stack,))
     group = lax.all_to_all(chunks, "pair", 0, 0, axis_index_groups=GROUPS)
+    other = lax.ppermute(group, axes, across(1, 2))
     edge = call(edge_kernel, jax.ShapeDtypeStruct((2, LINES, LANES), bf16), (group,))
     halo = lax.ppermute(edge, axes, swap)
-    group = call(join_kernel, jax.ShapeDtypeStruct((2 * Y * blocks + 2, LINES, LANES), bf16), (group, halo))
-    other = lax.ppermute(group, axes, across)
-
-    samples = (blocks + 1) * LANES
-    inner, weights = looks(
-        inner_kernel,
-        (jax.ShapeDtypeStruct((2 * N_INNER, LANES), f32), jax.ShapeDtypeStruct((samples, 2 * LANES), bf16)),
-        (group,),
-        N_INNER,
-        samples,
+    shapes = tuple(jax.ShapeDtypeStruct((2 * Y * SHARES[y] + 2, LINES, LANES), bf16) for y in EDGES)
+    first, last = call(join_kernel, shapes, (group, halo))
+    first = lax.ppermute(first, axes, across(0))
+    last = lax.ppermute(last, axes, across(Y - 1))
+
+    shapes = (
+        jax.ShapeDtypeStruct((2 * N_INNER, LANES), f32),
+        jax.ShapeDtypeStruct((BLOCKS * LANES, 2 * LANES), bf16),
     )
+    inner, weights = looks(inner_kernel, shapes, (group, halo), N_INNER)
     parts = looks(
         outer_kernel,
         jax.ShapeDtypeStruct((Y, 2, 32, LANES), f32),
-        (group, other, weights, inner),
+        (group, halo, other, first, last, weights, inner),
         N_OUTER,
-        samples,
     )
     parts = lax.all_to_all(parts, "pair", 0, 0, axis_index_groups=GROUPS)
     out = call(normalise_kernel, jax.ShapeDtypeStruct((2 * Y, 2, 2, LANES), f32), (parts,))

time: 57.6 us -> 55 us (0.955)
  waiting for transfers between devices: 18.4 us -> 12.7 us
  blocking collectives: 18.8 us -> 20.3 us
  starting transfers between devices: 16.7 us -> 18.1 us
    ppermute x1 -> x3, waiting for transfers between devices: 15.4 us -> 9.65 us  [the longest x1 9.64 us: local(): first = lax.ppermute(first, axes, across(0))]
    all_to_all x1, blocking collectives: 8.36 us -> 9.74 us  [local(): parts = lax.all_to_all(parts, 'pair', 0, 0, axis_index_groups=GROUPS)]
    ppermute x1 -> x3, starting transfers between devices: 14.8 us -> 16.2 us  [the longest x1 14.8 us: local(): first = lax.ppermute(first, axes, across(0))]
  transfers between devices with their start and end apart: 2 -> 4, of which waited for: 2 -> 2; matrix products, arithmetic and copies ran while one was open for 0% -> 0% of each run, Pallas kernels for 1% -> 2%
where the time goes in v3:
time: 55 us; the launch traced here: 54.8 us
  blocking collectives  20.3 us (37%)
  starting transfers between devices  18.1 us (33%)
  waiting for transfers between devices  12.7 us (23%)
  Pallas kernels  2.69 us (5%)
  local copies, waits for them, and re-layouts  0.92 us (2%)
    ppermute x1, starting transfers between devices, local(): first = lax.ppermute(first, axes, across(0))  14.8 us
    all_to_all x1, blocking collectives, local(): group = lax.all_to_all(chunks, 'pair', 0, 0, axis_index_groups=GROUPS)  10.6 us
    all_to_all x1, blocking collectives, local(): parts = lax.all_to_all(parts, 'pair', 0, 0, axis_index_groups=GROUPS)  9.74 us
    ppermute x1, waiting for transfers between devices, local(): first = lax.ppermute(first, axes, across(0))  9.64 us
    ppermute x1, waiting for transfers between devices, local(): halo = lax.ppermute(edge, axes, swap)  3.04 us
    pallas_call x6, Pallas kernels, call(): pl.pallas_call(kernel, out_shape=out_shape, in_specs=[VMEM] * len(operand...  2.69 us
    ppermute x1, starting transfers between devices, local(): halo = lax.ppermute(edge, axes, swap)  1.91 us
  transfers between devices with their start and end apart: 4, of which 2 were waited for; matrix products, arithmetic and copies ran while one was open for 0% of the time, Pallas kernels for 2%

profile of v3, /device:TPU:38, one launch (start us, length us, event | category | flops | bytes accessed | tf_op | source)
XLA Modules:
  0.0 54.8 jit_solution(7321781568138962283)
XLA Ops:
  0.0 0.0 copy-start
  0.0 0.9 %copy-done = bf16[1,2,16,2560]{3,2,1,0:T(8,128)(2,1)S(1)} copy-done((bf16[1,2,16,2560]{3,2,1,0:T(8,128)(2,1)S(1)}, bf16[1,2,16,2560]{3,2,1,0:T(8,128)(2,1)}, u32[]{:S(2)}) %copy-start) | copy-done | bytes 163864
  1.0 10.6 %all_to_all.10.group_ref = bf16[4,2,6,16,128]{4,3,2,1,0:T(8,128)(2,1)S(1)} all-to-all(bf16[4,2,6,16,128]{4,3,2,1,0:T(8,128)(2,1)S(1)} %shard_map.17), channel_id=1, replica_groups={{0,128,256,384},{64,192,320,448},{1,129,257,385},{65,193,321,449},{2,13..., dimensions={0} | all-to-all | bytes 393216 | tf_op jit(solution)/shard_map/all_to_all | solution.py:272
  11.6 0.7 %collective-permute-start.1 = (bf16[4,2,6,16,128]{4,3,2,1,0:T(8,128)(2,1)S(1)}, bf16[4,2,6,16,128]{4,3,2,1,0:T(8,128)(2,1)S(1)}, u32[]{:S(2)}, u32[]{:S(2)}) collective-permute-start(bf16[4,2,6,16,128]{4,3,2,1,0:T(8,128)(2,1)S(1)} %all_to_all.10.group_ref), channel_id=1, source_target_pairs={{128,192},{129,193},{130,194},{131,195},{132,196},{133,197},{134,1... | collective-permute-start | bytes 589832 | tf_op jit(solution)/shard_map/ppermute | solution.py:273
  12.2 0.2 shard_map.18
  12.4 1.9 %collective-permute-start = (bf16[2,16,128]{2,1,0:T(8,128)(2,1)S(1)}, bf16[2,16,128]{2,1,0:T(8,128)(2,1)S(1)}, u32[]{:S(2)}, u32[]{:S(2)}) collective-permute-start(bf16[2,16,128]{2,1,0:T(8,128)(2,1)S(1)} %shard_map.18), channel_id=1, source_target_pairs={{384,385},{385,384},{1,2},{2,1},{386,387},{387,386},{3,4},{4,3},{3... | collective-permute-start | bytes 24584 | tf_op jit(solution)/shard_map/ppermute | solution.py:275
  14.3 3.0 %collective-permute-done.halo_ref = bf16[2,16,128]{2,1,0:T(8,128)(2,1)S(1)} collective-permute-done((bf16[2,16,128]{2,1,0:T(8,128)(2,1)S(1)}, bf16[2,16,128]{2,1,0:T(8,128)(2,1)S(1)}, u32[]{:S(2)}, u32[]{:S(2)}) %collective-permute-start) | collective-permute-done | bytes 8224 | tf_op jit(solution)/shard_map/ppermute | solution.py:275
  17.4 0.7 %collective-permute-start.3 = (bf16[42,16,128]{2,1,0:T(8,128)(2,1)S(1)}, bf16[42,16,128]{2,1,0:T(8,128)(2,1)S(1)}, u32[]{:S(2)}, u32[]{:S(2)}) collective-permute-start(bf16[42,16,128]{2,1,0:T(8,128)(2,1)S(1)} %get-tuple-element.10), channel_id=1, source_target_pairs={{384,448},{385,449},{386,450},{387,451},{388,452},{389,453},{390,4... | collective-permute-start | bytes 516104 | tf_op jit(solution)/shard_map/ppermute | solution.py:279
  18.1 14.8 %collective-permute-start.2 = (bf16[26,16,128]{2,1,0:T(8,128)(2,1)S(1)}, bf16[26,16,128]{2,1,0:T(8,128)(2,1)S(1)}, u32[]{:S(2)}, u32[]{:S(2)}) collective-permute-start(bf16[26,16,128]{2,1,0:T(8,128)(2,1)S(1)} %get-tuple-element.9), channel_id=1, source_target_pairs={{0,64},{1,65},{2,66},{3,67},{4,68},{5,69},{6,70},{7,71},{8,72},{9,... | collective-permute-start | bytes 319496 | tf_op jit(solution)/shard_map/ppermute | solution.py:278
  32.9 0.9 %shard_map.20 = (f32[32,128]{1,0:T(8,128)S(1)}, bf16[768,256]{1,0:T(8,128)(2,1)S(1)}) custom-call(bf16[4,2,6,16,128]{4,3,2,1,0:T(8,128)(2,1)S(1)} %all_to_all.10.group_ref, bf16[2,16,128]{2,1,0:T(8,128)(2,1)S(1)} %collective-permute-done.halo_ref), custom_call_target="tpu_custom_call" | custom-call | flops 201326592 | bytes 1048576 | tf_op jit(solution)/shard_map/pallas_call | solution.py:238
  33.8 9.6 %collective-permute-done.2.first_ref = bf16[26,16,128]{2,1,0:T(8,128)(2,1)S(1)} collective-permute-done((bf16[26,16,128]{2,1,0:T(8,128)(2,1)S(1)}, bf16[26,16,128]{2,1,0:T(8,128)(2,1)S(1)}, u32[]{:S(2)}, u32[]{:S(2)}) %collective-permute-start.2) | collective-permute-done | bytes 106528 | tf_op jit(solution)/shard_map/ppermute | solution.py:278
  43.4 0.0 collective-permute-done.3.last_ref
  43.4 0.0 collective-permute-done.1.other_ref
  43.4 1.0 %shard_map.21 = f32[4,2,32,128]{3,2,1,0:T(8,128)S(1)} custom-call(bf16[4,2,6,16,128]{4,3,2,1,0:T(8,128)(2,1)S(1)} %all_to_all.10.group_ref, bf16[2,16,128]{2,1,0:T(8,128)(2,1)S(1)} %collective-permute-done.halo_ref, bf16[4,2,6,16,128]{4,3,2,1,0:T(8,128)(2,1)S(1)} %collective-permute-done.1.other_ref, ...), custom_call_target="tpu_custom_call" | custom-call | flops 452984832 | bytes 1048576 | tf_op jit(solution)/shard_map/pallas_call | solution.py:238
  44.4 9.7 %all_to_all.11.parts_ref = f32[4,2,32,128]{3,2,1,0:T(8,128)S(1)} all-to-all(f32[4,2,32,128]{3,2,1,0:T(8,128)S(1)} %shard_map.21), channel_id=1, replica_groups={{0,128,256,384},{64,192,320,448},{1,129,257,385},{65,193,321,449},{2,13..., dimensions={0} | all-to-all | bytes 262144 | tf_op jit(solution)/shard_map/all_to_all | solution.py:292
  54.1 0.6 %shard_map.22 = f32[8,2,2,128]{3,2,1,0:T(2,128)} custom-call(f32[4,2,32,128]{3,2,1,0:T(8,128)S(1)} %all_to_all.11.parts_ref), custom_call_target="tpu_custom_call" | custom-call | bytes 1048576 | tf_op jit(solution)/shard_map/pallas_call | solution.py:238
  (2 shorter events, 0.1 us)
Async XLA Ops:
  0.0 0.9 %copy-start = (bf16[1,2,16,2560]{3,2,1,0:T(8,128)(2,1)S(1)}, bf16[1,2,16,2560]{3,2,1,0:T(8,128)(2,1)}, u32[]{:S(2)}) copy-start(bf16[1,2,16,2560]{3,2,1,0:T(8,128)(2,1)} %stack_ref.1) | copy-start | bytes 491524
  11.6 31.9 %collective-permute-start.1 = (bf16[4,2,6,16,128]{4,3,2,1,0:T(8,128)(2,1)S(1)}, bf16[4,2,6,16,128]{4,3,2,1,0:T(8,128)(2,1)S(1)}, u32[]{:S(2)}, u32[]{:S(2)}) collective-permute-start(bf16[4,2,6,16,128]{4,3,2,1,0:T(8,128)(2,1)S(1)} %all_to_all.10.group_ref), channel_id=1, source_target_pairs={{128,192},{129,193},{130,194},{131,195},{132,196},{133,197},{134,1... | collective-permute-start | bytes 589832 | tf_op jit(solution)/shard_map/ppermute | solution.py:273
  12.4 5.0 %collective-permute-start = (bf16[2,16,128]{2,1,0:T(8,128)(2,1)S(1)}, bf16[2,16,128]{2,1,0:T(8,128)(2,1)S(1)}, u32[]{:S(2)}, u32[]{:S(2)}) collective-permute-start(bf16[2,16,128]{2,1,0:T(8,128)(2,1)S(1)} %shard_map.18), channel_id=1, source_target_pairs={{384,385},{385,384},{1,2},{2,1},{386,387},{387,386},{3,4},{4,3},{3... | collective-permute-start | bytes 24584 | tf_op jit(solution)/shard_map/ppermute | solution.py:275
  17.4 26.0 %collective-permute-start.3 = (bf16[42,16,128]{2,1,0:T(8,128)(2,1)S(1)}, bf16[42,16,128]{2,1,0:T(8,128)(2,1)S(1)}, u32[]{:S(2)}, u32[]{:S(2)}) collective-permute-start(bf16[42,16,128]{2,1,0:T(8,128)(2,1)S(1)} %get-tuple-element.10), channel_id=1, source_target_pairs={{384,448},{385,449},{386,450},{387,451},{388,452},{389,453},{390,4... | collective-permute-start | bytes 516104 | tf_op jit(solution)/shard_map/ppermute | solution.py:279
  18.1 25.4 %collective-permute-start.2 = (bf16[26,16,128]{2,1,0:T(8,128)(2,1)S(1)}, bf16[26,16,128]{2,1,0:T(8,128)(2,1)S(1)}, u32[]{:S(2)}, u32[]{:S(2)}) collective-permute-start(bf16[26,16,128]{2,1,0:T(8,128)(2,1)S(1)} %get-tuple-element.9), channel_id=1, source_target_pairs={{0,64},{1,65},{2,66},{3,67},{4,68},{5,69},{6,70},{7,71},{8,72},{9,... | collective-permute-start | bytes 319496 | tf_op jit(solution)/shard_map/ppermute | solution.py:278

commit v4 on v3

v4 whole, which is shorter than its diff:
```python
import jax
import jax.numpy as jnp
from jax import lax
from jax.experimental import pallas as pl
from jax.experimental.pallas import tpu as pltpu
from jax.sharding import PartitionSpec as P

AZ_TAPS = 31
RG_TAPS = 60
AZ_STEP = 8
RG_STEP = 20
LINES = 16
LANES = 128
SLOT = 32
WINDOW = 64
EPSILON = 1e-06
VMEM_LIMIT = 8 << 20

Y = 4
GROUPS = [[0, 2, 4, 6], [1, 3, 5, 7]]
INNER = [(i, j) for i in range(Y) for j in range(i + 1, Y)]
SHARES = (2, 6, 6, 6)
BLOCKS = max(SHARES)
LOOKS = sum(SHARES) * LANES // RG_STEP
N_INNER = Y + 2 * len(INNER)
N_OUTER = Y + 2 * Y * Y

f32 = jnp.float32
bf16 = jnp.bfloat16
VMEM = pl.BlockSpec(memory_space=pltpu.VMEM)


def place():
    pair = lax.axis_index("pair")
    return pair // 2, pair % 2, lax.axis_index("rng") % 2 == 1


def starts():
    return [sum(SHARES[:y]) for y in range(Y)], [sum(SHARES[y + 1 :]) for y in range(Y)]


def start_of(y, odd):
    even_tile, odd_tile = starts()
    return jnp.where(odd, odd_tile[y], even_tile[y])


def base_of(y, odd):
    even_tile, odd_tile = ([start * LANES // RG_STEP - 1 for start in tile] for tile in starts())
    return jnp.where(odd, odd_tile[y], even_tile[y])


def pick(y, values):
    out = jnp.int32(values[0])
    for i in range(1, Y):
        out = jnp.where(y == i, values[i], out)
    return out


def lanes(rows):
    return lax.broadcasted_iota(jnp.int32, (rows, LANES), 1)


def azimuth_weights():
    line = lax.broadcasted_iota(jnp.int32, (LINES, LANES), 0)
    weights = []
    for look in range(LINES // AZ_STEP):
        offset = line - (AZ_STEP * look + (AZ_STEP - AZ_TAPS) // 2)
        centred = (offset.astype(f32) - (AZ_TAPS - 1) / 2.0) / (AZ_TAPS / 4.0)
        inside = (offset >= 0) & (offset < AZ_TAPS)
        weights.append(jnp.where(inside, jnp.exp(-0.5 * centred * centred), 0.0))
    return weights


def range_weights(y, odd):
    shape = (BLOCKS * LANES, LANES)
    row = lax.broadcasted_iota(jnp.int32, shape, 0)
    column = lax.broadcasted_iota(jnp.int32, shape, 1) % WINDOW
    look = column + pick(y, [base_of(i, odd) for i in range(Y)])
    start = pick(y, [start_of(i, odd) for i in range(Y)])
    count = pick(y, SHARES) * LANES
    halo = row - (BLOCKS - 1) * LANES
    beyond = halo + jnp.where(odd, sum(SHARES) * LANES, -RG_STEP)
    own = row < count
    sample = jnp.where(own, start * LANES + row, beyond)
    tap = sample - RG_STEP * (look - 1)
    centred = (tap.astype(f32) - (RG_TAPS - 1) / 2.0) / (RG_TAPS / 4.0)
    inside = (tap >= 0) & (tap < RG_TAPS) & (own | ((y == 0) & (halo >= 0) & (halo < RG_STEP)))
    return jnp.where(inside, 2.0 * jnp.exp(-0.5 * centred * centred), 0.0)


def cut_kernel(stack_ref, out_ref):
    _, _, odd = place()
    for y in range(Y):
        start = start_of(y, odd)
        for part in range(2):
            for t in range(BLOCKS):
                if t < SHARES[y]:
                    at = pl.multiple_of((start + t) * LANES, LANES)
                    out_ref[y, part, t] = stack_ref[0, part, :, pl.ds(at, LANES)]
                else:
                    out_ref[y, part, t] = jnp.zeros((LINES, LANES), bf16)


def edge_kernel(group_ref, edge_ref):
    _, _, odd = place()
    for part in range(2):
        packed = jnp.zeros((LINES, LANES), f32)
        for i in range(Y):
            first = group_ref[i, part, 0].astype(f32)
            last = group_ref[i, part, SHARES[0] - 1].astype(f32)
            edge = jnp.where(odd, pltpu.roll(last, RG_STEP, 1), first)
            edge = jnp.where(lanes(LINES) < RG_STEP, edge, 0.0)
            packed = packed + (pltpu.roll(edge, SLOT * i, 1) if i else edge)
        edge_ref[part] = packed.astype(bf16)


def join_kernel(group_ref, halo_ref, out_ref):
    share = SHARES[0]
    for i in range(Y):
        for part in range(2):
            for t in range(share):
                out_ref[(2 * i + part) * share + t] = group_ref[i, part, t]
    for part in range(2):
        out_ref[2 * Y * share + part] = halo_ref[part]


def unpack(packed, i):
    rolled = pltpu.roll(packed, LANES - SLOT * i, 1) if i else packed
    return jnp.where(lanes(LINES) < RG_STEP, rolled, 0.0)


def dates_at(ref, t, halos, joined_ref=None):
    def one(i, part):
        value = ref[i, part, t].astype(f32)
        if joined_ref is not None and t < SHARES[0]:
            value = value + joined_ref[(2 * i + part) * SHARES[0] + t].astype(f32)
        if t == BLOCKS - 1:
            value = value + unpack(halos[part], i)
        return value

    return [(one(i, 0), one(i, 1)) for i in range(Y)]


def power(date):
    x, y = date
    return ((0.5 * x) * x + (0.5 * y) * y,)


def cross(row, column):
    hx, hy = 0.5 * row[0], 0.5 * row[1]
    x, y = column
    return hx * x + hy * y, hy * x - hx * y


def put(x_ref, fields, t, values):
    at = t * LANES
    for field, value in enumerate(values):
        high = value.astype(bf16)
        low = (value - high.astype(f32)).astype(bf16)
        x_ref[field * LINES : (field + 1) * LINES, at : at + LANES] = high
        x_ref[(fields + field) * LINES : (fields + field + 1) * LINES, at : at + LANES] = low


def looks_of(x_ref, weights, d_ref, fields):
    d_ref[...] = jnp.dot(x_ref[...], weights, preferred_element_type=f32)
    azimuth = azimuth_weights()
    for field in range(fields):
        high = d_ref[field * LINES : (field + 1) * LINES, :]
        low = d_ref[(fields + field) * LINES : (fields + field + 1) * LINES, :]
        both = high + low
        summed = both + pltpu.roll(both, WINDOW, 1)
        for a, weight in enumerate(azimuth):
            yield field, a, jnp.sum(summed * weight, axis=0, keepdims=True)


def inner_kernel(group_ref, halo_ref, out_ref, weight_ref, x_ref, d_ref):
    y, _, odd = place()
    weights = range_weights(y, odd)
    high = weights.astype(bf16)
    low = (weights - high.astype(f32)).astype(bf16)
    column = lax.broadcasted_iota(jnp.int32, weights.shape, 1)
    weight_ref[...] = jnp.where(column < WINDOW, high.astype(f32), low.astype(f32)).astype(bf16)
    halos = [halo_ref[part].astype(f32) for part in range(2)]
    for t in range(BLOCKS):
        group = dates_at(group_ref, t, halos)
        fields = [power(d) for d in group] + [cross(group[i], group[j]) for i, j in INNER]
        put(x_ref, N_INNER, t, [value for field in fields for value in field])
    for field, a, row in looks_of(x_ref, weight_ref[...], d_ref, N_INNER):
        out_ref[2 * field + a : 2 * field + a + 1, :] = row


def outer_kernel(group_ref, halo_ref, other_ref, joined_ref, weight_ref, inner_ref, out_ref, x_ref, d_ref):
    _, own, _ = place()
    halos = [halo_ref[part].astype(f32) for part in range(2)]
    other_halos = [joined_ref[2 * Y * SHARES[0] + part].astype(f32) for part in range(2)]
    for t in range(BLOCKS):
        group, other = dates_at(group_ref, t, halos), dates_at(other_ref, t, other_halos, joined_ref)
        fields = [power(d) for d in other] + [cross(i, j) for i in group for j in other]
        put(x_ref, N_OUTER, t, [value for field in fields for value in field])

    first = lanes(1) < WINDOW
    mine = (first & (own == 0)) | (~first & (own == 1))

    def inner(field, a):
        return inner_ref[2 * field + a : 2 * field + a + 1, :]

    def inner_part(i, j, part, a):
        if i == j:
            return inner(i, a) if part == 0 else jnp.zeros((1, LANES), f32)
        field = Y + 2 * INNER.index((min(i, j), max(i, j))) + part
        return -inner(field, a) if part == 1 and i > j else inner(field, a)

    for field, a, row in looks_of(x_ref, weight_ref[...], d_ref, N_OUTER):
        if field < Y:
            at = 16 + 2 * field + a
            row = jnp.where(mine, inner(field, a), row)
            for i in range(Y):
                out_ref[i, at : at + 1, :] = row
        else:
            i, j = divmod((field - Y) // 2, Y)
            part = (field - Y) % 2
            at = 8 * part + 2 * j + a
            out_ref[i, at : at + 1, :] = jnp.where(mine, inner_part(i, j, part, a), row)


def normalise_kernel(parts_ref, out_ref):
    y, own, odd = place()
    rows = parts_ref.shape[1]
    lane = lanes(rows)
    first = lane < WINDOW
    end = jnp.where(odd, 0, LOOKS - 1)
    own_tile = jnp.where(odd, Y, 0)
    sides = []
    for side in range(2):

        def window(part, base):
            part = jnp.where(first == (side == 0), part, 0.0)
            return pltpu.roll(part, (base + 2 * LANES - side * WINDOW) % LANES, 1)

        summed = window(parts_ref[Y - own_tile + Y - 1], base_of(Y - 1, ~odd))
        summed = jnp.where(lane == end, summed, 0.0)
        for i in range(Y):
            base = base_of(i, odd)
            inside = (lane >= base) & (lane < base + WINDOW)
            summed = summed + jnp.where(inside, window(parts_ref[own_tile + i], base), 0.0)
        sides.append(summed)
    column_powers = [summed[16:24] for summed in sides]
    row_power = jnp.where(own == 0, *column_powers)
    row = lax.broadcasted_iota(jnp.int32, row_power.shape, 0)
    row_power = jnp.where(row // 2 == y, row_power, 0.0)
    row_power = row_power + pltpu.roll(row_power, 4, 0)
    row_power = row_power + pltpu.roll(row_power, 2, 0)
    for side in range(2):
        scale = lax.rsqrt((row_power + EPSILON) * (column_powers[side] + EPSILON))
        for k in range(2):
            values = sides[side][8 * k : 8 * k + 8] * scale
            for j in range(Y):
                out_ref[2 * j + side, k] = values[2 * j : 2 * j + 2]


def call(kernel, out_shape, operands, scratch=(), flops=0):
    return pl.pallas_call(
        kernel,
        out_shape=out_shape,
        in_specs=[VMEM] * len(operands),
        out_specs=jax.tree.map(lambda _: VMEM, out_shape),
        scratch_shapes=list(scratch),
        compiler_params=pltpu.CompilerParams(vmem_limit_bytes=VMEM_LIMIT),
        cost_estimate=pl.CostEstimate(flops=flops, bytes_accessed=1 << 20, transcendentals=0),
    )(*operands)


def looks(kernel, out_shape, operands, fields):
    rows, samples = 2 * fields * LINES, BLOCKS * LANES
    scratch = [pltpu.VMEM((rows, samples), bf16), pltpu.VMEM((rows, LANES), f32)]
    return call(kernel, out_shape, operands, scratch, flops=2 * rows * samples * LANES)


def local(stack):
    tiles = lax.axis_size("rng")
    axes = ("pair", "rng")

    def device(y, h, n):
        return (2 * y + h) * tiles + n

    def across(*ys):
        return [(device(y, h, n), device(y, 1 - h, n)) for y in ys for h in range(2) for n in range(tiles)]

    swap = []
    for h in range(2):
        for n in range(1, tiles - 1, 2):
            swap += [(device(0, h, n), device(0, h, n + 1)), (device(0, h, n + 1), device(0, h, n))]
    chips = [[device(y, h, n + c) for c in range(2) for y in range(Y)] for h in range(2) for n in range(0, tiles, 2)]

    chunks = call(cut_kernel, jax.ShapeDtypeStruct((Y, 2, BLOCKS, LINES, LANES), bf16), (stack,))
    group = lax.all_to_all(chunks, "pair", 0, 0, axis_index_groups=GROUPS)
    edge = call(edge_kernel, jax.ShapeDtypeStruct((2, LINES, LANES), bf16), (group,))
    group, edge = lax.optimization_barrier((group, edge))
    halo = lax.ppermute(edge, axes, swap)
    other = lax.ppermute(group, axes, across(1, 2, 3))
    joined = call(join_kernel, jax.ShapeDtypeStruct((2 * Y * SHARES[0] + 2, LINES, LANES), bf16), (group, halo))
    joined = lax.ppermute(joined, axes, across(0))

    shapes = (
        jax.ShapeDtypeStruct((2 * N_INNER, LANES), f32),
        jax.ShapeDtypeStruct((BLOCKS * LANES, LANES), bf16),
    )
    inner, weights = looks(inner_kernel, shapes, (group, halo), N_INNER)
    parts = looks(
        outer_kernel,
        jax.ShapeDtypeStruct((Y, 24, LANES), f32),
        (group, halo, other, joined, weights, inner),
        N_OUTER,
    )
    parts = lax.all_to_all(jnp.concatenate([parts, parts]), axes, 0, 0, axis_index_groups=chips)
    out = call(normalise_kernel, jax.ShapeDtypeStruct((2 * Y, 2, 2, LANES), f32), (parts,))
    return out[None]


def solution(mesh):
    in_specs = (P("pair", None, None, "rng"),)
    out_specs = P("pair", None, None, None, "rng")
    return jax.shard_map(local, mesh=mesh, in_specs=in_specs, out_specs=out_specs, check_vma=False)
```

time: 55 us -> 51.2 us (0.931)
  the two profiles are of different devices: /device:TPU:38 before, /device:TPU:7 now
where the time goes in v4:
time: 51.2 us; the launch traced here: 50.9 us
  blocking collectives  22.3 us (44%)
  starting transfers between devices  21.5 us (42%)
  waiting for transfers between devices  3.32 us (6%)
  Pallas kernels  2.78 us (5%)
  local copies, waits for them, and re-layouts  0.92 us (2%)
    ppermute x1, starting transfers between devices, local(): joined = lax.ppermute(joined, axes, across(0))  15.4 us
    all_to_all x1, blocking collectives, local(): lax.all_to_all(jnp.concatenate([parts, parts]), axes, 0, 0, axis_index_gr...  13.1 us
    all_to_all x1, blocking collectives, local(): group = lax.all_to_all(chunks, 'pair', 0, 0, axis_index_groups=GROUPS)  9.16 us
    ppermute x1, starting transfers between devices, local(): halo = lax.ppermute(edge, axes, swap)  5.45 us
    pallas_call x6, Pallas kernels, call(): pl.pallas_call(kernel, out_shape=out_shape, in_specs=[VMEM] * len(operand...  2.78 us
    ppermute x1, waiting for transfers between devices, local(): joined = lax.ppermute(joined, axes, across(0))  1.7 us
    ppermute x1, waiting for transfers between devices, local(): halo = lax.ppermute(edge, axes, swap)  1.62 us
  transfers between devices with their start and end apart: 3, of which 2 were waited for; matrix products, arithmetic and copies ran while one was open for 0% of the time, Pallas kernels for 2%

profile of v4, /device:TPU:7, one launch (start us, length us, event | category | flops | bytes accessed | tf_op | source)
XLA Modules:
  0.0 50.9 jit_solution(2232463910235438646)
XLA Ops:
  0.0 0.0 copy-start
  0.0 0.9 %copy-done = bf16[1,2,16,2560]{3,2,1,0:T(8,128)(2,1)S(1)} copy-done((bf16[1,2,16,2560]{3,2,1,0:T(8,128)(2,1)S(1)}, bf16[1,2,16,2560]{3,2,1,0:T(8,128)(2,1)}, u32[]{:S(2)}) %copy-start) | copy-done | bytes 163864
  1.0 9.2 %all_to_all.10.group_ref = bf16[4,2,6,16,128]{4,3,2,1,0:T(8,128)(2,1)S(1)} all-to-all(bf16[4,2,6,16,128]{4,3,2,1,0:T(8,128)(2,1)S(1)} %shard_map.17), channel_id=1, replica_groups={{0,128,256,384},{64,192,320,448},{1,129,257,385},{65,193,321,449},{2,13..., dimensions={0} | all-to-all | bytes 393216 | tf_op jit(solution)/shard_map/all_to_all | solution.py:296
  10.1 0.1 shard_map.18
  10.3 0.7 %collective-permute-start.1 = (bf16[4,2,6,16,128]{4,3,2,1,0:T(8,128)(2,1)S(1)}, bf16[4,2,6,16,128]{4,3,2,1,0:T(8,128)(2,1)S(1)}, u32[]{:S(2)}, u32[]{:S(2)}) collective-permute-start(bf16[4,2,6,16,128]{4,3,2,1,0:T(8,128)(2,1)S(1)} %all_to_all.10.group_ref), channel_id=1, source_target_pairs={{128,192},{129,193},{130,194},{131,195},{132,196},{133,197},{134,1... | collective-permute-start | bytes 589832 | tf_op jit(solution)/shard_map/ppermute | solution.py:300
  10.9 5.5 %collective-permute-start = (bf16[2,16,128]{2,1,0:T(8,128)(2,1)S(1)}, bf16[2,16,128]{2,1,0:T(8,128)(2,1)S(1)}, u32[]{:S(2)}, u32[]{:S(2)}) collective-permute-start(bf16[2,16,128]{2,1,0:T(8,128)(2,1)S(1)} %shard_map.18), channel_id=1, source_target_pairs={{1,2},{2,1},{3,4},{4,3},{5,6},{6,5},{7,8},{8,7},{9,10},{10,9},{11,... | collective-permute-start | bytes 24584 | tf_op jit(solution)/shard_map/ppermute | solution.py:299
  16.4 1.6 %collective-permute-done.halo_ref = bf16[2,16,128]{2,1,0:T(8,128)(2,1)S(1)} collective-permute-done((bf16[2,16,128]{2,1,0:T(8,128)(2,1)S(1)}, bf16[2,16,128]{2,1,0:T(8,128)(2,1)S(1)}, u32[]{:S(2)}, u32[]{:S(2)}) %collective-permute-start) | collective-permute-done | bytes 8224 | tf_op jit(solution)/shard_map/ppermute | solution.py:299
  18.0 15.4 %collective-permute-start.2 = (bf16[18,16,128]{2,1,0:T(8,128)(2,1)S(1)}, bf16[18,16,128]{2,1,0:T(8,128)(2,1)S(1)}, u32[]{:S(2)}, u32[]{:S(2)}) collective-permute-start(bf16[18,16,128]{2,1,0:T(8,128)(2,1)S(1)} %shard_map.19), channel_id=1, source_target_pairs={{0,64},{1,65},{2,66},{3,67},{4,68},{5,69},{6,70},{7,71},{8,72},{9,... | collective-permute-start | bytes 221192 | tf_op jit(solution)/shard_map/ppermute | solution.py:302
  33.5 0.9 %shard_map.20 = (f32[32,128]{1,0:T(8,128)S(1)}, bf16[768,128]{1,0:T(8,128)(2,1)S(1)}) custom-call(bf16[4,2,6,16,128]{4,3,2,1,0:T(8,128)(2,1)S(1)} %all_to_all.10.group_ref, bf16[2,16,128]{2,1,0:T(8,128)(2,1)S(1)} %collective-permute-done.halo_ref), custom_call_target="tpu_custom_call" | custom-call | flops 100663296 | bytes 1048576 | tf_op jit(solution)/shard_map/pallas_call | solution.py:262
  34.4 1.7 %collective-permute-done.2.joined_ref = bf16[18,16,128]{2,1,0:T(8,128)(2,1)S(1)} collective-permute-done((bf16[18,16,128]{2,1,0:T(8,128)(2,1)S(1)}, bf16[18,16,128]{2,1,0:T(8,128)(2,1)S(1)}, u32[]{:S(2)}, u32[]{:S(2)}) %collective-permute-start.2) | collective-permute-done | bytes 73760 | tf_op jit(solution)/shard_map/ppermute | solution.py:302
  36.1 0.0 collective-permute-done.1.other_ref
  36.1 0.9 %shard_map.21 = f32[4,24,128]{2,1,0:T(8,128)S(1)} custom-call(bf16[4,2,6,16,128]{4,3,2,1,0:T(8,128)(2,1)S(1)} %all_to_all.10.group_ref, bf16[2,16,128]{2,1,0:T(8,128)(2,1)S(1)} %collective-permute-done.halo_ref, bf16[4,2,6,16,128]{4,3,2,1,0:T(8,128)(2,1)S(1)} %collective-permute-done.1.other_ref, bf16[18,16,128]{2,1,0:T(8,128)(2,1)S(1)} %collective-permute-done.2.joined_ref, ...), custom_call_target="tpu_custom_call" | custom-call | flops 226492416 | bytes 1048576 | tf_op jit(solution)/shard_map/pallas_call | solution.py:262
  37.1 13.1 %all_to_all.11.parts_ref = f32[8,24,128]{2,1,0:T(8,128)S(1)} all-to-all(f32[8,24,128]{2,1,0:T(8,128)S(1)} %pad_maximum_fusion), channel_id=1, replica_groups={{0,128,256,384,1,129,257,385},{2,130,258,386,3,131,259,387},{4,132,260,..., dimensions={0} | all-to-all | bytes 196608 | tf_op jit(solution)/shard_map/all_to_all | solution.py:315
  50.2 0.7 %shard_map.22 = f32[8,2,2,128]{3,2,1,0:T(2,128)} custom-call(f32[8,24,128]{2,1,0:T(8,128)S(1)} %all_to_all.11.parts_ref), custom_call_target="tpu_custom_call" | custom-call | bytes 1048576 | tf_op jit(solution)/shard_map/pallas_call | solution.py:262
  (3 shorter events, 0.1 us)
Async XLA Ops:
  0.0 0.9 %copy-start = (bf16[1,2,16,2560]{3,2,1,0:T(8,128)(2,1)S(1)}, bf16[1,2,16,2560]{3,2,1,0:T(8,128)(2,1)}, u32[]{:S(2)}) copy-start(bf16[1,2,16,2560]{3,2,1,0:T(8,128)(2,1)} %stack_ref.1) | copy-start | bytes 491524
  10.3 25.8 %collective-permute-start.1 = (bf16[4,2,6,16,128]{4,3,2,1,0:T(8,128)(2,1)S(1)}, bf16[4,2,6,16,128]{4,3,2,1,0:T(8,128)(2,1)S(1)}, u32[]{:S(2)}, u32[]{:S(2)}) collective-permute-start(bf16[4,2,6,16,128]{4,3,2,1,0:T(8,128)(2,1)S(1)} %all_to_all.10.group_ref), channel_id=1, source_target_pairs={{128,192},{129,193},{130,194},{131,195},{132,196},{133,197},{134,1... | collective-permute-start | bytes 589832 | tf_op jit(solution)/shard_map/ppermute | solution.py:300
  10.9 7.1 %collective-permute-start = (bf16[2,16,128]{2,1,0:T(8,128)(2,1)S(1)}, bf16[2,16,128]{2,1,0:T(8,128)(2,1)S(1)}, u32[]{:S(2)}, u32[]{:S(2)}) collective-permute-start(bf16[2,16,128]{2,1,0:T(8,128)(2,1)S(1)} %shard_map.18), channel_id=1, source_target_pairs={{1,2},{2,1},{3,4},{4,3},{5,6},{6,5},{7,8},{8,7},{9,10},{10,9},{11,... | collective-permute-start | bytes 24584 | tf_op jit(solution)/shard_map/ppermute | solution.py:299
  18.0 18.1 %collective-permute-start.2 = (bf16[18,16,128]{2,1,0:T(8,128)(2,1)S(1)}, bf16[18,16,128]{2,1,0:T(8,128)(2,1)S(1)}, u32[]{:S(2)}, u32[]{:S(2)}) collective-permute-start(bf16[18,16,128]{2,1,0:T(8,128)(2,1)S(1)} %shard_map.19), channel_id=1, source_target_pairs={{0,64},{1,65},{2,66},{3,67},{4,68},{5,69},{6,70},{7,71},{8,72},{9,... | collective-permute-start | bytes 221192 | tf_op jit(solution)/shard_map/ppermute | solution.py:302

commit v5 on v4

--- a/solution.py
+++ b/solution.py
@@ -295,7 +295,6 @@
     chunks = call(cut_kernel, jax.ShapeDtypeStruct((Y, 2, BLOCKS, LINES, LANES), bf16), (stack,))
     group = lax.all_to_all(chunks, "pair", 0, 0, axis_index_groups=GROUPS)
     edge = call(edge_kernel, jax.ShapeDtypeStruct((2, LINES, LANES), bf16), (group,))
-    group, edge = lax.optimization_barrier((group, edge))
     halo = lax.ppermute(edge, axes, swap)
     other = lax.ppermute(group, axes, across(1, 2, 3))
     joined = call(join_kernel, jax.ShapeDtypeStruct((2 * Y * SHARES[0] + 2, LINES, LANES), bf16), (group, halo))

time: 51.2 us -> 51 us (level)
  no operation moved by 1% of the time
where the time goes in v5:
time: 51 us; the launch traced here: 50.8 us
  blocking collectives  22.2 us (44%)
  starting transfers between devices  21.5 us (42%)
  waiting for transfers between devices  3.32 us (7%)
  Pallas kernels  2.78 us (5%)
  local copies, waits for them, and re-layouts  0.92 us (2%)
    ppermute x1, starting transfers between devices, local(): joined = lax.ppermute(joined, axes, across(0))  15.4 us
    all_to_all x1, blocking collectives, local(): lax.all_to_all(jnp.concatenate([parts, parts]), axes, 0, 0, axis_index_gr...  13 us
    all_to_all x1, blocking collectives, local(): group = lax.all_to_all(chunks, 'pair', 0, 0, axis_index_groups=GROUPS)  9.16 us
    ppermute x1, starting transfers between devices, local(): halo = lax.ppermute(edge, axes, swap)  5.44 us
    pallas_call x6, Pallas kernels, call(): pl.pallas_call(kernel, out_shape=out_shape, in_specs=[VMEM] * len(operand...  2.78 us
    ppermute x1, waiting for transfers between devices, local(): joined = lax.ppermute(joined, axes, across(0))  1.7 us
    ppermute x1, waiting for transfers between devices, local(): halo = lax.ppermute(edge, axes, swap)  1.62 us
  transfers between devices with their start and end apart: 3, of which 2 were waited for; matrix products, arithmetic and copies ran while one was open for 0% of the time, Pallas kernels for 2%

profile of v5, /device:TPU:7, one launch (start us, length us, event | category | flops | bytes accessed | tf_op | source)
XLA Modules:
  0.0 50.8 jit_solution(16348866923614807743)
XLA Ops:
  0.0 0.0 copy-start
  0.0 0.9 %copy-done = bf16[1,2,16,2560]{3,2,1,0:T(8,128)(2,1)S(1)} copy-done((bf16[1,2,16,2560]{3,2,1,0:T(8,128)(2,1)S(1)}, bf16[1,2,16,2560]{3,2,1,0:T(8,128)(2,1)}, u32[]{:S(2)}) %copy-start) | copy-done | bytes 163864
  1.0 9.2 %all_to_all.10.group_ref = bf16[4,2,6,16,128]{4,3,2,1,0:T(8,128)(2,1)S(1)} all-to-all(bf16[4,2,6,16,128]{4,3,2,1,0:T(8,128)(2,1)S(1)} %shard_map.17), channel_id=1, replica_groups={{0,128,256,384},{64,192,320,448},{1,129,257,385},{65,193,321,449},{2,13..., dimensions={0} | all-to-all | bytes 393216 | tf_op jit(solution)/shard_map/all_to_all | solution.py:296
  10.1 0.7 %collective-permute-start.1 = (bf16[4,2,6,16,128]{4,3,2,1,0:T(8,128)(2,1)S(1)}, bf16[4,2,6,16,128]{4,3,2,1,0:T(8,128)(2,1)S(1)}, u32[]{:S(2)}, u32[]{:S(2)}) collective-permute-start(bf16[4,2,6,16,128]{4,3,2,1,0:T(8,128)(2,1)S(1)} %all_to_all.10.group_ref), channel_id=1, source_target_pairs={{128,192},{129,193},{130,194},{131,195},{132,196},{133,197},{134,1... | collective-permute-start | bytes 589832 | tf_op jit(solution)/shard_map/ppermute | solution.py:299
  10.8 0.2 shard_map.18
  10.9 5.4 %collective-permute-start = (bf16[2,16,128]{2,1,0:T(8,128)(2,1)S(1)}, bf16[2,16,128]{2,1,0:T(8,128)(2,1)S(1)}, u32[]{:S(2)}, u32[]{:S(2)}) collective-permute-start(bf16[2,16,128]{2,1,0:T(8,128)(2,1)S(1)} %shard_map.18), channel_id=1, source_target_pairs={{1,2},{2,1},{3,4},{4,3},{5,6},{6,5},{7,8},{8,7},{9,10},{10,9},{11,... | collective-permute-start | bytes 24584 | tf_op jit(solution)/shard_map/ppermute | solution.py:298
  16.4 1.6 %collective-permute-done.halo_ref = bf16[2,16,128]{2,1,0:T(8,128)(2,1)S(1)} collective-permute-done((bf16[2,16,128]{2,1,0:T(8,128)(2,1)S(1)}, bf16[2,16,128]{2,1,0:T(8,128)(2,1)S(1)}, u32[]{:S(2)}, u32[]{:S(2)}) %collective-permute-start) | collective-permute-done | bytes 8224 | tf_op jit(solution)/shard_map/ppermute | solution.py:298
  18.0 15.4 %collective-permute-start.2 = (bf16[18,16,128]{2,1,0:T(8,128)(2,1)S(1)}, bf16[18,16,128]{2,1,0:T(8,128)(2,1)S(1)}, u32[]{:S(2)}, u32[]{:S(2)}) collective-permute-start(bf16[18,16,128]{2,1,0:T(8,128)(2,1)S(1)} %shard_map.19), channel_id=1, source_target_pairs={{0,64},{1,65},{2,66},{3,67},{4,68},{5,69},{6,70},{7,71},{8,72},{9,... | collective-permute-start | bytes 221192 | tf_op jit(solution)/shard_map/ppermute | solution.py:301
  33.5 0.9 %shard_map.20 = (f32[32,128]{1,0:T(8,128)S(1)}, bf16[768,128]{1,0:T(8,128)(2,1)S(1)}) custom-call(bf16[4,2,6,16,128]{4,3,2,1,0:T(8,128)(2,1)S(1)} %all_to_all.10.group_ref, bf16[2,16,128]{2,1,0:T(8,128)(2,1)S(1)} %collective-permute-done.halo_ref), custom_call_target="tpu_custom_call" | custom-call | flops 100663296 | bytes 1048576 | tf_op jit(solution)/shard_map/pallas_call | solution.py:262
  34.4 1.7 %collective-permute-done.2.joined_ref = bf16[18,16,128]{2,1,0:T(8,128)(2,1)S(1)} collective-permute-done((bf16[18,16,128]{2,1,0:T(8,128)(2,1)S(1)}, bf16[18,16,128]{2,1,0:T(8,128)(2,1)S(1)}, u32[]{:S(2)}, u32[]{:S(2)}) %collective-permute-start.2) | collective-permute-done | bytes 73760 | tf_op jit(solution)/shard_map/ppermute | solution.py:301
  36.1 0.0 collective-permute-done.1.other_ref
  36.1 0.9 %shard_map.21 = f32[4,24,128]{2,1,0:T(8,128)S(1)} custom-call(bf16[4,2,6,16,128]{4,3,2,1,0:T(8,128)(2,1)S(1)} %all_to_all.10.group_ref, bf16[2,16,128]{2,1,0:T(8,128)(2,1)S(1)} %collective-permute-done.halo_ref, bf16[4,2,6,16,128]{4,3,2,1,0:T(8,128)(2,1)S(1)} %collective-permute-done.1.other_ref, bf16[18,16,128]{2,1,0:T(8,128)(2,1)S(1)} %collective-permute-done.2.joined_ref, ...), custom_call_target="tpu_custom_call" | custom-call | flops 226492416 | bytes 1048576 | tf_op jit(solution)/shard_map/pallas_call | solution.py:262
  37.1 13.0 %all_to_all.11.parts_ref = f32[8,24,128]{2,1,0:T(8,128)S(1)} all-to-all(f32[8,24,128]{2,1,0:T(8,128)S(1)} %pad_maximum_fusion), channel_id=1, replica_groups={{0,128,256,384,1,129,257,385},{2,130,258,386,3,131,259,387},{4,132,260,..., dimensions={0} | all-to-all | bytes 196608 | tf_op jit(solution)/shard_map/all_to_all | solution.py:314
  50.1 0.7 %shard_map.22 = f32[8,2,2,128]{3,2,1,0:T(2,128)} custom-call(f32[8,24,128]{2,1,0:T(8,128)S(1)} %all_to_all.11.parts_ref), custom_call_target="tpu_custom_call" | custom-call | bytes 1048576 | tf_op jit(solution)/shard_map/pallas_call | solution.py:262
  (3 shorter events, 0.1 us)
Async XLA Ops:
  0.0 0.9 %copy-start = (bf16[1,2,16,2560]{3,2,1,0:T(8,128)(2,1)S(1)}, bf16[1,2,16,2560]{3,2,1,0:T(8,128)(2,1)}, u32[]{:S(2)}) copy-start(bf16[1,2,16,2560]{3,2,1,0:T(8,128)(2,1)} %stack_ref.1) | copy-start | bytes 491524
  10.1 26.0 %collective-permute-start.1 = (bf16[4,2,6,16,128]{4,3,2,1,0:T(8,128)(2,1)S(1)}, bf16[4,2,6,16,128]{4,3,2,1,0:T(8,128)(2,1)S(1)}, u32[]{:S(2)}, u32[]{:S(2)}) collective-permute-start(bf16[4,2,6,16,128]{4,3,2,1,0:T(8,128)(2,1)S(1)} %all_to_all.10.group_ref), channel_id=1, source_target_pairs={{128,192},{129,193},{130,194},{131,195},{132,196},{133,197},{134,1... | collective-permute-start | bytes 589832 | tf_op jit(solution)/shard_map/ppermute | solution.py:299
  10.9 7.1 %collective-permute-start = (bf16[2,16,128]{2,1,0:T(8,128)(2,1)S(1)}, bf16[2,16,128]{2,1,0:T(8,128)(2,1)S(1)}, u32[]{:S(2)}, u32[]{:S(2)}) collective-permute-start(bf16[2,16,128]{2,1,0:T(8,128)(2,1)S(1)} %shard_map.18), channel_id=1, source_target_pairs={{1,2},{2,1},{3,4},{4,3},{5,6},{6,5},{7,8},{8,7},{9,10},{10,9},{11,... | collective-permute-start | bytes 24584 | tf_op jit(solution)/shard_map/ppermute | solution.py:298
  18.0 18.1 %collective-permute-start.2 = (bf16[18,16,128]{2,1,0:T(8,128)(2,1)S(1)}, bf16[18,16,128]{2,1,0:T(8,128)(2,1)S(1)}, u32[]{:S(2)}, u32[]{:S(2)}) collective-permute-start(bf16[18,16,128]{2,1,0:T(8,128)(2,1)S(1)} %shard_map.19), channel_id=1, source_target_pairs={{0,64},{1,65},{2,66},{3,67},{4,68},{5,69},{6,70},{7,71},{8,72},{9,... | collective-permute-start | bytes 221192 | tf_op jit(solution)/shard_map/ppermute | solution.py:301

commit v6 on v5

--- a/solution.py
+++ b/solution.py
@@ -129,9 +129,9 @@
     return jnp.where(lanes(LINES) < RG_STEP, rolled, 0.0)
 
 
-def dates_at(ref, t, halos, joined_ref=None):
+def dates_at(refs, t, halos, joined_ref=None):
     def one(i, part):
-        value = ref[i, part, t].astype(f32)
+        value = sum(ref[i, part, t].astype(f32) for ref in refs)
         if joined_ref is not None and t < SHARES[0]:
             value = value + joined_ref[(2 * i + part) * SHARES[0] + t].astype(f32)
         if t == BLOCKS - 1:
@@ -182,19 +182,19 @@
     weight_ref[...] = jnp.where(column < WINDOW, high.astype(f32), low.astype(f32)).astype(bf16)
     halos = [halo_ref[part].astype(f32) for part in range(2)]
     for t in range(BLOCKS):
-        group = dates_at(group_ref, t, halos)
+        group = dates_at([group_ref], t, halos)
         fields = [power(d) for d in group] + [cross(group[i], group[j]) for i, j in INNER]
         put(x_ref, N_INNER, t, [value for field in fields for value in field])
     for field, a, row in looks_of(x_ref, weight_ref[...], d_ref, N_INNER):
         out_ref[2 * field + a : 2 * field + a + 1, :] = row
 
 
-def outer_kernel(group_ref, halo_ref, other_ref, joined_ref, weight_ref, inner_ref, out_ref, x_ref, d_ref):
+def outer_kernel(group_ref, halo_ref, even_ref, odd_ref, joined_ref, weight_ref, inner_ref, out_ref, x_ref, d_ref):
     _, own, _ = place()
     halos = [halo_ref[part].astype(f32) for part in range(2)]
     other_halos = [joined_ref[2 * Y * SHARES[0] + part].astype(f32) for part in range(2)]
     for t in range(BLOCKS):
-        group, other = dates_at(group_ref, t, halos), dates_at(other_ref, t, other_halos, joined_ref)
+        group, other = dates_at([group_ref], t, halos), dates_at([even_ref, odd_ref], t, other_halos, joined_ref)
         fields = [power(d) for d in other] + [cross(i, j) for i in group for j in other]
         put(x_ref, N_OUTER, t, [value for field in fields for value in field])
 
@@ -283,8 +283,9 @@
     def device(y, h, n):
         return (2 * y + h) * tiles + n
 
-    def across(*ys):
-        return [(device(y, h, n), device(y, 1 - h, n)) for y in ys for h in range(2) for n in range(tiles)]
+    def across(ys, cores=(0, 1)):
+        pairs = [(y, h, n) for y in ys for h in range(2) for n in range(tiles) if n % 2 in cores]
+        return [(device(y, h, n), device(y, 1 - h, n)) for y, h, n in pairs]
 
     swap = []
     for h in range(2):
@@ -296,9 +297,9 @@
     group = lax.all_to_all(chunks, "pair", 0, 0, axis_index_groups=GROUPS)
     edge = call(edge_kernel, jax.ShapeDtypeStruct((2, LINES, LANES), bf16), (group,))
     halo = lax.ppermute(edge, axes, swap)
-    other = lax.ppermute(group, axes, across(1, 2, 3))
+    others = [lax.ppermute(group, axes, across((1, 2, 3), (core,))) for core in range(2)]
     joined = call(join_kernel, jax.ShapeDtypeStruct((2 * Y * SHARES[0] + 2, LINES, LANES), bf16), (group, halo))
-    joined = lax.ppermute(joined, axes, across(0))
+    joined = lax.ppermute(joined, axes, across((0,)))
 
     shapes = (
         jax.ShapeDtypeStruct((2 * N_INNER, LANES), f32),
@@ -308,7 +309,7 @@
     parts = looks(
         outer_kernel,
         jax.ShapeDtypeStruct((Y, 24, LANES), f32),
-        (group, halo, other, joined, weights, inner),
+        (group, halo, *others, joined, weights, inner),
         N_OUTER,
     )
     parts = lax.all_to_all(jnp.concatenate([parts, parts]), axes, 0, 0, axis_index_groups=chips)

time: 51 us -> 50 us (0.980)
  the two profiles are of different devices: /device:TPU:7 before, /device:TPU:449 now
where the time goes in v6:
time: 50 us; the launch traced here: 49.7 us
  blocking collectives  25.3 us (51%)
  starting transfers between devices  11.6 us (23%)
  waiting for transfers between devices  9.03 us (18%)
  Pallas kernels  2.8 us (6%)
  local copies, waits for them, and re-layouts  0.92 us (2%)
    all_to_all x1, blocking collectives, local(): lax.all_to_all(jnp.concatenate([parts, parts]), axes, 0, 0, axis_index_gr...  16.2 us
    all_to_all x1, blocking collectives, local(): group = lax.all_to_all(chunks, 'pair', 0, 0, axis_index_groups=GROUPS)  9.16 us
    ppermute x1, waiting for transfers between devices, local(): joined = lax.ppermute(joined, axes, across((0,)))  7.71 us
    ppermute x1, starting transfers between devices, local(): joined = lax.ppermute(joined, axes, across((0,)))  5.15 us
    ppermute x1, starting transfers between devices, local(): halo = lax.ppermute(edge, axes, swap)  5.1 us
    pallas_call x6, Pallas kernels, call(): pl.pallas_call(kernel, out_shape=out_shape, in_specs=[VMEM] * len(operand...  2.8 us
    ppermute x2, starting transfers between devices, local(): lax.ppermute(group, axes, across((1, 2, 3), (core,)))  1.33 us
    ppermute x1, waiting for transfers between devices, local(): halo = lax.ppermute(edge, axes, swap)  1.32 us
  transfers between devices with their start and end apart: 4, of which 2 were waited for; matrix products, arithmetic and copies ran while one was open for 0% of the time, Pallas kernels for 2%

profile of v6, /device:TPU:449, one launch (start us, length us, event | category | flops | bytes accessed | tf_op | source)
XLA Modules:
  0.0 49.7 jit_solution(3176665293462243249)
XLA Ops:
  0.0 0.0 copy-start
  0.0 0.9 %copy-done = bf16[1,2,16,2560]{3,2,1,0:T(8,128)(2,1)S(1)} copy-done((bf16[1,2,16,2560]{3,2,1,0:T(8,128)(2,1)S(1)}, bf16[1,2,16,2560]{3,2,1,0:T(8,128)(2,1)}, u32[]{:S(2)}) %copy-start) | copy-done | bytes 163864
  1.0 9.2 %all_to_all.10.group_ref = bf16[4,2,6,16,128]{4,3,2,1,0:T(8,128)(2,1)S(1)} all-to-all(bf16[4,2,6,16,128]{4,3,2,1,0:T(8,128)(2,1)S(1)} %shard_map.17), channel_id=1, replica_groups={{0,128,256,384},{64,192,320,448},{1,129,257,385},{65,193,321,449},{2,13..., dimensions={0} | all-to-all | bytes 393216 | tf_op jit(solution)/shard_map/all_to_all | solution.py:297
  10.1 0.7 %collective-permute-start.2 = (bf16[4,2,6,16,128]{4,3,2,1,0:T(8,128)(2,1)S(1)}, bf16[4,2,6,16,128]{4,3,2,1,0:T(8,128)(2,1)S(1)}, u32[]{:S(2)}, u32[]{:S(2)}) collective-permute-start(bf16[4,2,6,16,128]{4,3,2,1,0:T(8,128)(2,1)S(1)} %all_to_all.10.group_ref), channel_id=1, source_target_pairs={{129,193},{131,195},{133,197},{135,199},{137,201},{139,203},{141,2... | collective-permute-start | bytes 589832 | tf_op jit(solution)/shard_map/ppermute | solution.py:300
  10.8 0.7 %collective-permute-start.1 = (bf16[4,2,6,16,128]{4,3,2,1,0:T(8,128)(2,1)S(1)}, bf16[4,2,6,16,128]{4,3,2,1,0:T(8,128)(2,1)S(1)}, u32[]{:S(2)}, u32[]{:S(2)}) collective-permute-start(bf16[4,2,6,16,128]{4,3,2,1,0:T(8,128)(2,1)S(1)} %all_to_all.10.group_ref), channel_id=1, source_target_pairs={{128,192},{130,194},{132,196},{134,198},{136,200},{138,202},{140,2... | collective-permute-start | bytes 589832 | tf_op jit(solution)/shard_map/ppermute | solution.py:300
  11.5 0.2 shard_map.18
  11.6 5.1 %collective-permute-start = (bf16[2,16,128]{2,1,0:T(8,128)(2,1)S(1)}, bf16[2,16,128]{2,1,0:T(8,128)(2,1)S(1)}, u32[]{:S(2)}, u32[]{:S(2)}) collective-permute-start(bf16[2,16,128]{2,1,0:T(8,128)(2,1)S(1)} %shard_map.18), channel_id=1, source_target_pairs={{1,2},{2,1},{3,4},{4,3},{5,6},{6,5},{7,8},{8,7},{9,10},{10,9},{11,... | collective-permute-start | bytes 24584 | tf_op jit(solution)/shard_map/ppermute | solution.py:299
  16.7 1.3 %collective-permute-done.halo_ref = bf16[2,16,128]{2,1,0:T(8,128)(2,1)S(1)} collective-permute-done((bf16[2,16,128]{2,1,0:T(8,128)(2,1)S(1)}, bf16[2,16,128]{2,1,0:T(8,128)(2,1)S(1)}, u32[]{:S(2)}, u32[]{:S(2)}) %collective-permute-start) | collective-permute-done | bytes 8224 | tf_op jit(solution)/shard_map/ppermute | solution.py:299
  18.1 5.1 %collective-permute-start.3 = (bf16[18,16,128]{2,1,0:T(8,128)(2,1)S(1)}, bf16[18,16,128]{2,1,0:T(8,128)(2,1)S(1)}, u32[]{:S(2)}, u32[]{:S(2)}) collective-permute-start(bf16[18,16,128]{2,1,0:T(8,128)(2,1)S(1)} %shard_map.19), channel_id=1, source_target_pairs={{0,64},{1,65},{2,66},{3,67},{4,68},{5,69},{6,70},{7,71},{8,72},{9,... | collective-permute-start | bytes 221192 | tf_op jit(solution)/shard_map/ppermute | solution.py:302
  23.2 0.9 %shard_map.20 = (f32[32,128]{1,0:T(8,128)S(1)}, bf16[768,128]{1,0:T(8,128)(2,1)S(1)}) custom-call(bf16[4,2,6,16,128]{4,3,2,1,0:T(8,128)(2,1)S(1)} %all_to_all.10.group_ref, bf16[2,16,128]{2,1,0:T(8,128)(2,1)S(1)} %collective-permute-done.halo_ref), custom_call_target="tpu_custom_call" | custom-call | flops 100663296 | bytes 1048576 | tf_op jit(solution)/shard_map/pallas_call | solution.py:262
  24.2 7.7 %collective-permute-done.3.joined_ref = bf16[18,16,128]{2,1,0:T(8,128)(2,1)S(1)} collective-permute-done((bf16[18,16,128]{2,1,0:T(8,128)(2,1)S(1)}, bf16[18,16,128]{2,1,0:T(8,128)(2,1)S(1)}, u32[]{:S(2)}, u32[]{:S(2)}) %collective-permute-start.3) | collective-permute-done | bytes 73760 | tf_op jit(solution)/shard_map/ppermute | solution.py:302
  31.9 0.0 collective-permute-done.2.odd_ref
  31.9 0.0 collective-permute-done.1.even_ref
  31.9 0.9 %shard_map.21 = f32[4,24,128]{2,1,0:T(8,128)S(1)} custom-call(bf16[4,2,6,16,128]{4,3,2,1,0:T(8,128)(2,1)S(1)} %all_to_all.10.group_ref, bf16[2,16,128]{2,1,0:T(8,128)(2,1)S(1)} %collective-permute-done.halo_ref, bf16[4,2,6,16,128]{4,3,2,1,0:T(8,128)(2,1)S(1)} %collective-permute-done.1.even_ref, ...), custom_call_target="tpu_custom_call" | custom-call | flops 226492416 | bytes 1048576 | tf_op jit(solution)/shard_map/pallas_call | solution.py:262
  32.8 16.2 %all_to_all.11.parts_ref = f32[8,24,128]{2,1,0:T(8,128)S(1)} all-to-all(f32[8,24,128]{2,1,0:T(8,128)S(1)} %pad_maximum_fusion), channel_id=1, replica_groups={{0,128,256,384,1,129,257,385},{2,130,258,386,3,131,259,387},{4,132,260,..., dimensions={0} | all-to-all | bytes 196608 | tf_op jit(solution)/shard_map/all_to_all | solution.py:315
  49.0 0.7 %shard_map.22 = f32[8,2,2,128]{3,2,1,0:T(2,128)} custom-call(f32[8,24,128]{2,1,0:T(8,128)S(1)} %all_to_all.11.parts_ref), custom_call_target="tpu_custom_call" | custom-call | bytes 1048576 | tf_op jit(solution)/shard_map/pallas_call | solution.py:262
  (3 shorter events, 0.1 us)
Async XLA Ops:
  0.0 0.9 %copy-start = (bf16[1,2,16,2560]{3,2,1,0:T(8,128)(2,1)S(1)}, bf16[1,2,16,2560]{3,2,1,0:T(8,128)(2,1)}, u32[]{:S(2)}) copy-start(bf16[1,2,16,2560]{3,2,1,0:T(8,128)(2,1)} %stack_ref.1) | copy-start | bytes 491524
  10.1 21.7 %collective-permute-start.2 = (bf16[4,2,6,16,128]{4,3,2,1,0:T(8,128)(2,1)S(1)}, bf16[4,2,6,16,128]{4,3,2,1,0:T(8,128)(2,1)S(1)}, u32[]{:S(2)}, u32[]{:S(2)}) collective-permute-start(bf16[4,2,6,16,128]{4,3,2,1,0:T(8,128)(2,1)S(1)} %all_to_all.10.group_ref), channel_id=1, source_target_pairs={{129,193},{131,195},{133,197},{135,199},{137,201},{139,203},{141,2... | collective-permute-start | bytes 589832 | tf_op jit(solution)/shard_map/ppermute | solution.py:300
  10.8 21.1 %collective-permute-start.1 = (bf16[4,2,6,16,128]{4,3,2,1,0:T(8,128)(2,1)S(1)}, bf16[4,2,6,16,128]{4,3,2,1,0:T(8,128)(2,1)S(1)}, u32[]{:S(2)}, u32[]{:S(2)}) collective-permute-start(bf16[4,2,6,16,128]{4,3,2,1,0:T(8,128)(2,1)S(1)} %all_to_all.10.group_ref), channel_id=1, source_target_pairs={{128,192},{130,194},{132,196},{134,198},{136,200},{138,202},{140,2... | collective-permute-start | bytes 589832 | tf_op jit(solution)/shard_map/ppermute | solution.py:300
  11.6 6.4 %collective-permute-start = (bf16[2,16,128]{2,1,0:T(8,128)(2,1)S(1)}, bf16[2,16,128]{2,1,0:T(8,128)(2,1)S(1)}, u32[]{:S(2)}, u32[]{:S(2)}) collective-permute-start(bf16[2,16,128]{2,1,0:T(8,128)(2,1)S(1)} %shard_map.18), channel_id=1, source_target_pairs={{1,2},{2,1},{3,4},{4,3},{5,6},{6,5},{7,8},{8,7},{9,10},{10,9},{11,... | collective-permute-start | bytes 24584 | tf_op jit(solution)/shard_map/ppermute | solution.py:299
  18.1 13.8 %collective-permute-start.3 = (bf16[18,16,128]{2,1,0:T(8,128)(2,1)S(1)}, bf16[18,16,128]{2,1,0:T(8,128)(2,1)S(1)}, u32[]{:S(2)}, u32[]{:S(2)}) collective-permute-start(bf16[18,16,128]{2,1,0:T(8,128)(2,1)S(1)} %shard_map.19), channel_id=1, source_target_pairs={{0,64},{1,65},{2,66},{3,67},{4,68},{5,69},{6,70},{7,71},{8,72},{9,... | collective-permute-start | bytes 221192 | tf_op jit(solution)/shard_map/ppermute | solution.py:302

commit v7 on v6

--- a/solution.py
+++ b/solution.py
@@ -129,11 +129,11 @@
     return jnp.where(lanes(LINES) < RG_STEP, rolled, 0.0)
 
 
-def dates_at(refs, t, halos, joined_ref=None):
+def dates_at(refs, t, halos, joined_refs=()):
     def one(i, part):
         value = sum(ref[i, part, t].astype(f32) for ref in refs)
-        if joined_ref is not None and t < SHARES[0]:
-            value = value + joined_ref[(2 * i + part) * SHARES[0] + t].astype(f32)
+        if t < SHARES[0]:
+            value = value + sum(ref[(2 * i + part) * SHARES[0] + t].astype(f32) for ref in joined_refs)
         if t == BLOCKS - 1:
             value = value + unpack(halos[part], i)
         return value
@@ -189,12 +189,13 @@
         out_ref[2 * field + a : 2 * field + a + 1, :] = row
 
 
-def outer_kernel(group_ref, halo_ref, even_ref, odd_ref, joined_ref, weight_ref, inner_ref, out_ref, x_ref, d_ref):
+def outer_kernel(group_ref, halo_ref, even_ref, odd_ref, *refs):
+    *joined_refs, weight_ref, inner_ref, out_ref, x_ref, d_ref = refs
     _, own, _ = place()
     halos = [halo_ref[part].astype(f32) for part in range(2)]
-    other_halos = [joined_ref[2 * Y * SHARES[0] + part].astype(f32) for part in range(2)]
+    other_halos = [sum(ref[2 * Y * SHARES[0] + part].astype(f32) for ref in joined_refs) for part in range(2)]
     for t in range(BLOCKS):
-        group, other = dates_at([group_ref], t, halos), dates_at([even_ref, odd_ref], t, other_halos, joined_ref)
+        group, other = dates_at([group_ref], t, halos), dates_at([even_ref, odd_ref], t, other_halos, joined_refs)
         fields = [power(d) for d in other] + [cross(i, j) for i in group for j in other]
         put(x_ref, N_OUTER, t, [value for field in fields for value in field])
 
@@ -227,14 +228,12 @@
     y, own, odd = place()
     rows = parts_ref.shape[1]
     lane = lanes(rows)
-    first = lane < WINDOW
     end = jnp.where(odd, 0, LOOKS - 1)
     own_tile = jnp.where(odd, Y, 0)
     sides = []
     for side in range(2):
 
         def window(part, base):
-            part = jnp.where(first == (side == 0), part, 0.0)
             return pltpu.roll(part, (base + 2 * LANES - side * WINDOW) % LANES, 1)
 
         summed = window(parts_ref[Y - own_tile + Y - 1], base_of(Y - 1, ~odd))
@@ -299,7 +298,7 @@
     halo = lax.ppermute(edge, axes, swap)
     others = [lax.ppermute(group, axes, across((1, 2, 3), (core,))) for core in range(2)]
     joined = call(join_kernel, jax.ShapeDtypeStruct((2 * Y * SHARES[0] + 2, LINES, LANES), bf16), (group, halo))
-    joined = lax.ppermute(joined, axes, across((0,)))
+    joineds = [lax.ppermute(joined, axes, across((0,), (core,))) for core in range(2)]
 
     shapes = (
         jax.ShapeDtypeStruct((2 * N_INNER, LANES), f32),
@@ -309,7 +308,7 @@
     parts = looks(
         outer_kernel,
         jax.ShapeDtypeStruct((Y, 24, LANES), f32),
-        (group, halo, *others, joined, weights, inner),
+        (group, halo, *others, *joineds, weights, inner),
         N_OUTER,
     )
     parts = lax.all_to_all(jnp.concatenate([parts, parts]), axes, 0, 0, axis_index_groups=chips)

time: 50 us -> 50 us (level)
  waiting for transfers between devices: 9.03 us -> 8.35 us
  starting transfers between devices: 11.6 us -> 12.2 us
    ppermute x1 -> x2, waiting for transfers between devices: 7.71 us -> 7.03 us  [local(): lax.ppermute(joined, axes, across((0,), (core,)))]
    ppermute x1 -> x2, starting transfers between devices: 5.15 us -> 5.81 us  [local(): lax.ppermute(joined, axes, across((0,), (core,)))]
  transfers between devices with their start and end apart: 4 -> 5, of which waited for: 2 -> 2; matrix products, arithmetic and copies ran while one was open for 0% -> 0% of each run, Pallas kernels for 2% -> 2%
where the time goes in v7:
time: 50 us; the launch traced here: 49.7 us
  blocking collectives  25.3 us (51%)
  starting transfers between devices  12.2 us (24%)
  waiting for transfers between devices  8.35 us (17%)
  Pallas kernels  2.81 us (6%)
  local copies, waits for them, and re-layouts  0.92 us (2%)
    all_to_all x1, blocking collectives, local(): lax.all_to_all(jnp.concatenate([parts, parts]), axes, 0, 0, axis_index_gr...  16.2 us
    all_to_all x1, blocking collectives, local(): group = lax.all_to_all(chunks, 'pair', 0, 0, axis_index_groups=GROUPS)  9.16 us
    ppermute x2, waiting for transfers between devices, local(): lax.ppermute(joined, axes, across((0,), (core,)))  7.03 us
    ppermute x2, starting transfers between devices, local(): lax.ppermute(joined, axes, across((0,), (core,)))  5.81 us
    ppermute x1, starting transfers between devices, local(): halo = lax.ppermute(edge, axes, swap)  5.1 us
    pallas_call x6, Pallas kernels, call(): pl.pallas_call(kernel, out_shape=out_shape, in_specs=[VMEM] * len(operand...  2.81 us
    ppermute x2, starting transfers between devices, local(): lax.ppermute(group, axes, across((1, 2, 3), (core,)))  1.33 us
    ppermute x1, waiting for transfers between devices, local(): halo = lax.ppermute(edge, axes, swap)  1.32 us
  transfers between devices with their start and end apart: 5, of which 2 were waited for; matrix products, arithmetic and copies ran while one was open for 0% of the time, Pallas kernels for 2%

profile of v7, /device:TPU:449, one launch (start us, length us, event | category | flops | bytes accessed | tf_op | source)
XLA Modules:
  0.0 49.7 jit_solution(669231729752423467)
XLA Ops:
  0.0 0.0 copy-start
  0.0 0.9 %copy-done = bf16[1,2,16,2560]{3,2,1,0:T(8,128)(2,1)S(1)} copy-done((bf16[1,2,16,2560]{3,2,1,0:T(8,128)(2,1)S(1)}, bf16[1,2,16,2560]{3,2,1,0:T(8,128)(2,1)}, u32[]{:S(2)}) %copy-start) | copy-done | bytes 163864
  1.0 9.2 %all_to_all.10.group_ref = bf16[4,2,6,16,128]{4,3,2,1,0:T(8,128)(2,1)S(1)} all-to-all(bf16[4,2,6,16,128]{4,3,2,1,0:T(8,128)(2,1)S(1)} %shard_map.17), channel_id=1, replica_groups={{0,128,256,384},{64,192,320,448},{1,129,257,385},{65,193,321,449},{2,13..., dimensions={0} | all-to-all | bytes 393216 | tf_op jit(solution)/shard_map/all_to_all | solution.py:296
  10.1 0.7 %collective-permute-start.2 = (bf16[4,2,6,16,128]{4,3,2,1,0:T(8,128)(2,1)S(1)}, bf16[4,2,6,16,128]{4,3,2,1,0:T(8,128)(2,1)S(1)}, u32[]{:S(2)}, u32[]{:S(2)}) collective-permute-start(bf16[4,2,6,16,128]{4,3,2,1,0:T(8,128)(2,1)S(1)} %all_to_all.10.group_ref), channel_id=1, source_target_pairs={{129,193},{131,195},{133,197},{135,199},{137,201},{139,203},{141,2... | collective-permute-start | bytes 589832 | tf_op jit(solution)/shard_map/ppermute | solution.py:299
  10.8 0.7 %collective-permute-start.1 = (bf16[4,2,6,16,128]{4,3,2,1,0:T(8,128)(2,1)S(1)}, bf16[4,2,6,16,128]{4,3,2,1,0:T(8,128)(2,1)S(1)}, u32[]{:S(2)}, u32[]{:S(2)}) collective-permute-start(bf16[4,2,6,16,128]{4,3,2,1,0:T(8,128)(2,1)S(1)} %all_to_all.10.group_ref), channel_id=1, source_target_pairs={{128,192},{130,194},{132,196},{134,198},{136,200},{138,202},{140,2... | collective-permute-start | bytes 589832 | tf_op jit(solution)/shard_map/ppermute | solution.py:299
  11.5 0.2 shard_map.18
  11.6 5.1 %collective-permute-start = (bf16[2,16,128]{2,1,0:T(8,128)(2,1)S(1)}, bf16[2,16,128]{2,1,0:T(8,128)(2,1)S(1)}, u32[]{:S(2)}, u32[]{:S(2)}) collective-permute-start(bf16[2,16,128]{2,1,0:T(8,128)(2,1)S(1)} %shard_map.18), channel_id=1, source_target_pairs={{1,2},{2,1},{3,4},{4,3},{5,6},{6,5},{7,8},{8,7},{9,10},{10,9},{11,... | collective-permute-start | bytes 24584 | tf_op jit(solution)/shard_map/ppermute | solution.py:298
  16.7 1.3 %collective-permute-done.halo_ref = bf16[2,16,128]{2,1,0:T(8,128)(2,1)S(1)} collective-permute-done((bf16[2,16,128]{2,1,0:T(8,128)(2,1)S(1)}, bf16[2,16,128]{2,1,0:T(8,128)(2,1)S(1)}, u32[]{:S(2)}, u32[]{:S(2)}) %collective-permute-start) | collective-permute-done | bytes 8224 | tf_op jit(solution)/shard_map/ppermute | solution.py:298
  18.1 5.1 %collective-permute-start.4 = (bf16[18,16,128]{2,1,0:T(8,128)(2,1)S(1)}, bf16[18,16,128]{2,1,0:T(8,128)(2,1)S(1)}, u32[]{:S(2)}, u32[]{:S(2)}) collective-permute-start(bf16[18,16,128]{2,1,0:T(8,128)(2,1)S(1)} %shard_map.19), channel_id=1, source_target_pairs={{1,65},{3,67},{5,69},{7,71},{9,73},{11,75},{13,77},{15,79},{17,81}... | collective-permute-start | bytes 221192 | tf_op jit(solution)/shard_map/ppermute | solution.py:301
  23.2 0.7 %collective-permute-start.3 = (bf16[18,16,128]{2,1,0:T(8,128)(2,1)S(1)}, bf16[18,16,128]{2,1,0:T(8,128)(2,1)S(1)}, u32[]{:S(2)}, u32[]{:S(2)}) collective-permute-start(bf16[18,16,128]{2,1,0:T(8,128)(2,1)S(1)} %shard_map.19), channel_id=1, source_target_pairs={{0,64},{2,66},{4,68},{6,70},{8,72},{10,74},{12,76},{14,78},{16,80}... | collective-permute-start | bytes 221192 | tf_op jit(solution)/shard_map/ppermute | solution.py:301
  23.9 0.9 %shard_map.20 = (f32[32,128]{1,0:T(8,128)S(1)}, bf16[768,128]{1,0:T(8,128)(2,1)S(1)}) custom-call(bf16[4,2,6,16,128]{4,3,2,1,0:T(8,128)(2,1)S(1)} %all_to_all.10.group_ref, bf16[2,16,128]{2,1,0:T(8,128)(2,1)S(1)} %collective-permute-done.halo_ref), custom_call_target="tpu_custom_call" | custom-call | flops 100663296 | bytes 1048576 | tf_op jit(solution)/shard_map/pallas_call | solution.py:261
  24.8 7.0 %collective-permute-done.4.refs_1_ = bf16[18,16,128]{2,1,0:T(8,128)(2,1)S(1)} collective-permute-done((bf16[18,16,128]{2,1,0:T(8,128)(2,1)S(1)}, bf16[18,16,128]{2,1,0:T(8,128)(2,1)S(1)}, u32[]{:S(2)}, u32[]{:S(2)}) %collective-permute-start.4) | collective-permute-done | bytes 73760 | tf_op jit(solution)/shard_map/ppermute | solution.py:301
  31.9 0.0 collective-permute-done.3.refs_0_
  31.9 0.0 collective-permute-done.2.odd_ref
  31.9 0.0 collective-permute-done.1.even_ref
  31.9 1.0 %shard_map.21 = f32[4,24,128]{2,1,0:T(8,128)S(1)} custom-call(bf16[4,2,6,16,128]{4,3,2,1,0:T(8,128)(2,1)S(1)} %all_to_all.10.group_ref, bf16[2,16,128]{2,1,0:T(8,128)(2,1)S(1)} %collective-permute-done.halo_ref, bf16[4,2,6,16,128]{4,3,2,1,0:T(8,128)(2,1)S(1)} %collective-permute-done.1.even_ref, ...), custom_call_target="tpu_custom_call" | custom-call | flops 226492416 | bytes 1048576 | tf_op jit(solution)/shard_map/pallas_call | solution.py:261
  32.9 16.2 %all_to_all.11.parts_ref = f32[8,24,128]{2,1,0:T(8,128)S(1)} all-to-all(f32[8,24,128]{2,1,0:T(8,128)S(1)} %pad_maximum_fusion), channel_id=1, replica_groups={{0,128,256,384,1,129,257,385},{2,130,258,386,3,131,259,387},{4,132,260,..., dimensions={0} | all-to-all | bytes 196608 | tf_op jit(solution)/shard_map/all_to_all | solution.py:314
  49.0 0.7 %shard_map.22 = f32[8,2,2,128]{3,2,1,0:T(2,128)} custom-call(f32[8,24,128]{2,1,0:T(8,128)S(1)} %all_to_all.11.parts_ref), custom_call_target="tpu_custom_call" | custom-call | bytes 1048576 | tf_op jit(solution)/shard_map/pallas_call | solution.py:261
  (3 shorter events, 0.1 us)
Async XLA Ops:
  0.0 0.9 %copy-start = (bf16[1,2,16,2560]{3,2,1,0:T(8,128)(2,1)S(1)}, bf16[1,2,16,2560]{3,2,1,0:T(8,128)(2,1)}, u32[]{:S(2)}) copy-start(bf16[1,2,16,2560]{3,2,1,0:T(8,128)(2,1)} %stack_ref.1) | copy-start | bytes 491524
  10.1 21.7 %collective-permute-start.2 = (bf16[4,2,6,16,128]{4,3,2,1,0:T(8,128)(2,1)S(1)}, bf16[4,2,6,16,128]{4,3,2,1,0:T(8,128)(2,1)S(1)}, u32[]{:S(2)}, u32[]{:S(2)}) collective-permute-start(bf16[4,2,6,16,128]{4,3,2,1,0:T(8,128)(2,1)S(1)} %all_to_all.10.group_ref), channel_id=1, source_target_pairs={{129,193},{131,195},{133,197},{135,199},{137,201},{139,203},{141,2... | collective-permute-start | bytes 589832 | tf_op jit(solution)/shard_map/ppermute | solution.py:299
  10.8 21.1 %collective-permute-start.1 = (bf16[4,2,6,16,128]{4,3,2,1,0:T(8,128)(2,1)S(1)}, bf16[4,2,6,16,128]{4,3,2,1,0:T(8,128)(2,1)S(1)}, u32[]{:S(2)}, u32[]{:S(2)}) collective-permute-start(bf16[4,2,6,16,128]{4,3,2,1,0:T(8,128)(2,1)S(1)} %all_to_all.10.group_ref), channel_id=1, source_target_pairs={{128,192},{130,194},{132,196},{134,198},{136,200},{138,202},{140,2... | collective-permute-start | bytes 589832 | tf_op jit(solution)/shard_map/ppermute | solution.py:299
  11.6 6.4 %collective-permute-start = (bf16[2,16,128]{2,1,0:T(8,128)(2,1)S(1)}, bf16[2,16,128]{2,1,0:T(8,128)(2,1)S(1)}, u32[]{:S(2)}, u32[]{:S(2)}) collective-permute-start(bf16[2,16,128]{2,1,0:T(8,128)(2,1)S(1)} %shard_map.18), channel_id=1, source_target_pairs={{1,2},{2,1},{3,4},{4,3},{5,6},{6,5},{7,8},{8,7},{9,10},{10,9},{11,... | collective-permute-start | bytes 24584 | tf_op jit(solution)/shard_map/ppermute | solution.py:298
  18.1 13.8 %collective-permute-start.4 = (bf16[18,16,128]{2,1,0:T(8,128)(2,1)S(1)}, bf16[18,16,128]{2,1,0:T(8,128)(2,1)S(1)}, u32[]{:S(2)}, u32[]{:S(2)}) collective-permute-start(bf16[18,16,128]{2,1,0:T(8,128)(2,1)S(1)} %shard_map.19), channel_id=1, source_target_pairs={{1,65},{3,67},{5,69},{7,71},{9,73},{11,75},{13,77},{15,79},{17,81}... | collective-permute-start | bytes 221192 | tf_op jit(solution)/shard_map/ppermute | solution.py:301
  23.2 8.6 %collective-permute-start.3 = (bf16[18,16,128]{2,1,0:T(8,128)(2,1)S(1)}, bf16[18,16,128]{2,1,0:T(8,128)(2,1)S(1)}, u32[]{:S(2)}, u32[]{:S(2)}) collective-permute-start(bf16[18,16,128]{2,1,0:T(8,128)(2,1)S(1)} %shard_map.19), channel_id=1, source_target_pairs={{0,64},{2,66},{4,68},{6,70},{8,72},{10,74},{12,76},{14,78},{16,80}... | collective-permute-start | bytes 221192 | tf_op jit(solution)/shard_map/ppermute | solution.py:301

commit v8 on v7

--- a/solution.py
+++ b/solution.py
@@ -153,16 +153,22 @@
 
 
 def put(x_ref, fields, t, values):
-    at = t * LANES
+    at = t % 2 * LANES
     for field, value in enumerate(values):
         high = value.astype(bf16)
         low = (value - high.astype(f32)).astype(bf16)
-        x_ref[field * LINES : (field + 1) * LINES, at : at + LANES] = high
-        x_ref[(fields + field) * LINES : (fields + field + 1) * LINES, at : at + LANES] = low
-
-
-def looks_of(x_ref, weights, d_ref, fields):
-    d_ref[...] = jnp.dot(x_ref[...], weights, preferred_element_type=f32)
+        x_ref[t // 2, field * LINES : (field + 1) * LINES, at : at + LANES] = high
+        x_ref[t // 2, (fields + field) * LINES : (fields + field + 1) * LINES, at : at + LANES] = low
+
+
+def contract(x_ref, weight_ref, d_ref, t):
+    if t % 2 == 1:
+        rows = slice((t - 1) * LANES, (t + 1) * LANES)
+        part = jnp.dot(x_ref[t // 2], weight_ref[rows, :], preferred_element_type=f32)
+        d_ref[...] = part if t == 1 else d_ref[...] + part
+
+
+def looks_of(d_ref, fields):
     azimuth = azimuth_weights()
     for field in range(fields):
         high = d_ref[field * LINES : (field + 1) * LINES, :]
@@ -185,7 +191,8 @@
         group = dates_at([group_ref], t, halos)
         fields = [power(d) for d in group] + [cross(group[i], group[j]) for i, j in INNER]
         put(x_ref, N_INNER, t, [value for field in fields for value in field])
-    for field, a, row in looks_of(x_ref, weight_ref[...], d_ref, N_INNER):
+        contract(x_ref, weight_ref, d_ref, t)
+    for field, a, row in looks_of(d_ref, N_INNER):
         out_ref[2 * field + a : 2 * field + a + 1, :] = row
 
 
@@ -198,6 +205,7 @@
         group, other = dates_at([group_ref], t, halos), dates_at([even_ref, odd_ref], t, other_halos, joined_refs)
         fields = [power(d) for d in other] + [cross(i, j) for i in group for j in other]
         put(x_ref, N_OUTER, t, [value for field in fields for value in field])
+        contract(x_ref, weight_ref, d_ref, t)
 
     first = lanes(1) < WINDOW
     mine = (first & (own == 0)) | (~first & (own == 1))
@@ -211,7 +219,7 @@
         field = Y + 2 * INNER.index((min(i, j), max(i, j))) + part
         return -inner(field, a) if part == 1 and i > j else inner(field, a)
 
-    for field, a, row in looks_of(x_ref, weight_ref[...], d_ref, N_OUTER):
+    for field, a, row in looks_of(d_ref, N_OUTER):
         if field < Y:
             at = 16 + 2 * field + a
             row = jnp.where(mine, inner(field, a), row)
@@ -271,7 +279,7 @@
 
 def looks(kernel, out_shape, operands, fields):
     rows, samples = 2 * fields * LINES, BLOCKS * LANES
-    scratch = [pltpu.VMEM((rows, samples), bf16), pltpu.VMEM((rows, LANES), f32)]
+    scratch = [pltpu.VMEM((BLOCKS // 2, rows, 2 * LANES), bf16), pltpu.VMEM((rows, LANES), f32)]
     return call(kernel, out_shape, operands, scratch, flops=2 * rows * samples * LANES)
 
 

time: 50 us -> 50 us (level)
  no operation moved by 1% of the time
where the time goes in v8:
time: 50 us; the launch traced here: 49.7 us
  blocking collectives  25.3 us (51%)
  starting transfers between devices  12.2 us (24%)
  waiting for transfers between devices  8.35 us (17%)
  Pallas kernels  2.8 us (6%)
  local copies, waits for them, and re-layouts  0.92 us (2%)
    all_to_all x1, blocking collectives, local(): lax.all_to_all(jnp.concatenate([parts, parts]), axes, 0, 0, axis_index_gr...  16.2 us
    all_to_all x1, blocking collectives, local(): group = lax.all_to_all(chunks, 'pair', 0, 0, axis_index_groups=GROUPS)  9.16 us
    ppermute x2, waiting for transfers between devices, local(): lax.ppermute(joined, axes, across((0,), (core,)))  7.03 us
    ppermute x2, starting transfers between devices, local(): lax.ppermute(joined, axes, across((0,), (core,)))  5.81 us
    ppermute x1, starting transfers between devices, local(): halo = lax.ppermute(edge, axes, swap)  5.1 us
    pallas_call x6, Pallas kernels, call(): pl.pallas_call(kernel, out_shape=out_shape, in_specs=[VMEM] * len(operand...  2.8 us
    ppermute x2, starting transfers between devices, local(): lax.ppermute(group, axes, across((1, 2, 3), (core,)))  1.33 us
    ppermute x1, waiting for transfers between devices, local(): halo = lax.ppermute(edge, axes, swap)  1.32 us
  transfers between devices with their start and end apart: 5, of which 2 were waited for; matrix products, arithmetic and copies ran while one was open for 0% of the time, Pallas kernels for 2%

profile of v8, /device:TPU:449, one launch (start us, length us, event | category | flops | bytes accessed | tf_op | source)
XLA Modules:
  0.0 49.7 jit_solution(2637901483792859939)
XLA Ops:
  0.0 0.0 copy-start
  0.0 0.9 %copy-done = bf16[1,2,16,2560]{3,2,1,0:T(8,128)(2,1)S(1)} copy-done((bf16[1,2,16,2560]{3,2,1,0:T(8,128)(2,1)S(1)}, bf16[1,2,16,2560]{3,2,1,0:T(8,128)(2,1)}, u32[]{:S(2)}) %copy-start) | copy-done | bytes 163864
  1.0 9.2 %all_to_all.10.group_ref = bf16[4,2,6,16,128]{4,3,2,1,0:T(8,128)(2,1)S(1)} all-to-all(bf16[4,2,6,16,128]{4,3,2,1,0:T(8,128)(2,1)S(1)} %shard_map.17), channel_id=1, replica_groups={{0,128,256,384},{64,192,320,448},{1,129,257,385},{65,193,321,449},{2,13..., dimensions={0} | all-to-all | bytes 393216 | tf_op jit(solution)/shard_map/all_to_all | solution.py:304
  10.1 0.7 %collective-permute-start.2 = (bf16[4,2,6,16,128]{4,3,2,1,0:T(8,128)(2,1)S(1)}, bf16[4,2,6,16,128]{4,3,2,1,0:T(8,128)(2,1)S(1)}, u32[]{:S(2)}, u32[]{:S(2)}) collective-permute-start(bf16[4,2,6,16,128]{4,3,2,1,0:T(8,128)(2,1)S(1)} %all_to_all.10.group_ref), channel_id=1, source_target_pairs={{129,193},{131,195},{133,197},{135,199},{137,201},{139,203},{141,2... | collective-permute-start | bytes 589832 | tf_op jit(solution)/shard_map/ppermute | solution.py:307
  10.8 0.7 %collective-permute-start.1 = (bf16[4,2,6,16,128]{4,3,2,1,0:T(8,128)(2,1)S(1)}, bf16[4,2,6,16,128]{4,3,2,1,0:T(8,128)(2,1)S(1)}, u32[]{:S(2)}, u32[]{:S(2)}) collective-permute-start(bf16[4,2,6,16,128]{4,3,2,1,0:T(8,128)(2,1)S(1)} %all_to_all.10.group_ref), channel_id=1, source_target_pairs={{128,192},{130,194},{132,196},{134,198},{136,200},{138,202},{140,2... | collective-permute-start | bytes 589832 | tf_op jit(solution)/shard_map/ppermute | solution.py:307
  11.5 0.2 shard_map.18
  11.6 5.1 %collective-permute-start = (bf16[2,16,128]{2,1,0:T(8,128)(2,1)S(1)}, bf16[2,16,128]{2,1,0:T(8,128)(2,1)S(1)}, u32[]{:S(2)}, u32[]{:S(2)}) collective-permute-start(bf16[2,16,128]{2,1,0:T(8,128)(2,1)S(1)} %shard_map.18), channel_id=1, source_target_pairs={{1,2},{2,1},{3,4},{4,3},{5,6},{6,5},{7,8},{8,7},{9,10},{10,9},{11,... | collective-permute-start | bytes 24584 | tf_op jit(solution)/shard_map/ppermute | solution.py:306
  16.7 1.3 %collective-permute-done.halo_ref = bf16[2,16,128]{2,1,0:T(8,128)(2,1)S(1)} collective-permute-done((bf16[2,16,128]{2,1,0:T(8,128)(2,1)S(1)}, bf16[2,16,128]{2,1,0:T(8,128)(2,1)S(1)}, u32[]{:S(2)}, u32[]{:S(2)}) %collective-permute-start) | collective-permute-done | bytes 8224 | tf_op jit(solution)/shard_map/ppermute | solution.py:306
  18.1 5.1 %collective-permute-start.4 = (bf16[18,16,128]{2,1,0:T(8,128)(2,1)S(1)}, bf16[18,16,128]{2,1,0:T(8,128)(2,1)S(1)}, u32[]{:S(2)}, u32[]{:S(2)}) collective-permute-start(bf16[18,16,128]{2,1,0:T(8,128)(2,1)S(1)} %shard_map.19), channel_id=1, source_target_pairs={{1,65},{3,67},{5,69},{7,71},{9,73},{11,75},{13,77},{15,79},{17,81}... | collective-permute-start | bytes 221192 | tf_op jit(solution)/shard_map/ppermute | solution.py:309
  23.2 0.7 %collective-permute-start.3 = (bf16[18,16,128]{2,1,0:T(8,128)(2,1)S(1)}, bf16[18,16,128]{2,1,0:T(8,128)(2,1)S(1)}, u32[]{:S(2)}, u32[]{:S(2)}) collective-permute-start(bf16[18,16,128]{2,1,0:T(8,128)(2,1)S(1)} %shard_map.19), channel_id=1, source_target_pairs={{0,64},{2,66},{4,68},{6,70},{8,72},{10,74},{12,76},{14,78},{16,80}... | collective-permute-start | bytes 221192 | tf_op jit(solution)/shard_map/ppermute | solution.py:309
  23.9 0.9 %shard_map.20 = (f32[32,128]{1,0:T(8,128)S(1)}, bf16[768,128]{1,0:T(8,128)(2,1)S(1)}) custom-call(bf16[4,2,6,16,128]{4,3,2,1,0:T(8,128)(2,1)S(1)} %all_to_all.10.group_ref, bf16[2,16,128]{2,1,0:T(8,128)(2,1)S(1)} %collective-permute-done.halo_ref), custom_call_target="tpu_custom_call" | custom-call | flops 100663296 | bytes 1048576 | tf_op jit(solution)/shard_map/pallas_call | solution.py:269
  24.8 7.0 %collective-permute-done.4.refs_1_ = bf16[18,16,128]{2,1,0:T(8,128)(2,1)S(1)} collective-permute-done((bf16[18,16,128]{2,1,0:T(8,128)(2,1)S(1)}, bf16[18,16,128]{2,1,0:T(8,128)(2,1)S(1)}, u32[]{:S(2)}, u32[]{:S(2)}) %collective-permute-start.4) | collective-permute-done | bytes 73760 | tf_op jit(solution)/shard_map/ppermute | solution.py:309
  31.9 0.0 collective-permute-done.3.refs_0_
  31.9 0.0 collective-permute-done.2.odd_ref
  31.9 0.0 collective-permute-done.1.even_ref
  31.9 0.9 %shard_map.21 = f32[4,24,128]{2,1,0:T(8,128)S(1)} custom-call(bf16[4,2,6,16,128]{4,3,2,1,0:T(8,128)(2,1)S(1)} %all_to_all.10.group_ref, bf16[2,16,128]{2,1,0:T(8,128)(2,1)S(1)} %collective-permute-done.halo_ref, bf16[4,2,6,16,128]{4,3,2,1,0:T(8,128)(2,1)S(1)} %collective-permute-done.1.even_ref, ...), custom_call_target="tpu_custom_call" | custom-call | flops 226492416 | bytes 1048576 | tf_op jit(solution)/shard_map/pallas_call | solution.py:269
  32.8 16.2 %all_to_all.11.parts_ref = f32[8,24,128]{2,1,0:T(8,128)S(1)} all-to-all(f32[8,24,128]{2,1,0:T(8,128)S(1)} %pad_maximum_fusion), channel_id=1, replica_groups={{0,128,256,384,1,129,257,385},{2,130,258,386,3,131,259,387},{4,132,260,..., dimensions={0} | all-to-all | bytes 196608 | tf_op jit(solution)/shard_map/all_to_all | solution.py:322
  49.0 0.7 %shard_map.22 = f32[8,2,2,128]{3,2,1,0:T(2,128)} custom-call(f32[8,24,128]{2,1,0:T(8,128)S(1)} %all_to_all.11.parts_ref), custom_call_target="tpu_custom_call" | custom-call | bytes 1048576 | tf_op jit(solution)/shard_map/pallas_call | solution.py:269
  (3 shorter events, 0.1 us)
Async XLA Ops:
  0.0 0.9 %copy-start = (bf16[1,2,16,2560]{3,2,1,0:T(8,128)(2,1)S(1)}, bf16[1,2,16,2560]{3,2,1,0:T(8,128)(2,1)}, u32[]{:S(2)}) copy-start(bf16[1,2,16,2560]{3,2,1,0:T(8,128)(2,1)} %stack_ref.1) | copy-start | bytes 491524
  10.1 21.7 %collective-permute-start.2 = (bf16[4,2,6,16,128]{4,3,2,1,0:T(8,128)(2,1)S(1)}, bf16[4,2,6,16,128]{4,3,2,1,0:T(8,128)(2,1)S(1)}, u32[]{:S(2)}, u32[]{:S(2)}) collective-permute-start(bf16[4,2,6,16,128]{4,3,2,1,0:T(8,128)(2,1)S(1)} %all_to_all.10.group_ref), channel_id=1, source_target_pairs={{129,193},{131,195},{133,197},{135,199},{137,201},{139,203},{141,2... | collective-permute-start | bytes 589832 | tf_op jit(solution)/shard_map/ppermute | solution.py:307
  10.8 21.1 %collective-permute-start.1 = (bf16[4,2,6,16,128]{4,3,2,1,0:T(8,128)(2,1)S(1)}, bf16[4,2,6,16,128]{4,3,2,1,0:T(8,128)(2,1)S(1)}, u32[]{:S(2)}, u32[]{:S(2)}) collective-permute-start(bf16[4,2,6,16,128]{4,3,2,1,0:T(8,128)(2,1)S(1)} %all_to_all.10.group_ref), channel_id=1, source_target_pairs={{128,192},{130,194},{132,196},{134,198},{136,200},{138,202},{140,2... | collective-permute-start | bytes 589832 | tf_op jit(solution)/shard_map/ppermute | solution.py:307
  11.6 6.4 %collective-permute-start = (bf16[2,16,128]{2,1,0:T(8,128)(2,1)S(1)}, bf16[2,16,128]{2,1,0:T(8,128)(2,1)S(1)}, u32[]{:S(2)}, u32[]{:S(2)}) collective-permute-start(bf16[2,16,128]{2,1,0:T(8,128)(2,1)S(1)} %shard_map.18), channel_id=1, source_target_pairs={{1,2},{2,1},{3,4},{4,3},{5,6},{6,5},{7,8},{8,7},{9,10},{10,9},{11,... | collective-permute-start | bytes 24584 | tf_op jit(solution)/shard_map/ppermute | solution.py:306
  18.1 13.8 %collective-permute-start.4 = (bf16[18,16,128]{2,1,0:T(8,128)(2,1)S(1)}, bf16[18,16,128]{2,1,0:T(8,128)(2,1)S(1)}, u32[]{:S(2)}, u32[]{:S(2)}) collective-permute-start(bf16[18,16,128]{2,1,0:T(8,128)(2,1)S(1)} %shard_map.19), channel_id=1, source_target_pairs={{1,65},{3,67},{5,69},{7,71},{9,73},{11,75},{13,77},{15,79},{17,81}... | collective-permute-start | bytes 221192 | tf_op jit(solution)/shard_map/ppermute | solution.py:309
  23.2 8.6 %collective-permute-start.3 = (bf16[18,16,128]{2,1,0:T(8,128)(2,1)S(1)}, bf16[18,16,128]{2,1,0:T(8,128)(2,1)S(1)}, u32[]{:S(2)}, u32[]{:S(2)}) collective-permute-start(bf16[18,16,128]{2,1,0:T(8,128)(2,1)S(1)} %shard_map.19), channel_id=1, source_target_pairs={{0,64},{2,66},{4,68},{6,70},{8,72},{10,74},{12,76},{14,78},{16,80}... | collective-permute-start | bytes 221192 | tf_op jit(solution)/shard_map/ppermute | solution.py:309

commit v9 on v7

--- a/solution.py
+++ b/solution.py
@@ -298,7 +298,7 @@
     halo = lax.ppermute(edge, axes, swap)
     others = [lax.ppermute(group, axes, across((1, 2, 3), (core,))) for core in range(2)]
     joined = call(join_kernel, jax.ShapeDtypeStruct((2 * Y * SHARES[0] + 2, LINES, LANES), bf16), (group, halo))
-    joineds = [lax.ppermute(joined, axes, across((0,), (core,))) for core in range(2)]
+    joineds = [lax.ppermute(joined, axes, across((0,), (core,))) for core in (1, 0)]
 
     shapes = (
         jax.ShapeDtypeStruct((2 * N_INNER, LANES), f32),

time: 50 us -> 50 us (level)
  waiting for transfers between devices: 8.35 us -> 10.6 us
  blocking collectives: 25.3 us -> 23.1 us
    all_to_all x1, blocking collectives: 16.2 us -> 13.9 us  [local(): lax.all_to_all(jnp.concatenate([parts, parts]), axes, 0, 0, axis_index_gr...]
    ppermute x2, waiting for transfers between devices: 7.03 us -> 9.27 us  [local(): lax.ppermute(joined, axes, across((0,), (core,)))]
where the time goes in v9:
time: 50 us; the launch traced here: 49.7 us
  blocking collectives  23.1 us (46%)
  starting transfers between devices  12.2 us (24%)
  waiting for transfers between devices  10.6 us (21%)
  Pallas kernels  2.81 us (6%)
  local copies, waits for them, and re-layouts  0.92 us (2%)
    all_to_all x1, blocking collectives, local(): lax.all_to_all(jnp.concatenate([parts, parts]), axes, 0, 0, axis_index_gr...  13.9 us
    ppermute x2, waiting for transfers between devices, local(): lax.ppermute(joined, axes, across((0,), (core,)))  9.27 us
    all_to_all x1, blocking collectives, local(): group = lax.all_to_all(chunks, 'pair', 0, 0, axis_index_groups=GROUPS)  9.16 us
    ppermute x2, starting transfers between devices, local(): lax.ppermute(joined, axes, across((0,), (core,)))  5.81 us
    ppermute x1, starting transfers between devices, local(): halo = lax.ppermute(edge, axes, swap)  5.1 us
    pallas_call x6, Pallas kernels, call(): pl.pallas_call(kernel, out_shape=out_shape, in_specs=[VMEM] * len(operand...  2.81 us
    ppermute x2, starting transfers between devices, local(): lax.ppermute(group, axes, across((1, 2, 3), (core,)))  1.33 us
    ppermute x1, waiting for transfers between devices, local(): halo = lax.ppermute(edge, axes, swap)  1.32 us
  transfers between devices with their start and end apart: 5, of which 2 were waited for; matrix products, arithmetic and copies ran while one was open for 0% of the time, Pallas kernels for 2%

profile of v9, /device:TPU:449, one launch (start us, length us, event | category | flops | bytes accessed | tf_op | source)
XLA Modules:
  0.0 49.7 jit_solution(1864318708893941853)
XLA Ops:
  0.0 0.0 copy-start
  0.0 0.9 %copy-done = bf16[1,2,16,2560]{3,2,1,0:T(8,128)(2,1)S(1)} copy-done((bf16[1,2,16,2560]{3,2,1,0:T(8,128)(2,1)S(1)}, bf16[1,2,16,2560]{3,2,1,0:T(8,128)(2,1)}, u32[]{:S(2)}) %copy-start) | copy-done | bytes 163864
  1.0 9.2 %all_to_all.10.group_ref = bf16[4,2,6,16,128]{4,3,2,1,0:T(8,128)(2,1)S(1)} all-to-all(bf16[4,2,6,16,128]{4,3,2,1,0:T(8,128)(2,1)S(1)} %shard_map.17), channel_id=1, replica_groups={{0,128,256,384},{64,192,320,448},{1,129,257,385},{65,193,321,449},{2,13..., dimensions={0} | all-to-all | bytes 393216 | tf_op jit(solution)/shard_map/all_to_all | solution.py:296
  10.1 0.7 %collective-permute-start.2 = (bf16[4,2,6,16,128]{4,3,2,1,0:T(8,128)(2,1)S(1)}, bf16[4,2,6,16,128]{4,3,2,1,0:T(8,128)(2,1)S(1)}, u32[]{:S(2)}, u32[]{:S(2)}) collective-permute-start(bf16[4,2,6,16,128]{4,3,2,1,0:T(8,128)(2,1)S(1)} %all_to_all.10.group_ref), channel_id=1, source_target_pairs={{129,193},{131,195},{133,197},{135,199},{137,201},{139,203},{141,2... | collective-permute-start | bytes 589832 | tf_op jit(solution)/shard_map/ppermute | solution.py:299
  10.8 0.7 %collective-permute-start.1 = (bf16[4,2,6,16,128]{4,3,2,1,0:T(8,128)(2,1)S(1)}, bf16[4,2,6,16,128]{4,3,2,1,0:T(8,128)(2,1)S(1)}, u32[]{:S(2)}, u32[]{:S(2)}) collective-permute-start(bf16[4,2,6,16,128]{4,3,2,1,0:T(8,128)(2,1)S(1)} %all_to_all.10.group_ref), channel_id=1, source_target_pairs={{128,192},{130,194},{132,196},{134,198},{136,200},{138,202},{140,2... | collective-permute-start | bytes 589832 | tf_op jit(solution)/shard_map/ppermute | solution.py:299
  11.5 0.2 shard_map.18
  11.6 5.1 %collective-permute-start = (bf16[2,16,128]{2,1,0:T(8,128)(2,1)S(1)}, bf16[2,16,128]{2,1,0:T(8,128)(2,1)S(1)}, u32[]{:S(2)}, u32[]{:S(2)}) collective-permute-start(bf16[2,16,128]{2,1,0:T(8,128)(2,1)S(1)} %shard_map.18), channel_id=1, source_target_pairs={{1,2},{2,1},{3,4},{4,3},{5,6},{6,5},{7,8},{8,7},{9,10},{10,9},{11,... | collective-permute-start | bytes 24584 | tf_op jit(solution)/shard_map/ppermute | solution.py:298
  16.7 1.3 %collective-permute-done.halo_ref = bf16[2,16,128]{2,1,0:T(8,128)(2,1)S(1)} collective-permute-done((bf16[2,16,128]{2,1,0:T(8,128)(2,1)S(1)}, bf16[2,16,128]{2,1,0:T(8,128)(2,1)S(1)}, u32[]{:S(2)}, u32[]{:S(2)}) %collective-permute-start) | collective-permute-done | bytes 8224 | tf_op jit(solution)/shard_map/ppermute | solution.py:298
  18.1 0.7 %collective-permute-start.4 = (bf16[18,16,128]{2,1,0:T(8,128)(2,1)S(1)}, bf16[18,16,128]{2,1,0:T(8,128)(2,1)S(1)}, u32[]{:S(2)}, u32[]{:S(2)}) collective-permute-start(bf16[18,16,128]{2,1,0:T(8,128)(2,1)S(1)} %shard_map.19), channel_id=1, source_target_pairs={{0,64},{2,66},{4,68},{6,70},{8,72},{10,74},{12,76},{14,78},{16,80}... | collective-permute-start | bytes 221192 | tf_op jit(solution)/shard_map/ppermute | solution.py:301
  18.7 5.2 %collective-permute-start.3 = (bf16[18,16,128]{2,1,0:T(8,128)(2,1)S(1)}, bf16[18,16,128]{2,1,0:T(8,128)(2,1)S(1)}, u32[]{:S(2)}, u32[]{:S(2)}) collective-permute-start(bf16[18,16,128]{2,1,0:T(8,128)(2,1)S(1)} %shard_map.19), channel_id=1, source_target_pairs={{1,65},{3,67},{5,69},{7,71},{9,73},{11,75},{13,77},{15,79},{17,81}... | collective-permute-start | bytes 221192 | tf_op jit(solution)/shard_map/ppermute | solution.py:301
  23.9 0.9 %shard_map.20 = (f32[32,128]{1,0:T(8,128)S(1)}, bf16[768,128]{1,0:T(8,128)(2,1)S(1)}) custom-call(bf16[4,2,6,16,128]{4,3,2,1,0:T(8,128)(2,1)S(1)} %all_to_all.10.group_ref, bf16[2,16,128]{2,1,0:T(8,128)(2,1)S(1)} %collective-permute-done.halo_ref), custom_call_target="tpu_custom_call" | custom-call | flops 100663296 | bytes 1048576 | tf_op jit(solution)/shard_map/pallas_call | solution.py:261
  24.8 0.0 collective-permute-done.4.refs_1_
  24.8 9.3 %collective-permute-done.3.refs_0_ = bf16[18,16,128]{2,1,0:T(8,128)(2,1)S(1)} collective-permute-done((bf16[18,16,128]{2,1,0:T(8,128)(2,1)S(1)}, bf16[18,16,128]{2,1,0:T(8,128)(2,1)S(1)}, u32[]{:S(2)}, u32[]{:S(2)}) %collective-permute-start.3) | collective-permute-done | bytes 73760 | tf_op jit(solution)/shard_map/ppermute | solution.py:301
  34.1 0.0 collective-permute-done.2.odd_ref
  34.1 0.0 collective-permute-done.1.even_ref
  34.1 1.0 %shard_map.21 = f32[4,24,128]{2,1,0:T(8,128)S(1)} custom-call(bf16[4,2,6,16,128]{4,3,2,1,0:T(8,128)(2,1)S(1)} %all_to_all.10.group_ref, bf16[2,16,128]{2,1,0:T(8,128)(2,1)S(1)} %collective-permute-done.halo_ref, bf16[4,2,6,16,128]{4,3,2,1,0:T(8,128)(2,1)S(1)} %collective-permute-done.1.even_ref, ...), custom_call_target="tpu_custom_call" | custom-call | flops 226492416 | bytes 1048576 | tf_op jit(solution)/shard_map/pallas_call | solution.py:261
  35.1 13.9 %all_to_all.11.parts_ref = f32[8,24,128]{2,1,0:T(8,128)S(1)} all-to-all(f32[8,24,128]{2,1,0:T(8,128)S(1)} %pad_maximum_fusion), channel_id=1, replica_groups={{0,128,256,384,1,129,257,385},{2,130,258,386,3,131,259,387},{4,132,260,..., dimensions={0} | all-to-all | bytes 196608 | tf_op jit(solution)/shard_map/all_to_all | solution.py:314
  49.0 0.7 %shard_map.22 = f32[8,2,2,128]{3,2,1,0:T(2,128)} custom-call(f32[8,24,128]{2,1,0:T(8,128)S(1)} %all_to_all.11.parts_ref), custom_call_target="tpu_custom_call" | custom-call | bytes 1048576 | tf_op jit(solution)/shard_map/pallas_call | solution.py:261
  (3 shorter events, 0.1 us)
Async XLA Ops:
  0.0 0.9 %copy-start = (bf16[1,2,16,2560]{3,2,1,0:T(8,128)(2,1)S(1)}, bf16[1,2,16,2560]{3,2,1,0:T(8,128)(2,1)}, u32[]{:S(2)}) copy-start(bf16[1,2,16,2560]{3,2,1,0:T(8,128)(2,1)} %stack_ref.1) | copy-start | bytes 491524
  10.1 24.0 %collective-permute-start.2 = (bf16[4,2,6,16,128]{4,3,2,1,0:T(8,128)(2,1)S(1)}, bf16[4,2,6,16,128]{4,3,2,1,0:T(8,128)(2,1)S(1)}, u32[]{:S(2)}, u32[]{:S(2)}) collective-permute-start(bf16[4,2,6,16,128]{4,3,2,1,0:T(8,128)(2,1)S(1)} %all_to_all.10.group_ref), channel_id=1, source_target_pairs={{129,193},{131,195},{133,197},{135,199},{137,201},{139,203},{141,2... | collective-permute-start | bytes 589832 | tf_op jit(solution)/shard_map/ppermute | solution.py:299
  10.8 23.3 %collective-permute-start.1 = (bf16[4,2,6,16,128]{4,3,2,1,0:T(8,128)(2,1)S(1)}, bf16[4,2,6,16,128]{4,3,2,1,0:T(8,128)(2,1)S(1)}, u32[]{:S(2)}, u32[]{:S(2)}) collective-permute-start(bf16[4,2,6,16,128]{4,3,2,1,0:T(8,128)(2,1)S(1)} %all_to_all.10.group_ref), channel_id=1, source_target_pairs={{128,192},{130,194},{132,196},{134,198},{136,200},{138,202},{140,2... | collective-permute-start | bytes 589832 | tf_op jit(solution)/shard_map/ppermute | solution.py:299
  11.6 6.4 %collective-permute-start = (bf16[2,16,128]{2,1,0:T(8,128)(2,1)S(1)}, bf16[2,16,128]{2,1,0:T(8,128)(2,1)S(1)}, u32[]{:S(2)}, u32[]{:S(2)}) collective-permute-start(bf16[2,16,128]{2,1,0:T(8,128)(2,1)S(1)} %shard_map.18), channel_id=1, source_target_pairs={{1,2},{2,1},{3,4},{4,3},{5,6},{6,5},{7,8},{8,7},{9,10},{10,9},{11,... | collective-permute-start | bytes 24584 | tf_op jit(solution)/shard_map/ppermute | solution.py:298
  18.1 6.8 %collective-permute-start.4 = (bf16[18,16,128]{2,1,0:T(8,128)(2,1)S(1)}, bf16[18,16,128]{2,1,0:T(8,128)(2,1)S(1)}, u32[]{:S(2)}, u32[]{:S(2)}) collective-permute-start(bf16[18,16,128]{2,1,0:T(8,128)(2,1)S(1)} %shard_map.19), channel_id=1, source_target_pairs={{0,64},{2,66},{4,68},{6,70},{8,72},{10,74},{12,76},{14,78},{16,80}... | collective-permute-start | bytes 221192 | tf_op jit(solution)/shard_map/ppermute | solution.py:301
  18.7 15.4 %collective-permute-start.3 = (bf16[18,16,128]{2,1,0:T(8,128)(2,1)S(1)}, bf16[18,16,128]{2,1,0:T(8,128)(2,1)S(1)}, u32[]{:S(2)}, u32[]{:S(2)}) collective-permute-start(bf16[18,16,128]{2,1,0:T(8,128)(2,1)S(1)} %shard_map.19), channel_id=1, source_target_pairs={{1,65},{3,67},{5,69},{7,71},{9,73},{11,75},{13,77},{15,79},{17,81}... | collective-permute-start | bytes 221192 | tf_op jit(solution)/shard_map/ppermute | solution.py:301

commit v10 on v7

--- a/solution.py
+++ b/solution.py
@@ -229,19 +229,19 @@
     rows = parts_ref.shape[1]
     lane = lanes(rows)
     end = jnp.where(odd, 0, LOOKS - 1)
-    own_tile = jnp.where(odd, Y, 0)
+    core = jnp.where(odd, 1, 0)
     sides = []
     for side in range(2):
 
         def window(part, base):
             return pltpu.roll(part, (base + 2 * LANES - side * WINDOW) % LANES, 1)
 
-        summed = window(parts_ref[Y - own_tile + Y - 1], base_of(Y - 1, ~odd))
+        summed = window(parts_ref[2 * (Y - 1) + 1 - core], base_of(Y - 1, ~odd))
         summed = jnp.where(lane == end, summed, 0.0)
         for i in range(Y):
             base = base_of(i, odd)
             inside = (lane >= base) & (lane < base + WINDOW)
-            summed = summed + jnp.where(inside, window(parts_ref[own_tile + i], base), 0.0)
+            summed = summed + jnp.where(inside, window(parts_ref[2 * i + core], base), 0.0)
         sides.append(summed)
     column_powers = [summed[16:24] for summed in sides]
     row_power = jnp.where(own == 0, *column_powers)
@@ -290,7 +290,7 @@
     for h in range(2):
         for n in range(1, tiles - 1, 2):
             swap += [(device(0, h, n), device(0, h, n + 1)), (device(0, h, n + 1), device(0, h, n))]
-    chips = [[device(y, h, n + c) for c in range(2) for y in range(Y)] for h in range(2) for n in range(0, tiles, 2)]
+    chips = [[device(y, h, n + c) for y in range(Y) for c in range(2)] for h in range(2) for n in range(0, tiles, 2)]
 
     chunks = call(cut_kernel, jax.ShapeDtypeStruct((Y, 2, BLOCKS, LINES, LANES), bf16), (stack,))
     group = lax.all_to_all(chunks, "pair", 0, 0, axis_index_groups=GROUPS)
@@ -311,7 +311,7 @@
         (group, halo, *others, *joineds, weights, inner),
         N_OUTER,
     )
-    parts = lax.all_to_all(jnp.concatenate([parts, parts]), axes, 0, 0, axis_index_groups=chips)
+    parts = lax.all_to_all(jnp.repeat(parts, 2, axis=0), axes, 0, 0, axis_index_groups=chips)
     out = call(normalise_kernel, jax.ShapeDtypeStruct((2 * Y, 2, 2, LANES), f32), (parts,))
     return out[None]
 

time: 50 us -> 50.1 us (level)
  no operation moved by 1% of the time
where the time goes in v10:
time: 50.1 us; the launch traced here: 49.7 us
  blocking collectives  25.3 us (50%)
  starting transfers between devices  12.2 us (24%)
  waiting for transfers between devices  8.35 us (17%)
  Pallas kernels  2.81 us (6%)
  local copies, waits for them, and re-layouts  0.92 us (2%)
    all_to_all x1, blocking collectives, local(): lax.all_to_all(jnp.repeat(parts, 2, axis=0), axes, 0, 0, axis_index_group...  16.1 us
    all_to_all x1, blocking collectives, local(): group = lax.all_to_all(chunks, 'pair', 0, 0, axis_index_groups=GROUPS)  9.16 us
    ppermute x2, waiting for transfers between devices, local(): lax.ppermute(joined, axes, across((0,), (core,)))  7.03 us
    ppermute x2, starting transfers between devices, local(): lax.ppermute(joined, axes, across((0,), (core,)))  5.81 us
    ppermute x1, starting transfers between devices, local(): halo = lax.ppermute(edge, axes, swap)  5.1 us
    pallas_call x6, Pallas kernels, call(): pl.pallas_call(kernel, out_shape=out_shape, in_specs=[VMEM] * len(operand...  2.81 us
    ppermute x2, starting transfers between devices, local(): lax.ppermute(group, axes, across((1, 2, 3), (core,)))  1.33 us
    ppermute x1, waiting for transfers between devices, local(): halo = lax.ppermute(edge, axes, swap)  1.32 us
  transfers between devices with their start and end apart: 5, of which 2 were waited for; matrix products, arithmetic and copies ran while one was open for 0% of the time, Pallas kernels for 2%

profile of v10, /device:TPU:449, one launch (start us, length us, event | category | flops | bytes accessed | tf_op | source)
XLA Modules:
  0.0 49.7 jit_solution(2585463211072478068)
XLA Ops:
  0.0 0.0 copy-start
  0.0 0.9 %copy-done = bf16[1,2,16,2560]{3,2,1,0:T(8,128)(2,1)S(1)} copy-done((bf16[1,2,16,2560]{3,2,1,0:T(8,128)(2,1)S(1)}, bf16[1,2,16,2560]{3,2,1,0:T(8,128)(2,1)}, u32[]{:S(2)}) %copy-start) | copy-done | bytes 163864
  1.0 9.2 %all_to_all.10.group_ref = bf16[4,2,6,16,128]{4,3,2,1,0:T(8,128)(2,1)S(1)} all-to-all(bf16[4,2,6,16,128]{4,3,2,1,0:T(8,128)(2,1)S(1)} %shard_map.17), channel_id=1, replica_groups={{0,128,256,384},{64,192,320,448},{1,129,257,385},{65,193,321,449},{2,13..., dimensions={0} | all-to-all | bytes 393216 | tf_op jit(solution)/shard_map/all_to_all | solution.py:296
  10.1 0.7 %collective-permute-start.2 = (bf16[4,2,6,16,128]{4,3,2,1,0:T(8,128)(2,1)S(1)}, bf16[4,2,6,16,128]{4,3,2,1,0:T(8,128)(2,1)S(1)}, u32[]{:S(2)}, u32[]{:S(2)}) collective-permute-start(bf16[4,2,6,16,128]{4,3,2,1,0:T(8,128)(2,1)S(1)} %all_to_all.10.group_ref), channel_id=1, source_target_pairs={{129,193},{131,195},{133,197},{135,199},{137,201},{139,203},{141,2... | collective-permute-start | bytes 589832 | tf_op jit(solution)/shard_map/ppermute | solution.py:299
  10.8 0.7 %collective-permute-start.1 = (bf16[4,2,6,16,128]{4,3,2,1,0:T(8,128)(2,1)S(1)}, bf16[4,2,6,16,128]{4,3,2,1,0:T(8,128)(2,1)S(1)}, u32[]{:S(2)}, u32[]{:S(2)}) collective-permute-start(bf16[4,2,6,16,128]{4,3,2,1,0:T(8,128)(2,1)S(1)} %all_to_all.10.group_ref), channel_id=1, source_target_pairs={{128,192},{130,194},{132,196},{134,198},{136,200},{138,202},{140,2... | collective-permute-start | bytes 589832 | tf_op jit(solution)/shard_map/ppermute | solution.py:299
  11.5 0.2 shard_map.18
  11.6 5.1 %collective-permute-start = (bf16[2,16,128]{2,1,0:T(8,128)(2,1)S(1)}, bf16[2,16,128]{2,1,0:T(8,128)(2,1)S(1)}, u32[]{:S(2)}, u32[]{:S(2)}) collective-permute-start(bf16[2,16,128]{2,1,0:T(8,128)(2,1)S(1)} %shard_map.18), channel_id=1, source_target_pairs={{1,2},{2,1},{3,4},{4,3},{5,6},{6,5},{7,8},{8,7},{9,10},{10,9},{11,... | collective-permute-start | bytes 24584 | tf_op jit(solution)/shard_map/ppermute | solution.py:298
  16.7 1.3 %collective-permute-done.halo_ref = bf16[2,16,128]{2,1,0:T(8,128)(2,1)S(1)} collective-permute-done((bf16[2,16,128]{2,1,0:T(8,128)(2,1)S(1)}, bf16[2,16,128]{2,1,0:T(8,128)(2,1)S(1)}, u32[]{:S(2)}, u32[]{:S(2)}) %collective-permute-start) | collective-permute-done | bytes 8224 | tf_op jit(solution)/shard_map/ppermute | solution.py:298
  18.1 5.1 %collective-permute-start.4 = (bf16[18,16,128]{2,1,0:T(8,128)(2,1)S(1)}, bf16[18,16,128]{2,1,0:T(8,128)(2,1)S(1)}, u32[]{:S(2)}, u32[]{:S(2)}) collective-permute-start(bf16[18,16,128]{2,1,0:T(8,128)(2,1)S(1)} %shard_map.19), channel_id=1, source_target_pairs={{1,65},{3,67},{5,69},{7,71},{9,73},{11,75},{13,77},{15,79},{17,81}... | collective-permute-start | bytes 221192 | tf_op jit(solution)/shard_map/ppermute | solution.py:301
  23.2 0.7 %collective-permute-start.3 = (bf16[18,16,128]{2,1,0:T(8,128)(2,1)S(1)}, bf16[18,16,128]{2,1,0:T(8,128)(2,1)S(1)}, u32[]{:S(2)}, u32[]{:S(2)}) collective-permute-start(bf16[18,16,128]{2,1,0:T(8,128)(2,1)S(1)} %shard_map.19), channel_id=1, source_target_pairs={{0,64},{2,66},{4,68},{6,70},{8,72},{10,74},{12,76},{14,78},{16,80}... | collective-permute-start | bytes 221192 | tf_op jit(solution)/shard_map/ppermute | solution.py:301
  23.9 0.9 %shard_map.20 = (f32[32,128]{1,0:T(8,128)S(1)}, bf16[768,128]{1,0:T(8,128)(2,1)S(1)}) custom-call(bf16[4,2,6,16,128]{4,3,2,1,0:T(8,128)(2,1)S(1)} %all_to_all.10.group_ref, bf16[2,16,128]{2,1,0:T(8,128)(2,1)S(1)} %collective-permute-done.halo_ref), custom_call_target="tpu_custom_call" | custom-call | flops 100663296 | bytes 1048576 | tf_op jit(solution)/shard_map/pallas_call | solution.py:261
  24.8 7.0 %collective-permute-done.4.refs_1_ = bf16[18,16,128]{2,1,0:T(8,128)(2,1)S(1)} collective-permute-done((bf16[18,16,128]{2,1,0:T(8,128)(2,1)S(1)}, bf16[18,16,128]{2,1,0:T(8,128)(2,1)S(1)}, u32[]{:S(2)}, u32[]{:S(2)}) %collective-permute-start.4) | collective-permute-done | bytes 73760 | tf_op jit(solution)/shard_map/ppermute | solution.py:301
  31.9 0.0 collective-permute-done.3.refs_0_
  31.9 0.0 collective-permute-done.2.odd_ref
  31.9 0.0 collective-permute-done.1.even_ref
  31.9 1.0 %shard_map.21 = f32[4,24,128]{2,1,0:T(8,128)S(1)} custom-call(bf16[4,2,6,16,128]{4,3,2,1,0:T(8,128)(2,1)S(1)} %all_to_all.10.group_ref, bf16[2,16,128]{2,1,0:T(8,128)(2,1)S(1)} %collective-permute-done.halo_ref, bf16[4,2,6,16,128]{4,3,2,1,0:T(8,128)(2,1)S(1)} %collective-permute-done.1.even_ref, ...), custom_call_target="tpu_custom_call" | custom-call | flops 226492416 | bytes 1048576 | tf_op jit(solution)/shard_map/pallas_call | solution.py:261
  32.9 16.1 %all_to_all.11.parts_ref = f32[8,24,128]{2,1,0:T(8,128)S(1)} all-to-all(f32[8,24,128]{2,1,0:T(8,128)S(1)} %bitcast.2), channel_id=1, replica_groups={{0,1,128,129,256,257,384,385},{2,3,130,131,258,259,386,387},{4,5,132,13..., dimensions={0} | all-to-all | bytes 196608 | tf_op jit(solution)/shard_map/all_to_all | solution.py:314
  49.0 0.7 %shard_map.22 = f32[8,2,2,128]{3,2,1,0:T(2,128)} custom-call(f32[8,24,128]{2,1,0:T(8,128)S(1)} %all_to_all.11.parts_ref), custom_call_target="tpu_custom_call" | custom-call | bytes 1048576 | tf_op jit(solution)/shard_map/pallas_call | solution.py:261
  (3 shorter events, 0.1 us)
Async XLA Ops:
  0.0 0.9 %copy-start = (bf16[1,2,16,2560]{3,2,1,0:T(8,128)(2,1)S(1)}, bf16[1,2,16,2560]{3,2,1,0:T(8,128)(2,1)}, u32[]{:S(2)}) copy-start(bf16[1,2,16,2560]{3,2,1,0:T(8,128)(2,1)} %stack_ref.1) | copy-start | bytes 491524
  10.1 21.7 %collective-permute-start.2 = (bf16[4,2,6,16,128]{4,3,2,1,0:T(8,128)(2,1)S(1)}, bf16[4,2,6,16,128]{4,3,2,1,0:T(8,128)(2,1)S(1)}, u32[]{:S(2)}, u32[]{:S(2)}) collective-permute-start(bf16[4,2,6,16,128]{4,3,2,1,0:T(8,128)(2,1)S(1)} %all_to_all.10.group_ref), channel_id=1, source_target_pairs={{129,193},{131,195},{133,197},{135,199},{137,201},{139,203},{141,2... | collective-permute-start | bytes 589832 | tf_op jit(solution)/shard_map/ppermute | solution.py:299
  10.8 21.1 %collective-permute-start.1 = (bf16[4,2,6,16,128]{4,3,2,1,0:T(8,128)(2,1)S(1)}, bf16[4,2,6,16,128]{4,3,2,1,0:T(8,128)(2,1)S(1)}, u32[]{:S(2)}, u32[]{:S(2)}) collective-permute-start(bf16[4,2,6,16,128]{4,3,2,1,0:T(8,128)(2,1)S(1)} %all_to_all.10.group_ref), channel_id=1, source_target_pairs={{128,192},{130,194},{132,196},{134,198},{136,200},{138,202},{140,2... | collective-permute-start | bytes 589832 | tf_op jit(solution)/shard_map/ppermute | solution.py:299
  11.6 6.4 %collective-permute-start = (bf16[2,16,128]{2,1,0:T(8,128)(2,1)S(1)}, bf16[2,16,128]{2,1,0:T(8,128)(2,1)S(1)}, u32[]{:S(2)}, u32[]{:S(2)}) collective-permute-start(bf16[2,16,128]{2,1,0:T(8,128)(2,1)S(1)} %shard_map.18), channel_id=1, source_target_pairs={{1,2},{2,1},{3,4},{4,3},{5,6},{6,5},{7,8},{8,7},{9,10},{10,9},{11,... | collective-permute-start | bytes 24584 | tf_op jit(solution)/shard_map/ppermute | solution.py:298
  18.1 13.8 %collective-permute-start.4 = (bf16[18,16,128]{2,1,0:T(8,128)(2,1)S(1)}, bf16[18,16,128]{2,1,0:T(8,128)(2,1)S(1)}, u32[]{:S(2)}, u32[]{:S(2)}) collective-permute-start(bf16[18,16,128]{2,1,0:T(8,128)(2,1)S(1)} %shard_map.19), channel_id=1, source_target_pairs={{1,65},{3,67},{5,69},{7,71},{9,73},{11,75},{13,77},{15,79},{17,81}... | collective-permute-start | bytes 221192 | tf_op jit(solution)/shard_map/ppermute | solution.py:301
  23.2 8.6 %collective-permute-start.3 = (bf16[18,16,128]{2,1,0:T(8,128)(2,1)S(1)}, bf16[18,16,128]{2,1,0:T(8,128)(2,1)S(1)}, u32[]{:S(2)}, u32[]{:S(2)}) collective-permute-start(bf16[18,16,128]{2,1,0:T(8,128)(2,1)S(1)} %shard_map.19), channel_id=1, source_target_pairs={{0,64},{2,66},{4,68},{6,70},{8,72},{10,74},{12,76},{14,78},{16,80}... | collective-permute-start | bytes 221192 | tf_op jit(solution)/shard_map/ppermute | solution.py:301
